TPU v7x, 256 devices: a whole 4x4x8 slice. The times are simulated.
256 devices in a mesh: dp: 32 (over y, x, core), feat: 8 (over z).
Axes of the slice: x: 4, y: 4, z: 8, core: 2. Of those that a mesh axis runs over, the one named last changes fastest.
Arguments:
- view_a: bfloat16 [8192, 4096], P('dp', 'feat'), may hold values from -51 to 51, as said below
- view_b: bfloat16 [8192, 4096], P('dp', 'feat'), may hold values from -51 to 51, as said below
Outputs:
- grad_a: bfloat16 [8192, 4096], P('dp', 'feat')
- grad_b: bfloat16 [8192, 4096], P('dp', 'feat')
- loss_value: float32 [], replicated
Inputs may be any that keep to these rules, and one draw needn't show every extreme that they name: `view_a`: Real-valued projector outputs. `view_b`: Real-valued projector outputs.
All inputs are finite; a program needn't handle non-finite values.
Results may differ from a plain program's by a relative error of at most 0.0083.
Values may be sent and summed in bfloat16 or wider, within the bound.
No kernel may reach another device: no remote copies, remote signals or barrier semaphores. Data moves between devices by JAX's collectives and lax.ppermute only.
A program may use at most 64 MiB of HBM per device.

v0:
```python
import functools

import jax
import jax.numpy as jnp
from jax import lax
from jax.experimental import pallas as pl
from jax.experimental.pallas import tpu as pltpu
from jax.sharding import Mesh, PartitionSpec as P

OFF_WEIGHT = 0.0051
EPSILON = 1e-05
F32 = jnp.float32
BF16 = jnp.bfloat16
PLANE = ("y", "x")
CONTRACT_LAST = (((1,), (1,)), ((), ()))
EXTRA = 16
MIB = 1 << 20
VMEM = pl.BlockSpec(memory_space=pltpu.VMEM)
SMEM = pl.BlockSpec(memory_space=pltpu.SMEM)


def shift(value, step, second=False):
    y_size, x_size = lax.axis_size("y"), lax.axis_size("x")
    pairs = []
    for y in range(y_size):
        for x in range(x_size):
            for c in range(2):
                along_y = (c == 1) != second
                to_y = (y + step) % y_size if along_y else y
                to_x = x if along_y else (x + step) % x_size
                pairs.append(((y * x_size + x) * 2 + c, (to_y * x_size + to_x) * 2 + c))
    return lax.ppermute(value, ("y", "x", "c"), pairs)


def swap(value):
    return lax.ppermute(value, "c", [(0, 1), (1, 0)])


def spread(value, axes, size):
    copies = jnp.broadcast_to(value[None], (size,) + value.shape)
    return lax.all_to_all(copies, axes, split_axis=0, concat_axis=0, tiled=True)


def rotate(value, by):
    twice = jnp.concatenate([value, value], axis=0)
    return lax.dynamic_slice_in_dim(twice, by, value.shape[0], axis=0)


def others(value, second=False):
    return [shift(value, step, second) for step in (1, 3, 2)]


def normalise(raw, mean, inverse):
    return ((raw.astype(F32) - mean) * inverse).astype(BF16)


def rounded(raw, mean, inverse):
    return lax.reduce_precision((raw.astype(F32) - mean) * inverse, 8, 7).astype(BF16)


def widen_body(at, stats, raw, keep, give, held, done):
    blocks, _, half = keep.shape
    copies = [
        pltpu.make_async_copy(raw.at[g], held.at[g], done.at[g]) for g in range(blocks)
    ]
    for copy in copies:
        copy.start()
    for g in range(blocks):
        copies[g].wait()
        for place, out in enumerate((keep, give)):
            spot = 1 - at[2] if place else at[2]
            cols = pl.ds(pl.multiple_of(spot * half, half), half)
            out[g] = normalise(held[g, :, cols], stats[g, 1:2, cols], stats[g, 3:4, cols])


def widen(at, stats, raw):
    blocks, rows, width = raw.shape
    return pl.pallas_call(
        widen_body,
        in_specs=[SMEM, VMEM, pl.BlockSpec(memory_space=pltpu.HBM)],
        out_specs=[VMEM] * 2,
        out_shape=[jax.ShapeDtypeStruct((blocks, rows, width // 2), BF16)] * 2,
        scratch_shapes=[pltpu.VMEM(raw.shape, BF16), pltpu.SemaphoreType.DMA((blocks,))],
        compiler_params=pltpu.CompilerParams(vmem_limit_bytes=8 * MIB),
        cost_estimate=pl.CostEstimate(
            flops=6 * blocks * rows * width, bytes_accessed=4 * MIB, transcendentals=0
        ),
        name="widen",
    )(at, stats, raw)


def correlate_body(keep, other, lhs, *parts):
    blocks, rows, half = other.shape
    quarter = lhs.shape[0] // 4
    for g in range(blocks):
        rhs = jnp.concatenate([keep[g], other[g]], axis=0)
        for turned in range(4):
            part = jnp.dot(
                lhs[turned * quarter : (turned + 1) * quarter],
                rhs,
                preferred_element_type=F32,
            )
            parts[turned][g] = part.astype(BF16)


def correlate(keep, other, lhs):
    blocks, rows, half = other.shape
    part = jax.ShapeDtypeStruct((blocks, lhs.shape[0] // 4, half), BF16)
    return pl.pallas_call(
        correlate_body,
        in_specs=[VMEM] * 3,
        out_specs=[VMEM] * 4,
        out_shape=[part] * 4,
        compiler_params=pltpu.CompilerParams(vmem_limit_bytes=6 * MIB),
        cost_estimate=pl.CostEstimate(
            flops=8 * rows * half * half * blocks, bytes_accessed=4 * MIB, transcendentals=0
        ),
        name="correlate",
    )(keep, other, lhs)


def tile_body(scale, at, diagonal, own, ahead, behind, across, pull, outward):
    blocks, quarter, half = pull.shape
    row = lax.broadcasted_iota(jnp.int32, (quarter, half), 0)
    col = lax.broadcasted_iota(jnp.int32, (quarter, half), 1)
    same = col + at[2] * half == row + at[4] * quarter
    size = jnp.zeros((8, half), F32)
    for g in range(blocks):
        total = (own[g].astype(F32) + across[g].astype(F32)) + (
            ahead[g].astype(F32) + behind[g].astype(F32)
        )
        value = jnp.where(same & (at[3] == g), 0.0, scale * total).astype(BF16)
        pull[g] = value
        outward[g, :quarter] = value
        wide = value.astype(F32)
        size = size + jnp.sum((wide * wide).reshape(quarter // 8, 8, half), axis=0)
    share = diagonal[0:1, 0:1] + (0.25 / OFF_WEIGHT) * jnp.sum(size).reshape(1, 1)
    share = jnp.broadcast_to(share, (EXTRA, half))
    high = share.astype(BF16)
    share = share - high.astype(F32)
    middle = share.astype(BF16)
    low = (share - middle.astype(F32)).astype(BF16)
    line = lax.broadcasted_iota(jnp.int32, (EXTRA, half), 0)
    extra = jnp.where(line == 0, high, jnp.where(line == 1, middle, low))
    for g in range(blocks):
        outward[g, quarter:] = extra


def make_tile(at, scale, diagonal, pieces):
    blocks, quarter, half = pieces[0].shape
    return pl.pallas_call(
        functools.partial(tile_body, scale),
        in_specs=[SMEM] + [VMEM] * 5,
        out_specs=[VMEM] * 2,
        out_shape=[
            jax.ShapeDtypeStruct(pieces[0].shape, BF16),
            jax.ShapeDtypeStruct((blocks, quarter + EXTRA, half), BF16),
        ],
        compiler_params=pltpu.CompilerParams(vmem_limit_bytes=6 * MIB),
        cost_estimate=pl.CostEstimate(
            flops=6 * pieces[0].size, bytes_accessed=3 * MIB, transcendentals=0
        ),
        name="tile",
    )(at, diagonal, *pieces)


def place(at, turned, quarter):
    spot = lax.rem(at[4] + turned, 4) * quarter
    return pl.ds(pl.multiple_of(spot, quarter), quarter)


def finish(view, norm, vec, total, extra, weight, mean_row, left_row, images):
    mean, inverse = vec[mean_row : mean_row + 1], vec[mean_row + 2 : mean_row + 3]
    pull, match, left = vec[4:5], vec[5:6], vec[left_row : left_row + 1]
    back = total + norm.astype(F32) * pull
    centre = (extra + pull * left) * (1.0 / images)
    along = weight + pull * match
    white = (view.astype(F32) - mean) * inverse
    return (inverse * (back - centre - white * along)).astype(BF16)


def rows_body(at, near, far, stats, *refs):
    pieces, (near_part, far_part, packed) = refs[:4], refs[4:]
    blocks, rows, half = near.shape
    width = 2 * half
    cols = pl.ds(pl.multiple_of(at[2] * half, half), half)
    ones = jnp.ones((EXTRA, half), BF16)
    size = jnp.zeros((EXTRA, width), F32)
    for g in range(blocks):
        for turned in range(4):
            packed[place(at, turned, width // 4)] = pieces[turned][g]
        rhs = packed[...]
        square = rhs.astype(F32)
        square = (square * square).astype(BF16)
        size = size + lax.dot_general(
            ones, square, CONTRACT_LAST, preferred_element_type=F32
        )
        extra = jnp.broadcast_to(stats[g, 5:6, cols], (EXTRA, half)).astype(BF16)
        lhs = jnp.concatenate([far[g], extra], axis=0)
        far_more = lax.dot_general(lhs, rhs, CONTRACT_LAST, preferred_element_type=F32)
        near_more = lax.dot_general(
            near[g], rhs, CONTRACT_LAST, preferred_element_type=F32
        )
        if g:
            far_part[: rows + EXTRA] += far_more
            near_part[:rows] += near_more
        else:
            far_part[: rows + EXTRA] = far_more
            near_part[:rows] = near_more
    far_part[rows + 8 : rows + EXTRA] = size[:8] * (0.5 / OFF_WEIGHT)
    near_part[rows:] = far_part[rows:]


def cols_body(images, at, near, far, stats, view, norm, vec, *refs):
    pieces, (near_grad, far_grad, loss, packed, total) = refs[:4], refs[4:]
    blocks, rows, width = near.shape
    half = width // 2
    spot = pl.ds(pl.multiple_of(at[2] * half, half), half)
    size = jnp.zeros((1, half), F32)
    for g in range(blocks):
        for turned in range(4):
            packed[g, place(at, turned, width // 4)] = pieces[turned][g, : width // 4]
        rhs = packed[g]
        square = rhs.astype(F32)
        size = size + jnp.sum(square * square, axis=0, keepdims=True)
        extra = jnp.broadcast_to(stats[g, 4:5], (EXTRA, width)).astype(BF16)
        lhs = jnp.concatenate([near[g], far[g], extra], axis=0)
        part = jnp.dot(lhs, rhs, preferred_element_type=F32)
        if g:
            total[...] += part
        else:
            total[...] = part
    shares = []
    for turned in range(4):
        share = jnp.zeros((1, 128), F32)
        for g in range(blocks):
            lines = pieces[turned][g, width // 4 :, :128].astype(F32)
            share = share + ((lines[0:1] + lines[1:2]) + lines[2:3])
        shares.append(share)
    loss[...] = (shares[0] + shares[2]) + (shares[1] + shares[3])
    weight = size * (0.5 / OFF_WEIGHT)
    for which, grad in enumerate((near_grad, far_grad)):
        part = slice(which * rows, (which + 1) * rows)
        grad[...] = finish(
            view[part, spot],
            norm[part, spot],
            vec[:, spot],
            total[part],
            total[2 * rows : 2 * rows + 1],
            weight,
            1,
            6,
            images,
        )


def gradient(body, outs, scratch, name, *operands):
    return pl.pallas_call(
        body,
        in_specs=[SMEM] + [VMEM] * (len(operands) - 1),
        out_specs=[VMEM] * len(outs),
        out_shape=outs,
        scratch_shapes=scratch,
        compiler_params=pltpu.CompilerParams(vmem_limit_bytes=10 * MIB),
        cost_estimate=pl.CostEstimate(
            flops=1 << 30, bytes_accessed=7 * MIB, transcendentals=0
        ),
        name=name,
    )(*operands)


def local(view_a, view_b):
    rows, width = view_a.shape
    chips = lax.axis_size("y") * lax.axis_size("x")
    blocks = lax.axis_size("z")
    images = rows * 2 * chips
    half = width // 2
    x_at, y_at, c_at, z_at = (lax.axis_index(name) for name in ("x", "y", "c", "z"))
    first_at = jnp.where(c_at == 0, x_at, y_at)
    at = jnp.stack([x_at, y_at, c_at, z_at, first_at]).astype(jnp.int32)

    raw_b = lax.all_gather(view_b, "z", axis=0, tiled=False)
    raw_a = lax.all_gather(view_a, "z", axis=0, tiled=False)
    chip_view = jnp.concatenate([view_b, swap(view_b)], axis=0)

    values_a = view_a.astype(F32)
    values_b = view_b.astype(F32)
    local_a = jnp.sum(values_a, axis=0) / rows
    local_b = jnp.sum(values_b, axis=0) / rows
    apart_a = values_a - local_a
    apart_b = values_b - local_b
    mine = jnp.stack(
        [
            local_a,
            local_b,
            jnp.sum(apart_a * apart_a, axis=0),
            jnp.sum(apart_b * apart_b, axis=0),
            jnp.sum(apart_a * apart_b, axis=0),
        ]
    )
    pair = swap(mine)
    gap = mine[:2] - pair[:2]
    joined = jnp.concatenate(
        [
            (mine[:2] + pair[:2]) * 0.5,
            mine[2:4] + pair[2:4] + gap * gap * (rows / 2),
            mine[4:] + pair[4:] + gap[:1] * gap[1:] * (rows / 2),
        ]
    )
    all_stats = spread(joined, PLANE, chips)
    means = jnp.sum(all_stats[:, :2], axis=0) / chips
    away = all_stats[:, :2] - means
    squares = jnp.sum(all_stats[:, 2:4] + 2 * rows * away * away, axis=0)
    cross = jnp.sum(all_stats[:, 4] + 2 * rows * away[:, 0] * away[:, 1], axis=0)
    inverse = lax.rsqrt(squares / images + EPSILON)
    on_diagonal = cross / images * inverse[0] * inverse[1]
    deficit = 1.0 - on_diagonal
    pull_diagonal = lax.reduce_precision(-2.0 * deficit, 8, 7)
    norm_a = rounded(view_a, means[0], inverse[0])
    norm_b = rounded(view_b, means[1], inverse[1])

    left = inverse * (2 * rows * jnp.sum(all_stats[:, :2], axis=0) - images * means)
    stats = jnp.concatenate([means, inverse, left])
    wide_stats = spread(stats, "z", blocks)
    vec = jnp.concatenate([stats[:4], pull_diagonal[None], on_diagonal[None], left])

    chip_a = jnp.concatenate([norm_a, swap(norm_a)], axis=0)
    lhs = rotate(chip_a.T.reshape(4, width // 4, 2 * rows), first_at).reshape(width, 2 * rows)

    diagonal = jnp.sum((deficit * deficit).reshape(4, width // 4), axis=1)
    diagonal = 0.5 * lax.dynamic_slice_in_dim(diagonal, first_at, 1, axis=0)
    diagonal = jnp.broadcast_to(diagonal[None], (1, 128))
    raw_b, wide_stats, lhs, chip_a, chip_view, vec, diagonal = lax.optimization_barrier(
        (raw_b, wide_stats, lhs, chip_a, chip_view, vec, diagonal)
    )
    near_b, give = widen(at, wide_stats, raw_b)
    far_b = swap(give)
    parts = correlate(near_b, far_b, lhs)
    total = parts[0].astype(F32)
    for step in (1, 3, 2):
        total = total + shift(parts[step], step).astype(F32)
    total = total.astype(BF16)
    pull, outward = make_tile(
        at, 2.0 * OFF_WEIGHT / images, diagonal, [total] + others(total, second=True)
    )
    inward = lax.all_to_all(outward, "z", split_axis=0, concat_axis=0, tiled=True)

    ahead, behind, across = others(pull)
    row_pieces = [pull, behind, across, ahead]
    row_pieces, inward, raw_a = lax.optimization_barrier((row_pieces, inward, raw_a))
    ahead, behind, across = others(inward)
    col_pieces = [inward, behind, across, ahead]

    wide_a = rounded(raw_a, wide_stats[:, 0:1], wide_stats[:, 2:3])
    far_a = rounded(swap(raw_a), wide_stats[:, 0:1], wide_stats[:, 2:3])

    part = jax.ShapeDtypeStruct((rows + EXTRA, width), F32)
    near_part, far_part = gradient(
        rows_body,
        [part, part],
        [pltpu.VMEM((width, half), BF16)],
        "rows",
        at,
        near_b,
        far_b,
        wide_stats,
        *row_pieces,
    )
    far_a, far_part = lax.optimization_barrier((far_a, far_part))
    near_part = near_part + swap(far_part)
    grad_a = finish(
        view_a,
        norm_b,
        vec,
        near_part[:rows],
        near_part[rows : rows + 1],
        near_part[rows + 8 : rows + 9],
        0,
        7,
        images,
    )
    near_grad, far_grad, loss = gradient(
        functools.partial(cols_body, images),
        [jax.ShapeDtypeStruct((rows, half), BF16)] * 2 + [jax.ShapeDtypeStruct((1, 128), F32)],
        [pltpu.VMEM((blocks, width, half), BF16), pltpu.VMEM((2 * rows + EXTRA, half), F32)],
        "cols",
        at,
        wide_a,
        far_a,
        wide_stats,
        chip_view,
        chip_a,
        vec,
        *col_pieces,
    )
    loss_value = (loss + swap(loss))[0, 0]
    other_grad = swap(far_grad)
    grad_b = jnp.where(
        c_at == 0,
        jnp.concatenate([near_grad, other_grad], axis=1),
        jnp.concatenate([other_grad, near_grad], axis=1),
    )
    return (grad_a, grad_b, loss_value)


def solution(mesh):
    split = P(("y", "x", "c"), "z")
    chips = Mesh(mesh.devices.reshape(4, 4, 2, 8), ("y", "x", "c", "z"))
    return jax.shard_map(
        local,
        mesh=chips,
        in_specs=(split, split),
        out_specs=(split, split, P()),
        check_vma=False,
    )
```

profile of v0, /device:TPU:1, one launch (start us, length us, event | category | flops | bytes accessed | tf_op | source)
XLA Modules:
  0.0 155.8 jit_solution(15402420317362786854)
XLA Ops:
  7.2 0.7 all-gather.5.cloned.1.call-update
  7.9 1.0 convert_reduce_fusion.1
  8.9 1.0 convert_reduce_fusion
  10.0 1.2 fusion.5
  11.2 3.3 %collective-permute-start = (f32[5,512]{1,0:T(8,128)S(1)}, f32[5,512]{1,0:T(8,128)S(1)}, u32[]{:S(2)}, u32[]{:S(2)}) collective-permute-start(f32[5,512]{1,0:T(8,128)S(1)} %stack.40), channel_id=1, source_target_pairs={{0,8},{8,0},{1,9},{9,1},{2,10},{10,2},{3,11},{11,3},{4,12},{12,4},... | collective-permute-start | bytes 30728 | tf_op jit(solution)/shard_map/ppermute | solution.py:36
  14.5 0.8 collective-permute-done
  15.4 0.7 broadcast_in_dim.8
  16.2 5.0 %all-to-all-start = ((f32[16,5,512]{2,1,0:T(8,128)}), f32[16,5,512]{2,1,0:T(8,128)S(1)}, u32[]{:S(2)}, u32[]{:S(2)}) async-start(f32[16,5,512]{2,1,0:T(8,128)} %broadcast_in_dim.8), calls=%async_computation | async-start | bytes 524288 | tf_op jit(solution)/shard_map/all_to_all | solution.py:41
  21.3 0.7 collective-permute-start.2
  22.1 7.3 %all-to-all-done = f32[16,5,512]{2,1,0:T(8,128)S(1)} async-done(((f32[16,5,512]{2,1,0:T(8,128)}), f32[16,5,512]{2,1,0:T(8,128)S(1)}, u32[]{:S(2)}, u32[]{:S(2)}) %all-to-all-start) | async-done | bytes 163872 | tf_op jit(solution)/shard_map/all_to_all | solution.py:41
  29.7 1.6 %collective-permute-start.1 = (bf16[256,512]{1,0:T(8,128)(2,1)S(1)}, bf16[256,512]{1,0:T(8,128)(2,1)S(1)}, u32[]{:S(2)}, u32[]{:S(2)}) collective-permute-start(bf16[256,512]{1,0:T(8,128)(2,1)S(1)} %fusion.11), channel_id=1, source_target_pairs={{0,8},{8,0},{1,9},{9,1},{2,10},{10,2},{3,11},{11,3},{4,12},{12,4},... | collective-permute-start | bytes 786440 | tf_op jit(solution)/shard_map/ppermute | solution.py:36
  31.3 0.7 broadcast_in_dim.9
  31.9 8.2 %all-to-all-start.1 = ((f32[8,6,512]{2,1,0:T(8,128)}), f32[8,6,512]{2,1,0:T(8,128)S(1)}, u32[]{:S(2)}, u32[]{:S(2)}) async-start(f32[8,6,512]{2,1,0:T(8,128)} %broadcast_in_dim.9), calls=%async_computation.1 | async-start | bytes 262144 | tf_op jit(solution)/shard_map/all_to_all | solution.py:41
  41.8 1.0 fusion.17
  43.1 7.0 %all-to-all-done.1.stats = f32[8,6,512]{2,1,0:T(8,128)S(1)} async-done(((f32[8,6,512]{2,1,0:T(8,128)}), f32[8,6,512]{2,1,0:T(8,128)S(1)}, u32[]{:S(2)}, u32[]{:S(2)}) %all-to-all-start.1) | async-done | bytes 98336 | tf_op jit(solution)/shard_map/all_to_all | solution.py:41
  50.0 3.6 %all-gather.5.cloned.1.call-done = bf16[2048,512]{1,0:T(8,128)(2,1)} async-done(((bf16[256,512]{1,0:T(8,128)(2,1)}), bf16[2048,512]{1,0:T(8,128)(2,1)}) %all-gather.5.cloned.1.call-update) | async-done | bytes 2097168 | tf_op jit(solution)/shard_map/all_gather | solution.py:282
  53.6 1.6 %copy-done = bf16[2048,512]{1,0:T(8,128)(2,1)S(1)} copy-done((bf16[2048,512]{1,0:T(8,128)(2,1)S(1)}, bf16[2048,512]{1,0:T(8,128)(2,1)}, u32[]{:S(2)}) %copy-start) | copy-done | bytes 2097176
  55.2 1.3 widen.1
  56.5 3.9 %collective-permute-start.3 = (bf16[8,256,256]{2,1,0:T(8,128)(2,1)S(1)}, bf16[8,256,256]{2,1,0:T(8,128)(2,1)S(1)}, u32[]{:S(2)}, u32[]{:S(2)}) collective-permute-start(bf16[8,256,256]{2,1,0:T(8,128)(2,1)S(1)} %get-tuple-element.35), channel_id=1, source_target_pairs={{0,8},{8,0},{1,9},{9,1},{2,10},{10,2},{3,11},{11,3},{4,12},{12,4},... | collective-permute-start | bytes 3145736 | tf_op jit(solution)/shard_map/ppermute | solution.py:36
  60.4 2.3 %collective-permute-done.3.other.far = bf16[8,256,256]{2,1,0:T(8,128)(2,1)S(1)} collective-permute-done((bf16[8,256,256]{2,1,0:T(8,128)(2,1)S(1)}, bf16[8,256,256]{2,1,0:T(8,128)(2,1)S(1)}, u32[]{:S(2)}, u32[]{:S(2)}) %collective-permute-start.3) | collective-permute-done | bytes 1048608 | tf_op jit(solution)/shard_map/ppermute | solution.py:36
  62.7 1.3 correlate.1
  64.0 2.8 %collective-permute-start.6 = (bf16[8,128,256]{2,1,0:T(8,128)(2,1)S(1)}, bf16[8,128,256]{2,1,0:T(8,128)(2,1)S(1)}, u32[]{:S(2)}, u32[]{:S(2)}) collective-permute-start(bf16[8,128,256]{2,1,0:T(8,128)(2,1)S(1)} %get-tuple-element.41), channel_id=1, source_target_pairs={{0,32},{8,136},{16,48},{24,152},{32,0},{40,168},{48,16},{56,184},{... | collective-permute-start | bytes 1572872 | tf_op jit(solution)/shard_map/ppermute | solution.py:32
  66.8 0.9 collective-permute-start.5
  68.3 5.7 %collective-permute-done.6 = bf16[8,128,256]{2,1,0:T(8,128)(2,1)S(1)} collective-permute-done((bf16[8,128,256]{2,1,0:T(8,128)(2,1)S(1)}, bf16[8,128,256]{2,1,0:T(8,128)(2,1)S(1)}, u32[]{:S(2)}, u32[]{:S(2)}) %collective-permute-start.6) | collective-permute-done | bytes 524320 | tf_op jit(solution)/shard_map/ppermute | solution.py:32
  73.9 5.9 %collective-permute-done.5 = bf16[8,128,256]{2,1,0:T(8,128)(2,1)S(1)} collective-permute-done((bf16[8,128,256]{2,1,0:T(8,128)(2,1)S(1)}, bf16[8,128,256]{2,1,0:T(8,128)(2,1)S(1)}, u32[]{:S(2)}, u32[]{:S(2)}) %collective-permute-start.5) | collective-permute-done | bytes 524320 | tf_op jit(solution)/shard_map/ppermute | solution.py:32
  80.1 1.1 collective-permute-start.7
  81.2 1.6 %collective-permute-start.8 = (bf16[8,128,256]{2,1,0:T(8,128)(2,1)S(1)}, bf16[8,128,256]{2,1,0:T(8,128)(2,1)S(1)}, u32[]{:S(2)}, u32[]{:S(2)}) collective-permute-start(bf16[8,128,256]{2,1,0:T(8,128)(2,1)S(1)} %add_convert_fusion.own), channel_id=1, source_target_pairs={{0,192},{8,56},{16,208},{24,8},{32,224},{40,24},{48,240},{56,40},{... | collective-permute-start | bytes 1572872 | tf_op jit(solution)/shard_map/ppermute | solution.py:32
  82.8 1.6 %collective-permute-start.9 = (bf16[8,128,256]{2,1,0:T(8,128)(2,1)S(1)}, bf16[8,128,256]{2,1,0:T(8,128)(2,1)S(1)}, u32[]{:S(2)}, u32[]{:S(2)}) collective-permute-start(bf16[8,128,256]{2,1,0:T(8,128)(2,1)S(1)} %add_convert_fusion.own), channel_id=1, source_target_pairs={{0,128},{8,40},{16,144},{24,56},{32,160},{40,8},{48,176},{56,24},{... | collective-permute-start | bytes 1572872 | tf_op jit(solution)/shard_map/ppermute | solution.py:32
  84.5 5.3 %collective-permute-done.7.ahead = bf16[8,128,256]{2,1,0:T(8,128)(2,1)S(1)} collective-permute-done((bf16[8,128,256]{2,1,0:T(8,128)(2,1)S(1)}, bf16[8,128,256]{2,1,0:T(8,128)(2,1)S(1)}, u32[]{:S(2)}, u32[]{:S(2)}) %collective-permute-start.7) | collective-permute-done | bytes 524320 | tf_op jit(solution)/shard_map/ppermute | solution.py:32
  89.8 4.8 %collective-permute-done.8.behind = bf16[8,128,256]{2,1,0:T(8,128)(2,1)S(1)} collective-permute-done((bf16[8,128,256]{2,1,0:T(8,128)(2,1)S(1)}, bf16[8,128,256]{2,1,0:T(8,128)(2,1)S(1)}, u32[]{:S(2)}, u32[]{:S(2)}) %collective-permute-start.8) | collective-permute-done | bytes 524320 | tf_op jit(solution)/shard_map/ppermute | solution.py:32
  94.6 1.8 %collective-permute-done.9.across = bf16[8,128,256]{2,1,0:T(8,128)(2,1)S(1)} collective-permute-done((bf16[8,128,256]{2,1,0:T(8,128)(2,1)S(1)}, bf16[8,128,256]{2,1,0:T(8,128)(2,1)S(1)}, u32[]{:S(2)}, u32[]{:S(2)}) %collective-permute-start.9) | collective-permute-done | bytes 524320 | tf_op jit(solution)/shard_map/ppermute | solution.py:32
  96.4 2.1 %tile.1 = (bf16[8,128,256]{2,1,0:T(8,128)(2,1)S(1)}, bf16[8,144,256]{2,1,0:T(8,128)(2,1)}) custom-call(s32[5]{0:T(128)S(1)} %stack.47.at, f32[1,128]{1,0:T(1,128)S(1)} %broadcast_in_dim.11.diagonal, bf16[8,128,256]{2,1,0:T(8,128)(2,1)S(1)} %add_convert_fusion.own, bf16[8,128,256]{2,1,0:T(8,128)(2,1)S(1)} %collective-permute-done.7.ahead, ...), custom_call_target="tpu_custom_call" | custom-call | flops 1572864 | bytes 3145728 | tf_op jit(solution)/shard_map/tile/pallas_call | solution.py:151
  98.4 4.1 %all-to-all-start.2 = ((bf16[8,144,256]{2,1,0:T(8,128)(2,1)}), bf16[8,144,256]{2,1,0:T(8,128)(2,1)S(1)}, u32[]{:S(2)}, u32[]{:S(2)}) async-start(bf16[8,144,256]{2,1,0:T(8,128)(2,1)} %get-tuple-element.43), calls=%async_computation.2 | async-start | bytes 1179648 | tf_op jit(solution)/shard_map/all_to_all | solution.py:346
  102.5 1.8 %collective-permute-start.10 = (bf16[8,128,256]{2,1,0:T(8,128)(2,1)S(1)}, bf16[8,128,256]{2,1,0:T(8,128)(2,1)}, u32[]{:S(2)}, u32[]{:S(2)}) collective-permute-start(bf16[8,128,256]{2,1,0:T(8,128)(2,1)S(1)} %get-tuple-element.44.refs_0_), channel_id=1, source_target_pairs={{0,48},{8,200},{16,0},{24,216},{32,16},{40,232},{48,32},{56,248},{... | collective-permute-start | bytes 1572872 | tf_op jit(solution)/shard_map/ppermute | solution.py:32
  104.4 0.7 collective-permute-start.11
  105.5 10.6 %collective-permute-done.10.refs_1_ = bf16[8,128,256]{2,1,0:T(8,128)(2,1)} collective-permute-done((bf16[8,128,256]{2,1,0:T(8,128)(2,1)S(1)}, bf16[8,128,256]{2,1,0:T(8,128)(2,1)}, u32[]{:S(2)}, u32[]{:S(2)}) %collective-permute-start.10) | collective-permute-done | bytes 524320 | tf_op jit(solution)/shard_map/ppermute | solution.py:32
  116.1 3.8 %collective-permute-done.12.refs_3_ = bf16[8,128,256]{2,1,0:T(8,128)(2,1)} collective-permute-done((bf16[8,128,256]{2,1,0:T(8,128)(2,1)S(1)}, bf16[8,128,256]{2,1,0:T(8,128)(2,1)}, u32[]{:S(2)}, u32[]{:S(2)}) %collective-permute-start.12) | collective-permute-done | bytes 524320 | tf_op jit(solution)/shard_map/ppermute | solution.py:32
  119.9 3.5 %collective-permute-start.13 = (bf16[8,256,512]{2,1,0:T(8,128)(2,1)}, bf16[8,256,512]{2,1,0:T(8,128)(2,1)S(1)}, u32[]{:S(2)}, u32[]{:S(2)}) collective-permute-start(bf16[8,256,512]{2,1,0:T(8,128)(2,1)} %bitcast.48), channel_id=1, source_target_pairs={{0,8},{8,0},{1,9},{9,1},{2,10},{10,2},{3,11},{11,3},{4,12},{12,4},... | collective-permute-start | bytes 6291464 | tf_op jit(solution)/shard_map/ppermute | solution.py:36
  123.5 2.7 %collective-permute-start.15 = (bf16[8,144,256]{2,1,0:T(8,128)(2,1)S(1)}, bf16[8,144,256]{2,1,0:T(8,128)(2,1)S(1)}, u32[]{:S(2)}, u32[]{:S(2)}) collective-permute-start(bf16[8,144,256]{2,1,0:T(8,128)(2,1)S(1)} %all-to-all-done.2.refs_0_), channel_id=1, source_target_pairs={{0,48},{8,200},{16,0},{24,216},{32,16},{40,232},{48,32},{56,248},{... | collective-permute-start | bytes 1769480 | tf_op jit(solution)/shard_map/ppermute | solution.py:32
  126.9 1.2 copy-done.2
  128.1 3.8 %rows.1 = (f32[272,512]{1,0:T(8,128)S(1)}, f32[272,512]{1,0:T(8,128)S(1)}) custom-call(s32[5]{0:T(128)S(1)} %stack.47.at, bf16[8,256,256]{2,1,0:T(8,128)(2,1)S(1)} %get-tuple-element.34.keep.near, bf16[8,256,256]{2,1,0:T(8,128)(2,1)S(1)} %copy-done.2, f32[8,6,512]{2,1,0:T(8,128)S(1)} %all-to-all-done.1.stats, ...), custom_call_target="tpu_custom_call" | custom-call | flops 1073741824 | bytes 7340032 | tf_op jit(solution)/shard_map/rows/pallas_call | solution.py:258
  131.9 1.1 reduce-precision_convert_fusion
  133.1 6.2 %collective-permute-done.15.refs_1_ = bf16[8,144,256]{2,1,0:T(8,128)(2,1)S(1)} collective-permute-done((bf16[8,144,256]{2,1,0:T(8,128)(2,1)S(1)}, bf16[8,144,256]{2,1,0:T(8,128)(2,1)S(1)}, u32[]{:S(2)}, u32[]{:S(2)}) %collective-permute-start.15) | collective-permute-done | bytes 589856 | tf_op jit(solution)/shard_map/ppermute | solution.py:32
  139.3 3.4 %collective-permute-done.17.refs_3_ = bf16[8,144,256]{2,1,0:T(8,128)(2,1)S(1)} collective-permute-done((bf16[8,144,256]{2,1,0:T(8,128)(2,1)S(1)}, bf16[8,144,256]{2,1,0:T(8,128)(2,1)S(1)}, u32[]{:S(2)}, u32[]{:S(2)}) %collective-permute-start.17) | collective-permute-done | bytes 589856 | tf_op jit(solution)/shard_map/ppermute | solution.py:32
  142.7 2.3 %cols.1 = (bf16[256,256]{1,0:T(8,128)(2,1)S(1)}, bf16[256,256]{1,0:T(8,128)(2,1)S(1)}, f32[1,128]{1,0:T(1,128)S(1)}) custom-call(s32[5]{0:T(128)S(1)} %stack.47.at, bf16[8,256,512]{2,1,0:T(8,128)(2,1)S(1)} %get-tuple-element.77.near, bf16[8,256,512]{2,1,0:T(8,128)(2,1)S(1)} %get-tuple-element.52.far, f32[8,6,512]{2,1,0:T(8,128)S(1)} %all-to-all-done.1.stats, ...), custom_call_target="tpu_custom_call" | custom-call | flops 1073741824 | bytes 7340032 | tf_op jit(solution)/shard_map/cols/pallas_call | solution.py:258
  145.7 0.8 collective-permute-done.19
  147.0 0.8 maximum_select_fusion
  148.0 0.9 fusion.16
  (66 shorter events, 5.2 us)
Async XLA Ops:
  7.2 14.1 %copy-start.5 = (bf16[256,512]{1,0:T(8,128)(2,1)S(1)}, bf16[256,512]{1,0:T(8,128)(2,1)}, u32[]{:S(2)}) copy-start(bf16[256,512]{1,0:T(8,128)(2,1)} %param.3) | copy-start | bytes 786436
  7.2 22.4 %copy-start.3 = (bf16[256,512]{1,0:T(8,128)(2,1)S(1)}, bf16[256,512]{1,0:T(8,128)(2,1)}, u32[]{:S(2)}) copy-start(bf16[256,512]{1,0:T(8,128)(2,1)} %param.2) | copy-start | bytes 786436
  7.2 46.4 %all-gather.5.cloned.1.call-start = ((), (), s32[]{:S(2)}) async-start(), calls=%async_computation.3 | async-start | bytes 2359296 | tf_op jit(solution)/shard_map/all_gather | solution.py:282
  11.2 4.2 %collective-permute-start = (f32[5,512]{1,0:T(8,128)S(1)}, f32[5,512]{1,0:T(8,128)S(1)}, u32[]{:S(2)}, u32[]{:S(2)}) collective-permute-start(f32[5,512]{1,0:T(8,128)S(1)} %stack.40), channel_id=1, source_target_pairs={{0,8},{8,0},{1,9},{9,1},{2,10},{10,2},{3,11},{11,3},{4,12},{12,4},... | collective-permute-start | bytes 30728 | tf_op jit(solution)/shard_map/ppermute | solution.py:36
  16.2 13.2 %all-to-all-start = ((f32[16,5,512]{2,1,0:T(8,128)}), f32[16,5,512]{2,1,0:T(8,128)S(1)}, u32[]{:S(2)}, u32[]{:S(2)}) async-start(f32[16,5,512]{2,1,0:T(8,128)} %broadcast_in_dim.8), calls=%async_computation | async-start | bytes 524288 | tf_op jit(solution)/shard_map/all_to_all | solution.py:41
  21.2 84.3 %all-gather.7.cloned.1.call-start = ((), (), s32[]{:S(2)}) async-start(), calls=%async_computation.4 | async-start | bytes 2359296 | tf_op jit(solution)/shard_map/all_gather | solution.py:283
  21.3 20.3 %collective-permute-start.2 = (bf16[256,512]{1,0:T(8,128)(2,1)S(1)}, bf16[256,512]{1,0:T(8,128)(2,1)S(1)}, u32[]{:S(2)}, u32[]{:S(2)}) collective-permute-start(bf16[256,512]{1,0:T(8,128)(2,1)S(1)} %copy-done.5), channel_id=1, source_target_pairs={{0,8},{8,0},{1,9},{9,1},{2,10},{10,2},{3,11},{11,3},{4,12},{12,4},... | collective-permute-start | bytes 786440 | tf_op jit(solution)/shard_map/ppermute | solution.py:36
  29.7 11.9 %collective-permute-start.1 = (bf16[256,512]{1,0:T(8,128)(2,1)S(1)}, bf16[256,512]{1,0:T(8,128)(2,1)S(1)}, u32[]{:S(2)}, u32[]{:S(2)}) collective-permute-start(bf16[256,512]{1,0:T(8,128)(2,1)S(1)} %fusion.11), channel_id=1, source_target_pairs={{0,8},{8,0},{1,9},{9,1},{2,10},{10,2},{3,11},{11,3},{4,12},{12,4},... | collective-permute-start | bytes 786440 | tf_op jit(solution)/shard_map/ppermute | solution.py:36
  31.9 18.1 %all-to-all-start.1 = ((f32[8,6,512]{2,1,0:T(8,128)}), f32[8,6,512]{2,1,0:T(8,128)S(1)}, u32[]{:S(2)}, u32[]{:S(2)}) async-start(f32[8,6,512]{2,1,0:T(8,128)} %broadcast_in_dim.9), calls=%async_computation.1 | async-start | bytes 262144 | tf_op jit(solution)/shard_map/all_to_all | solution.py:41
  53.6 1.6 %copy-start = (bf16[2048,512]{1,0:T(8,128)(2,1)S(1)}, bf16[2048,512]{1,0:T(8,128)(2,1)}, u32[]{:S(2)}) copy-start(bf16[2048,512]{1,0:T(8,128)(2,1)} %all-gather.5.cloned.1.call-done) | copy-start | bytes 6291460
  56.5 6.2 %collective-permute-start.3 = (bf16[8,256,256]{2,1,0:T(8,128)(2,1)S(1)}, bf16[8,256,256]{2,1,0:T(8,128)(2,1)S(1)}, u32[]{:S(2)}, u32[]{:S(2)}) collective-permute-start(bf16[8,256,256]{2,1,0:T(8,128)(2,1)S(1)} %get-tuple-element.35), channel_id=1, source_target_pairs={{0,8},{8,0},{1,9},{9,1},{2,10},{10,2},{3,11},{11,3},{4,12},{12,4},... | collective-permute-start | bytes 3145736 | tf_op jit(solution)/shard_map/ppermute | solution.py:36
  62.7 17.1 %copy-start.1 = (bf16[8,256,256]{2,1,0:T(8,128)(2,1)}, bf16[8,256,256]{2,1,0:T(8,128)(2,1)S(1)}, u32[]{:S(2)}) copy-start(bf16[8,256,256]{2,1,0:T(8,128)(2,1)S(1)} %collective-permute-done.3.other.far) | copy-start | bytes 3145732
  64.0 10.0 %collective-permute-start.6 = (bf16[8,128,256]{2,1,0:T(8,128)(2,1)S(1)}, bf16[8,128,256]{2,1,0:T(8,128)(2,1)S(1)}, u32[]{:S(2)}, u32[]{:S(2)}) collective-permute-start(bf16[8,128,256]{2,1,0:T(8,128)(2,1)S(1)} %get-tuple-element.41), channel_id=1, source_target_pairs={{0,32},{8,136},{16,48},{24,152},{32,0},{40,168},{48,16},{56,184},{... | collective-permute-start | bytes 1572872 | tf_op jit(solution)/shard_map/ppermute | solution.py:32
  66.8 13.0 %collective-permute-start.5 = (bf16[8,128,256]{2,1,0:T(8,128)(2,1)S(1)}, bf16[8,128,256]{2,1,0:T(8,128)(2,1)S(1)}, u32[]{:S(2)}, u32[]{:S(2)}) collective-permute-start(bf16[8,128,256]{2,1,0:T(8,128)(2,1)S(1)} %get-tuple-element.40), channel_id=1, source_target_pairs={{0,48},{8,200},{16,0},{24,216},{32,16},{40,232},{48,32},{56,248},{... | collective-permute-start | bytes 1572872 | tf_op jit(solution)/shard_map/ppermute | solution.py:32
  67.7 12.1 %collective-permute-start.4 = (bf16[8,128,256]{2,1,0:T(8,128)(2,1)S(1)}, bf16[8,128,256]{2,1,0:T(8,128)(2,1)S(1)}, u32[]{:S(2)}, u32[]{:S(2)}) collective-permute-start(bf16[8,128,256]{2,1,0:T(8,128)(2,1)S(1)} %get-tuple-element.39), channel_id=1, source_target_pairs={{0,16},{8,72},{16,32},{24,88},{32,48},{40,104},{48,0},{56,120},{64... | collective-permute-start | bytes 1572872 | tf_op jit(solution)/shard_map/ppermute | solution.py:32
  80.1 9.7 %collective-permute-start.7 = (bf16[8,128,256]{2,1,0:T(8,128)(2,1)S(1)}, bf16[8,128,256]{2,1,0:T(8,128)(2,1)S(1)}, u32[]{:S(2)}, u32[]{:S(2)}) collective-permute-start(bf16[8,128,256]{2,1,0:T(8,128)(2,1)S(1)} %add_convert_fusion.own), channel_id=1, source_target_pairs={{0,64},{8,24},{16,80},{24,40},{32,96},{40,56},{48,112},{56,8},{64,... | collective-permute-start | bytes 1572872 | tf_op jit(solution)/shard_map/ppermute | solution.py:32
  81.2 13.4 %collective-permute-start.8 = (bf16[8,128,256]{2,1,0:T(8,128)(2,1)S(1)}, bf16[8,128,256]{2,1,0:T(8,128)(2,1)S(1)}, u32[]{:S(2)}, u32[]{:S(2)}) collective-permute-start(bf16[8,128,256]{2,1,0:T(8,128)(2,1)S(1)} %add_convert_fusion.own), channel_id=1, source_target_pairs={{0,192},{8,56},{16,208},{24,8},{32,224},{40,24},{48,240},{56,40},{... | collective-permute-start | bytes 1572872 | tf_op jit(solution)/shard_map/ppermute | solution.py:32
  82.8 13.5 %collective-permute-start.9 = (bf16[8,128,256]{2,1,0:T(8,128)(2,1)S(1)}, bf16[8,128,256]{2,1,0:T(8,128)(2,1)S(1)}, u32[]{:S(2)}, u32[]{:S(2)}) collective-permute-start(bf16[8,128,256]{2,1,0:T(8,128)(2,1)S(1)} %add_convert_fusion.own), channel_id=1, source_target_pairs={{0,128},{8,40},{16,144},{24,56},{32,160},{40,8},{48,176},{56,24},{... | collective-permute-start | bytes 1572872 | tf_op jit(solution)/shard_map/ppermute | solution.py:32
  98.4 21.5 %all-to-all-start.2 = ((bf16[8,144,256]{2,1,0:T(8,128)(2,1)}), bf16[8,144,256]{2,1,0:T(8,128)(2,1)S(1)}, u32[]{:S(2)}, u32[]{:S(2)}) async-start(bf16[8,144,256]{2,1,0:T(8,128)(2,1)} %get-tuple-element.43), calls=%async_computation.2 | async-start | bytes 1179648 | tf_op jit(solution)/shard_map/all_to_all | solution.py:346
  102.5 13.6 %collective-permute-start.10 = (bf16[8,128,256]{2,1,0:T(8,128)(2,1)S(1)}, bf16[8,128,256]{2,1,0:T(8,128)(2,1)}, u32[]{:S(2)}, u32[]{:S(2)}) collective-permute-start(bf16[8,128,256]{2,1,0:T(8,128)(2,1)S(1)} %get-tuple-element.44.refs_0_), channel_id=1, source_target_pairs={{0,48},{8,200},{16,0},{24,216},{32,16},{40,232},{48,32},{56,248},{... | collective-permute-start | bytes 1572872 | tf_op jit(solution)/shard_map/ppermute | solution.py:32
  104.4 11.7 %collective-permute-start.11 = (bf16[8,128,256]{2,1,0:T(8,128)(2,1)S(1)}, bf16[8,128,256]{2,1,0:T(8,128)(2,1)}, u32[]{:S(2)}, u32[]{:S(2)}) collective-permute-start(bf16[8,128,256]{2,1,0:T(8,128)(2,1)S(1)} %get-tuple-element.44.refs_0_), channel_id=1, source_target_pairs={{0,32},{8,136},{16,48},{24,152},{32,0},{40,168},{48,16},{56,184},{... | collective-permute-start | bytes 1572872 | tf_op jit(solution)/shard_map/ppermute | solution.py:32
  105.0 14.9 %collective-permute-start.12 = (bf16[8,128,256]{2,1,0:T(8,128)(2,1)S(1)}, bf16[8,128,256]{2,1,0:T(8,128)(2,1)}, u32[]{:S(2)}, u32[]{:S(2)}) collective-permute-start(bf16[8,128,256]{2,1,0:T(8,128)(2,1)S(1)} %get-tuple-element.44.refs_0_), channel_id=1, source_target_pairs={{0,16},{8,72},{16,32},{24,88},{32,48},{40,104},{48,0},{56,120},{64... | collective-permute-start | bytes 1572872 | tf_op jit(solution)/shard_map/ppermute | solution.py:32
  119.9 12.0 %collective-permute-start.13 = (bf16[8,256,512]{2,1,0:T(8,128)(2,1)}, bf16[8,256,512]{2,1,0:T(8,128)(2,1)S(1)}, u32[]{:S(2)}, u32[]{:S(2)}) collective-permute-start(bf16[8,256,512]{2,1,0:T(8,128)(2,1)} %bitcast.48), channel_id=1, source_target_pairs={{0,8},{8,0},{1,9},{9,1},{2,10},{10,2},{3,11},{11,3},{4,12},{12,4},... | collective-permute-start | bytes 6291464 | tf_op jit(solution)/shard_map/ppermute | solution.py:36
  123.5 15.9 %collective-permute-start.15 = (bf16[8,144,256]{2,1,0:T(8,128)(2,1)S(1)}, bf16[8,144,256]{2,1,0:T(8,128)(2,1)S(1)}, u32[]{:S(2)}, u32[]{:S(2)}) collective-permute-start(bf16[8,144,256]{2,1,0:T(8,128)(2,1)S(1)} %all-to-all-done.2.refs_0_), channel_id=1, source_target_pairs={{0,48},{8,200},{16,0},{24,216},{32,16},{40,232},{48,32},{56,248},{... | collective-permute-start | bytes 1769480 | tf_op jit(solution)/shard_map/ppermute | solution.py:32
  126.2 13.2 %collective-permute-start.16 = (bf16[8,144,256]{2,1,0:T(8,128)(2,1)S(1)}, bf16[8,144,256]{2,1,0:T(8,128)(2,1)S(1)}, u32[]{:S(2)}, u32[]{:S(2)}) collective-permute-start(bf16[8,144,256]{2,1,0:T(8,128)(2,1)S(1)} %all-to-all-done.2.refs_0_), channel_id=1, source_target_pairs={{0,32},{8,136},{16,48},{24,152},{32,0},{40,168},{48,16},{56,184},{... | collective-permute-start | bytes 1769480 | tf_op jit(solution)/shard_map/ppermute | solution.py:32
  126.5 16.3 %collective-permute-start.17 = (bf16[8,144,256]{2,1,0:T(8,128)(2,1)S(1)}, bf16[8,144,256]{2,1,0:T(8,128)(2,1)S(1)}, u32[]{:S(2)}, u32[]{:S(2)}) collective-permute-start(bf16[8,144,256]{2,1,0:T(8,128)(2,1)S(1)} %all-to-all-done.2.refs_0_), channel_id=1, source_target_pairs={{0,16},{8,72},{16,32},{24,88},{32,48},{40,104},{48,0},{56,120},{64... | collective-permute-start | bytes 1769480 | tf_op jit(solution)/shard_map/ppermute | solution.py:32
  126.8 1.2 copy-start.2
  128.1 3.8 %copy-start.7 = (bf16[2048,512]{1,0:T(8,128)(2,1)S(1)}, bf16[2048,512]{1,0:T(8,128)(2,1)}, u32[]{:S(2)}) copy-start(bf16[2048,512]{1,0:T(8,128)(2,1)} %all-gather.7.cloned.1.call-done) | copy-start | bytes 6291460
  133.0 14.9 %collective-permute-start.14 = (f32[272,512]{1,0:T(8,128)S(1)}, f32[272,512]{1,0:T(8,128)S(1)}, u32[]{:S(2)}, u32[]{:S(2)}) collective-permute-start(f32[272,512]{1,0:T(8,128)S(1)} %get-tuple-element.51), channel_id=1, source_target_pairs={{0,8},{8,0},{1,9},{9,1},{2,10},{10,2},{3,11},{11,3},{4,12},{12,4},... | collective-permute-start | bytes 1671176 | tf_op jit(solution)/shard_map/ppermute | solution.py:36
  145.1 2.9 %copy-start.4 = (bf16[256,512]{1,0:T(8,128)(2,1)S(1)}, bf16[256,512]{1,0:T(8,128)(2,1)}, u32[]{:S(2)}) copy-start(bf16[256,512]{1,0:T(8,128)(2,1)} %param.2) | copy-start | bytes 786436
  145.1 2.9 %copy-start.6 = (bf16[256,512]{1,0:T(8,128)(2,1)S(1)}, bf16[256,512]{1,0:T(8,128)(2,1)}, u32[]{:S(2)}) copy-start(bf16[256,512]{1,0:T(8,128)(2,1)} %param.3) | copy-start | bytes 786436
  145.1 2.0 %collective-permute-start.18 = (bf16[256,256]{1,0:T(8,128)(2,1)S(1)}, bf16[256,256]{1,0:T(8,128)(2,1)S(1)}, u32[]{:S(2)}, u32[]{:S(2)}) collective-permute-start(bf16[256,256]{1,0:T(8,128)(2,1)S(1)} %get-tuple-element.57), channel_id=1, source_target_pairs={{0,8},{8,0},{1,9},{9,1},{2,10},{10,2},{3,11},{11,3},{4,12},{12,4},... | collective-permute-start | bytes 393224 | tf_op jit(solution)/shard_map/ppermute | solution.py:36
  145.2 1.3 collective-permute-start.19
Sparse Core Ops, SparseCore 0:
  9.8 43.7 all-gather.4
  55.4 39.2 all-gather.6
where the time goes:
time: 156 us
  waiting for transfers between devices  69.9 us (45%)
  starting transfers between devices  46.1 us (30%)
  between operations  15 us (10%)
  Pallas kernels  10.8 us (7%)
  other arithmetic  8.51 us (5%)
  local copies, waits for them, and re-layouts  5.49 us (4%)
    ppermute x12, waiting for transfers between devices, shift(): return lax.ppermute(value, ('y', 'x', 'c'), pairs)  47.5 us
    ppermute x12, starting transfers between devices, shift(): return lax.ppermute(value, ('y', 'x', 'c'), pairs)  15 us
    all_to_all x2, waiting for transfers between devices, spread(): return lax.all_to_all(copies, axes, split_axis=0, concat_axis=0, tiled=True)  14.2 us
    ppermute x8, starting transfers between devices, swap(): return lax.ppermute(value, 'c', [(0, 1), (1, 0)])  13.7 us
    all_to_all x2, starting transfers between devices, spread(): return lax.all_to_all(copies, axes, split_axis=0, concat_axis=0, tiled=True)  13.2 us
    pallas_call x2, Pallas kernels, gradient(): pl.pallas_call(body, in_specs=[SMEM] + [VMEM] * (len(operands) - 1), out_...  6.14 us
    all_to_all x1, starting transfers between devices, local(): lax.all_to_all(outward, 'z', split_axis=0, concat_axis=0, tiled=True)  4.1 us
    ppermute x8, waiting for transfers between devices, swap(): return lax.ppermute(value, 'c', [(0, 1), (1, 0)])  3.98 us
  transfers between devices with their start and end apart: 25, of which 15 were waited for; matrix products, arithmetic and copies ran while one was open for 6% of the time, Pallas kernels for 7%

commit v1 on v0

--- a/solution.py
+++ b/solution.py
@@ -58,42 +58,16 @@
     return lax.reduce_precision((raw.astype(F32) - mean) * inverse, 8, 7).astype(BF16)
 
 
-def widen_body(at, stats, raw, keep, give, held, done):
-    blocks, _, half = keep.shape
-    copies = [
-        pltpu.make_async_copy(raw.at[g], held.at[g], done.at[g]) for g in range(blocks)
-    ]
-    for copy in copies:
-        copy.start()
-    for g in range(blocks):
-        copies[g].wait()
-        for place, out in enumerate((keep, give)):
-            spot = 1 - at[2] if place else at[2]
-            cols = pl.ds(pl.multiple_of(spot * half, half), half)
-            out[g] = normalise(held[g, :, cols], stats[g, 1:2, cols], stats[g, 3:4, cols])
-
-
-def widen(at, stats, raw):
-    blocks, rows, width = raw.shape
-    return pl.pallas_call(
-        widen_body,
-        in_specs=[SMEM, VMEM, pl.BlockSpec(memory_space=pltpu.HBM)],
-        out_specs=[VMEM] * 2,
-        out_shape=[jax.ShapeDtypeStruct((blocks, rows, width // 2), BF16)] * 2,
-        scratch_shapes=[pltpu.VMEM(raw.shape, BF16), pltpu.SemaphoreType.DMA((blocks,))],
-        compiler_params=pltpu.CompilerParams(vmem_limit_bytes=8 * MIB),
-        cost_estimate=pl.CostEstimate(
-            flops=6 * blocks * rows * width, bytes_accessed=4 * MIB, transcendentals=0
-        ),
-        name="widen",
-    )(at, stats, raw)
-
-
-def correlate_body(keep, other, lhs, *parts):
-    blocks, rows, half = other.shape
+def correlate_body(at, stats, raw, lhs, *parts):
+    blocks, _, half = parts[0].shape
     quarter = lhs.shape[0] // 4
-    for g in range(blocks):
-        rhs = jnp.concatenate([keep[g], other[g]], axis=0)
+    cols = pl.ds(pl.multiple_of(at[2] * half, half), half)
+    near_at, far_at = at[2] * blocks, (1 - at[2]) * blocks
+    for g in range(blocks):
+        mean, inverse = stats[g, 1:2, cols], stats[g, 3:4, cols]
+        near = normalise(raw[near_at + g, :, cols], mean, inverse)
+        far = normalise(raw[far_at + g, :, cols], mean, inverse)
+        rhs = jnp.concatenate([near, far], axis=0)
         for turned in range(4):
             part = jnp.dot(
                 lhs[turned * quarter : (turned + 1) * quarter],
@@ -103,20 +77,21 @@
             parts[turned][g] = part.astype(BF16)
 
 
-def correlate(keep, other, lhs):
-    blocks, rows, half = other.shape
+def correlate(at, stats, raw, lhs):
+    both, rows, width = raw.shape
+    blocks, half = both // 2, width // 2
     part = jax.ShapeDtypeStruct((blocks, lhs.shape[0] // 4, half), BF16)
     return pl.pallas_call(
         correlate_body,
-        in_specs=[VMEM] * 3,
+        in_specs=[SMEM, VMEM, VMEM, VMEM],
         out_specs=[VMEM] * 4,
         out_shape=[part] * 4,
         compiler_params=pltpu.CompilerParams(vmem_limit_bytes=6 * MIB),
         cost_estimate=pl.CostEstimate(
-            flops=8 * rows * half * half * blocks, bytes_accessed=4 * MIB, transcendentals=0
+            flops=8 * rows * half * half * blocks, bytes_accessed=6 * MIB, transcendentals=0
         ),
         name="correlate",
-    )(keep, other, lhs)
+    )(at, stats, raw, lhs)
 
 
 def tile_body(scale, at, diagonal, own, ahead, behind, across, pull, outward):
@@ -179,10 +154,11 @@
     return (inverse * (back - centre - white * along)).astype(BF16)
 
 
-def rows_body(at, near, far, stats, *refs):
+def rows_body(at, raw, stats, *refs):
     pieces, (near_part, far_part, packed) = refs[:4], refs[4:]
-    blocks, rows, half = near.shape
-    width = 2 * half
+    both, rows, width = raw.shape
+    blocks, half = both // 2, width // 2
+    near_at, far_at = at[2] * blocks, (1 - at[2]) * blocks
     cols = pl.ds(pl.multiple_of(at[2] * half, half), half)
     ones = jnp.ones((EXTRA, half), BF16)
     size = jnp.zeros((EXTRA, width), F32)
@@ -196,10 +172,13 @@
             ones, square, CONTRACT_LAST, preferred_element_type=F32
         )
         extra = jnp.broadcast_to(stats[g, 5:6, cols], (EXTRA, half)).astype(BF16)
-        lhs = jnp.concatenate([far[g], extra], axis=0)
+        mean, inverse = stats[g, 1:2, cols], stats[g, 3:4, cols]
+        near = normalise(raw[near_at + g, :, cols], mean, inverse)
+        far = normalise(raw[far_at + g, :, cols], mean, inverse)
+        lhs = jnp.concatenate([far, extra], axis=0)
         far_more = lax.dot_general(lhs, rhs, CONTRACT_LAST, preferred_element_type=F32)
         near_more = lax.dot_general(
-            near[g], rhs, CONTRACT_LAST, preferred_element_type=F32
+            near, rhs, CONTRACT_LAST, preferred_element_type=F32
         )
         if g:
             far_part[: rows + EXTRA] += far_more
@@ -279,7 +258,7 @@
     first_at = jnp.where(c_at == 0, x_at, y_at)
     at = jnp.stack([x_at, y_at, c_at, z_at, first_at]).astype(jnp.int32)
 
-    raw_b = lax.all_gather(view_b, "z", axis=0, tiled=False)
+    raw_b = lax.all_gather(view_b, ("c", "z"), axis=0, tiled=False)
     raw_a = lax.all_gather(view_a, "z", axis=0, tiled=False)
     chip_view = jnp.concatenate([view_b, swap(view_b)], axis=0)
 
@@ -333,9 +312,7 @@
     raw_b, wide_stats, lhs, chip_a, chip_view, vec, diagonal = lax.optimization_barrier(
         (raw_b, wide_stats, lhs, chip_a, chip_view, vec, diagonal)
     )
-    near_b, give = widen(at, wide_stats, raw_b)
-    far_b = swap(give)
-    parts = correlate(near_b, far_b, lhs)
+    parts = correlate(at, wide_stats, raw_b, lhs)
     total = parts[0].astype(F32)
     for step in (1, 3, 2):
         total = total + shift(parts[step], step).astype(F32)
@@ -361,8 +338,7 @@
         [pltpu.VMEM((width, half), BF16)],
         "rows",
         at,
-        near_b,
-        far_b,
+        raw_b,
         wide_stats,
         *row_pieces,
     )

time: 156 us -> 155 us (level)
  starting transfers between devices: 46.1 us -> 41.4 us
    ppermute x8 -> x7, starting transfers between devices: 13.7 us -> 9.72 us  [swap(): return lax.ppermute(value, 'c', [(0, 1), (1, 0)])]
    all_gather x1, waiting for transfers between devices: 3.57 us -> 6.86 us  [local(): raw_b = lax.all_gather(view_b, ('c', 'z'), axis=0, tiled=False)]
    ppermute x8 -> x7, waiting for transfers between devices: 3.98 us -> 1.69 us  [swap(): return lax.ppermute(value, 'c', [(0, 1), (1, 0)])]
    unnamed x17 -> x13, local copies, waits for them, and re-layouts: 2.85 us -> 4.4 us
  transfers between devices with their start and end apart: 25 -> 24, of which waited for: 15 -> 15; matrix products, arithmetic and copies ran while one was open for 6% -> 7% of each run, Pallas kernels for 7% -> 6%
where the time goes in v1:
time: 155 us; the launch traced here: 154 us
  waiting for transfers between devices  71.4 us (46%)
  starting transfers between devices  41.4 us (27%)
  between operations  15 us (10%)
  Pallas kernels  9.8 us (6%)
  other arithmetic  9.46 us (6%)
  local copies, waits for them, and re-layouts  7.04 us (5%)
    ppermute x12, waiting for transfers between devices, shift(): return lax.ppermute(value, ('y', 'x', 'c'), pairs)  47.1 us
    all_to_all x2, waiting for transfers between devices, spread(): return lax.all_to_all(copies, axes, split_axis=0, concat_axis=0, tiled=True)  15 us
    ppermute x12, starting transfers between devices, shift(): return lax.ppermute(value, ('y', 'x', 'c'), pairs)  14 us
    all_to_all x2, starting transfers between devices, spread(): return lax.all_to_all(copies, axes, split_axis=0, concat_axis=0, tiled=True)  13.2 us
    ppermute x7, starting transfers between devices, swap(): return lax.ppermute(value, 'c', [(0, 1), (1, 0)])  9.72 us
    all_gather x1, waiting for transfers between devices, local(): raw_b = lax.all_gather(view_b, ('c', 'z'), axis=0, tiled=False)  6.86 us
    pallas_call x2, Pallas kernels, gradient(): pl.pallas_call(body, in_specs=[SMEM] + [VMEM] * (len(operands) - 1), out_...  5.89 us
    unnamed x13, local copies, waits for them, and re-layouts  4.4 us
  transfers between devices with their start and end apart: 24, of which 15 were waited for; matrix products, arithmetic and copies ran while one was open for 7% of the time, Pallas kernels for 6%

profile of v1, /device:TPU:1, one launch (start us, length us, event | category | flops | bytes accessed | tf_op | source)
XLA Modules:
  0.0 154.0 jit_solution(14167941710232396240)
XLA Ops:
  7.2 0.7 all-gather.5.cloned.1.call-update
  7.9 1.0 convert_reduce_fusion.1
  8.9 1.0 convert_reduce_fusion
  10.0 1.2 fusion.5
  11.2 3.3 %collective-permute-start = (f32[5,512]{1,0:T(8,128)S(1)}, f32[5,512]{1,0:T(8,128)S(1)}, u32[]{:S(2)}, u32[]{:S(2)}) collective-permute-start(f32[5,512]{1,0:T(8,128)S(1)} %stack.40), channel_id=1, source_target_pairs={{0,8},{8,0},{1,9},{9,1},{2,10},{10,2},{3,11},{11,3},{4,12},{12,4},... | collective-permute-start | bytes 30728 | tf_op jit(solution)/shard_map/ppermute | solution.py:36
  14.5 0.8 collective-permute-done
  15.4 0.7 broadcast_in_dim.8
  16.2 5.0 %all-to-all-start = ((f32[16,5,512]{2,1,0:T(8,128)}), f32[16,5,512]{2,1,0:T(8,128)S(1)}, u32[]{:S(2)}, u32[]{:S(2)}) async-start(f32[16,5,512]{2,1,0:T(8,128)} %broadcast_in_dim.8), calls=%async_computation | async-start | bytes 524288 | tf_op jit(solution)/shard_map/all_to_all | solution.py:41
  21.2 0.7 collective-permute-start.2
  22.1 7.3 %all-to-all-done = f32[16,5,512]{2,1,0:T(8,128)S(1)} async-done(((f32[16,5,512]{2,1,0:T(8,128)}), f32[16,5,512]{2,1,0:T(8,128)S(1)}, u32[]{:S(2)}, u32[]{:S(2)}) %all-to-all-start) | async-done | bytes 163872 | tf_op jit(solution)/shard_map/all_to_all | solution.py:41
  29.6 1.0 fusion.11
  30.6 1.6 %collective-permute-start.1 = (bf16[256,512]{1,0:T(8,128)(2,1)S(1)}, bf16[256,512]{1,0:T(8,128)(2,1)S(1)}, u32[]{:S(2)}, u32[]{:S(2)}) collective-permute-start(bf16[256,512]{1,0:T(8,128)(2,1)S(1)} %fusion.11), channel_id=1, source_target_pairs={{0,8},{8,0},{1,9},{9,1},{2,10},{10,2},{3,11},{11,3},{4,12},{12,4},... | collective-permute-start | bytes 786440 | tf_op jit(solution)/shard_map/ppermute | solution.py:36
  32.2 0.7 broadcast_in_dim.9
  32.9 8.2 %all-to-all-start.1 = ((f32[8,6,512]{2,1,0:T(8,128)}), f32[8,6,512]{2,1,0:T(8,128)S(1)}, u32[]{:S(2)}, u32[]{:S(2)}) async-start(f32[8,6,512]{2,1,0:T(8,128)} %broadcast_in_dim.9), calls=%async_computation.1 | async-start | bytes 262144 | tf_op jit(solution)/shard_map/all_to_all | solution.py:41
  41.2 0.6 dynamic_slice.7
  42.7 1.0 fusion.17
  44.0 7.7 %all-to-all-done.1.stats = f32[8,6,512]{2,1,0:T(8,128)S(1)} async-done(((f32[8,6,512]{2,1,0:T(8,128)}), f32[8,6,512]{2,1,0:T(8,128)S(1)}, u32[]{:S(2)}, u32[]{:S(2)}) %all-to-all-start.1) | async-done | bytes 98336 | tf_op jit(solution)/shard_map/all_to_all | solution.py:41
  51.7 6.9 %all-gather.5.cloned.1.call-done = bf16[4096,512]{1,0:T(8,128)(2,1)} async-done(((bf16[256,512]{1,0:T(8,128)(2,1)}), bf16[4096,512]{1,0:T(8,128)(2,1)}) %all-gather.5.cloned.1.call-update) | async-done | bytes 4194320 | tf_op jit(solution)/shard_map/all_gather | solution.py:261
  58.6 2.2 %copy-done = bf16[4096,512]{1,0:T(8,128)(2,1)S(1)} copy-done((bf16[4096,512]{1,0:T(8,128)(2,1)S(1)}, bf16[4096,512]{1,0:T(8,128)(2,1)}, u32[]{:S(2)}) %copy-start) | copy-done | bytes 4194328
  60.8 1.8 %correlate.1 = (bf16[8,128,256]{2,1,0:T(8,128)(2,1)S(1)}, bf16[8,128,256]{2,1,0:T(8,128)(2,1)S(1)}, bf16[8,128,256]{2,1,0:T(8,128)(2,1)S(1)}, bf16[8,128,256]{2,1,0:T(8,128)(2,1)S(1)}) custom-call(s32[5]{0:T(128)S(1)} %stack.47.at, f32[8,6,512]{2,1,0:T(8,128)S(1)} %all-to-all-done.1.stats, bf16[16,256,512]{2,1,0:T(8,128)(2,1)S(1)} %bitcast.46, ...), custom_call_target="tpu_custom_call" | custom-call | flops 1073741824 | bytes 6291456 | tf_op jit(solution)/shard_map/correlate/pallas_call | solution.py:84
  62.6 2.5 %collective-permute-start.5 = (bf16[8,128,256]{2,1,0:T(8,128)(2,1)S(1)}, bf16[8,128,256]{2,1,0:T(8,128)(2,1)S(1)}, u32[]{:S(2)}, u32[]{:S(2)}) collective-permute-start(bf16[8,128,256]{2,1,0:T(8,128)(2,1)S(1)} %get-tuple-element.37), channel_id=1, source_target_pairs={{0,32},{8,136},{16,48},{24,152},{32,0},{40,168},{48,16},{56,184},{... | collective-permute-start | bytes 1572872 | tf_op jit(solution)/shard_map/ppermute | solution.py:32
  65.1 0.9 collective-permute-start.4
  66.5 6.0 %collective-permute-done.5 = bf16[8,128,256]{2,1,0:T(8,128)(2,1)S(1)} collective-permute-done((bf16[8,128,256]{2,1,0:T(8,128)(2,1)S(1)}, bf16[8,128,256]{2,1,0:T(8,128)(2,1)S(1)}, u32[]{:S(2)}, u32[]{:S(2)}) %collective-permute-start.5) | collective-permute-done | bytes 524320 | tf_op jit(solution)/shard_map/ppermute | solution.py:32
  72.6 5.4 %collective-permute-done.4 = bf16[8,128,256]{2,1,0:T(8,128)(2,1)S(1)} collective-permute-done((bf16[8,128,256]{2,1,0:T(8,128)(2,1)S(1)}, bf16[8,128,256]{2,1,0:T(8,128)(2,1)S(1)}, u32[]{:S(2)}, u32[]{:S(2)}) %collective-permute-start.4) | collective-permute-done | bytes 524320 | tf_op jit(solution)/shard_map/ppermute | solution.py:32
  78.5 1.0 collective-permute-start.6
  79.5 1.7 %collective-permute-start.7 = (bf16[8,128,256]{2,1,0:T(8,128)(2,1)S(1)}, bf16[8,128,256]{2,1,0:T(8,128)(2,1)S(1)}, u32[]{:S(2)}, u32[]{:S(2)}) collective-permute-start(bf16[8,128,256]{2,1,0:T(8,128)(2,1)S(1)} %add_convert_fusion.own), channel_id=1, source_target_pairs={{0,192},{8,56},{16,208},{24,8},{32,224},{40,24},{48,240},{56,40},{... | collective-permute-start | bytes 1572872 | tf_op jit(solution)/shard_map/ppermute | solution.py:32
  81.3 1.2 collective-permute-start.8
  82.5 5.8 %collective-permute-done.6.ahead = bf16[8,128,256]{2,1,0:T(8,128)(2,1)S(1)} collective-permute-done((bf16[8,128,256]{2,1,0:T(8,128)(2,1)S(1)}, bf16[8,128,256]{2,1,0:T(8,128)(2,1)S(1)}, u32[]{:S(2)}, u32[]{:S(2)}) %collective-permute-start.6) | collective-permute-done | bytes 524320 | tf_op jit(solution)/shard_map/ppermute | solution.py:32
  88.2 4.8 %collective-permute-done.7.behind = bf16[8,128,256]{2,1,0:T(8,128)(2,1)S(1)} collective-permute-done((bf16[8,128,256]{2,1,0:T(8,128)(2,1)S(1)}, bf16[8,128,256]{2,1,0:T(8,128)(2,1)S(1)}, u32[]{:S(2)}, u32[]{:S(2)}) %collective-permute-start.7) | collective-permute-done | bytes 524320 | tf_op jit(solution)/shard_map/ppermute | solution.py:32
  93.0 1.3 collective-permute-done.8.across
  94.4 2.1 %tile.1 = (bf16[8,128,256]{2,1,0:T(8,128)(2,1)S(1)}, bf16[8,144,256]{2,1,0:T(8,128)(2,1)}) custom-call(s32[5]{0:T(128)S(1)} %stack.47.at, f32[1,128]{1,0:T(1,128)S(1)} %broadcast_in_dim.11.diagonal, bf16[8,128,256]{2,1,0:T(8,128)(2,1)S(1)} %add_convert_fusion.own, bf16[8,128,256]{2,1,0:T(8,128)(2,1)S(1)} %collective-permute-done.6.ahead, ...), custom_call_target="tpu_custom_call" | custom-call | flops 1572864 | bytes 3145728 | tf_op jit(solution)/shard_map/tile/pallas_call | solution.py:126
  96.5 4.4 %all-to-all-start.2 = ((bf16[8,144,256]{2,1,0:T(8,128)(2,1)}), bf16[8,144,256]{2,1,0:T(8,128)(2,1)S(1)}, u32[]{:S(2)}, u32[]{:S(2)}) async-start(bf16[8,144,256]{2,1,0:T(8,128)(2,1)} %get-tuple-element.39), calls=%async_computation.2 | async-start | bytes 1179648 | tf_op jit(solution)/shard_map/all_to_all | solution.py:323
  100.8 2.2 %collective-permute-start.9 = (bf16[8,128,256]{2,1,0:T(8,128)(2,1)S(1)}, bf16[8,128,256]{2,1,0:T(8,128)(2,1)S(1)}, u32[]{:S(2)}, u32[]{:S(2)}) collective-permute-start(bf16[8,128,256]{2,1,0:T(8,128)(2,1)S(1)} %get-tuple-element.40.refs_0_), channel_id=1, source_target_pairs={{0,48},{8,200},{16,0},{24,216},{32,16},{40,232},{48,32},{56,248},{... | collective-permute-start | bytes 1572872 | tf_op jit(solution)/shard_map/ppermute | solution.py:32
  103.0 0.6 collective-permute-start.10
  103.9 10.9 %collective-permute-done.9.refs_1_ = bf16[8,128,256]{2,1,0:T(8,128)(2,1)S(1)} collective-permute-done((bf16[8,128,256]{2,1,0:T(8,128)(2,1)S(1)}, bf16[8,128,256]{2,1,0:T(8,128)(2,1)S(1)}, u32[]{:S(2)}, u32[]{:S(2)}) %collective-permute-start.9) | collective-permute-done | bytes 524320 | tf_op jit(solution)/shard_map/ppermute | solution.py:32
  114.7 3.8 %collective-permute-done.11.refs_3_ = bf16[8,128,256]{2,1,0:T(8,128)(2,1)} collective-permute-done((bf16[8,128,256]{2,1,0:T(8,128)(2,1)S(1)}, bf16[8,128,256]{2,1,0:T(8,128)(2,1)}, u32[]{:S(2)}, u32[]{:S(2)}) %collective-permute-start.11) | collective-permute-done | bytes 524320 | tf_op jit(solution)/shard_map/ppermute | solution.py:32
  118.5 3.4 %collective-permute-start.12 = (bf16[8,256,512]{2,1,0:T(8,128)(2,1)}, bf16[8,256,512]{2,1,0:T(8,128)(2,1)S(1)}, u32[]{:S(2)}, u32[]{:S(2)}) collective-permute-start(bf16[8,256,512]{2,1,0:T(8,128)(2,1)} %bitcast.49), channel_id=1, source_target_pairs={{0,8},{8,0},{1,9},{9,1},{2,10},{10,2},{3,11},{11,3},{4,12},{12,4},... | collective-permute-start | bytes 6291464 | tf_op jit(solution)/shard_map/ppermute | solution.py:36
  122.0 2.4 %collective-permute-start.14 = (bf16[8,144,256]{2,1,0:T(8,128)(2,1)S(1)}, bf16[8,144,256]{2,1,0:T(8,128)(2,1)S(1)}, u32[]{:S(2)}, u32[]{:S(2)}) collective-permute-start(bf16[8,144,256]{2,1,0:T(8,128)(2,1)S(1)} %all-to-all-done.2.refs_0_), channel_id=1, source_target_pairs={{0,48},{8,200},{16,0},{24,216},{32,16},{40,232},{48,32},{56,248},{... | collective-permute-start | bytes 1769480 | tf_op jit(solution)/shard_map/ppermute | solution.py:32
  124.4 0.6 collective-permute-start.15
  125.1 2.2 %copy-done.1 = bf16[4096,512]{1,0:T(8,128)(2,1)S(1)} copy-done((bf16[4096,512]{1,0:T(8,128)(2,1)S(1)}, bf16[4096,512]{1,0:T(8,128)(2,1)}, u32[]{:S(2)}) %copy-start.1) | copy-done | bytes 4194328
  127.3 3.6 %rows.1 = (f32[272,512]{1,0:T(8,128)S(1)}, f32[272,512]{1,0:T(8,128)S(1)}) custom-call(s32[5]{0:T(128)S(1)} %stack.47.at, bf16[16,256,512]{2,1,0:T(8,128)(2,1)S(1)} %bitcast.47, f32[8,6,512]{2,1,0:T(8,128)S(1)} %all-to-all-done.1.stats, bf16[8,128,256]{2,1,0:T(8,128)(2,1)S(1)} %get-tuple-element.40.refs_0_, ...), custom_call_target="tpu_custom_call" | custom-call | flops 1073741824 | bytes 7340032 | tf_op jit(solution)/shard_map/rows/pallas_call | solution.py:237
  130.8 1.1 reduce-precision_convert_fusion
  132.1 5.5 %collective-permute-done.14.refs_1_ = bf16[8,144,256]{2,1,0:T(8,128)(2,1)S(1)} collective-permute-done((bf16[8,144,256]{2,1,0:T(8,128)(2,1)S(1)}, bf16[8,144,256]{2,1,0:T(8,128)(2,1)S(1)}, u32[]{:S(2)}, u32[]{:S(2)}) %collective-permute-start.14) | collective-permute-done | bytes 589856 | tf_op jit(solution)/shard_map/ppermute | solution.py:32
  137.5 3.4 %collective-permute-done.16.refs_3_ = bf16[8,144,256]{2,1,0:T(8,128)(2,1)S(1)} collective-permute-done((bf16[8,144,256]{2,1,0:T(8,128)(2,1)S(1)}, bf16[8,144,256]{2,1,0:T(8,128)(2,1)S(1)}, u32[]{:S(2)}, u32[]{:S(2)}) %collective-permute-start.16) | collective-permute-done | bytes 589856 | tf_op jit(solution)/shard_map/ppermute | solution.py:32
  141.0 2.3 %cols.1 = (bf16[256,256]{1,0:T(8,128)(2,1)S(1)}, bf16[256,256]{1,0:T(8,128)(2,1)S(1)}, f32[1,128]{1,0:T(1,128)S(1)}) custom-call(s32[5]{0:T(128)S(1)} %stack.47.at, bf16[8,256,512]{2,1,0:T(8,128)(2,1)S(1)} %get-tuple-element.73.near, bf16[8,256,512]{2,1,0:T(8,128)(2,1)S(1)} %get-tuple-element.48.far, f32[8,6,512]{2,1,0:T(8,128)S(1)} %all-to-all-done.1.stats, ...), custom_call_target="tpu_custom_call" | custom-call | flops 1073741824 | bytes 7340032 | tf_op jit(solution)/shard_map/cols/pallas_call | solution.py:237
  143.9 0.8 collective-permute-done.18
  145.2 0.8 maximum_select_fusion
  146.2 0.9 fusion.16
  (59 shorter events, 4.0 us)
Async XLA Ops:
  7.2 35.3 %copy-start.3 = (bf16[256,512]{1,0:T(8,128)(2,1)S(1)}, bf16[256,512]{1,0:T(8,128)(2,1)}, u32[]{:S(2)}) copy-start(bf16[256,512]{1,0:T(8,128)(2,1)} %param.3) | copy-start | bytes 786436
  7.2 51.4 %all-gather.5.cloned.1.call-start = ((), (), s32[]{:S(2)}) async-start(), calls=%async_computation.3 | async-start | bytes 4456448 | tf_op jit(solution)/shard_map/all_gather | solution.py:261
  11.2 4.2 %collective-permute-start = (f32[5,512]{1,0:T(8,128)S(1)}, f32[5,512]{1,0:T(8,128)S(1)}, u32[]{:S(2)}, u32[]{:S(2)}) collective-permute-start(f32[5,512]{1,0:T(8,128)S(1)} %stack.40), channel_id=1, source_target_pairs={{0,8},{8,0},{1,9},{9,1},{2,10},{10,2},{3,11},{11,3},{4,12},{12,4},... | collective-permute-start | bytes 30728 | tf_op jit(solution)/shard_map/ppermute | solution.py:36
  16.2 13.2 %all-to-all-start = ((f32[16,5,512]{2,1,0:T(8,128)}), f32[16,5,512]{2,1,0:T(8,128)S(1)}, u32[]{:S(2)}, u32[]{:S(2)}) async-start(f32[16,5,512]{2,1,0:T(8,128)} %broadcast_in_dim.8), calls=%async_computation | async-start | bytes 524288 | tf_op jit(solution)/shard_map/all_to_all | solution.py:41
  21.2 82.7 %all-gather.7.cloned.1.call-start = ((), (), s32[]{:S(2)}) async-start(), calls=%async_computation.4 | async-start | bytes 2359296 | tf_op jit(solution)/shard_map/all_gather | solution.py:262
  21.2 21.2 %collective-permute-start.2 = (bf16[256,512]{1,0:T(8,128)(2,1)}, bf16[256,512]{1,0:T(8,128)(2,1)S(1)}, u32[]{:S(2)}, u32[]{:S(2)}) collective-permute-start(bf16[256,512]{1,0:T(8,128)(2,1)} %param.3), channel_id=1, source_target_pairs={{0,8},{8,0},{1,9},{9,1},{2,10},{10,2},{3,11},{11,3},{4,12},{12,4},... | collective-permute-start | bytes 786440 | tf_op jit(solution)/shard_map/ppermute | solution.py:36
  30.6 11.9 %collective-permute-start.1 = (bf16[256,512]{1,0:T(8,128)(2,1)S(1)}, bf16[256,512]{1,0:T(8,128)(2,1)S(1)}, u32[]{:S(2)}, u32[]{:S(2)}) collective-permute-start(bf16[256,512]{1,0:T(8,128)(2,1)S(1)} %fusion.11), channel_id=1, source_target_pairs={{0,8},{8,0},{1,9},{9,1},{2,10},{10,2},{3,11},{11,3},{4,12},{12,4},... | collective-permute-start | bytes 786440 | tf_op jit(solution)/shard_map/ppermute | solution.py:36
  32.9 18.9 %all-to-all-start.1 = ((f32[8,6,512]{2,1,0:T(8,128)}), f32[8,6,512]{2,1,0:T(8,128)S(1)}, u32[]{:S(2)}, u32[]{:S(2)}) async-start(f32[8,6,512]{2,1,0:T(8,128)} %broadcast_in_dim.9), calls=%async_computation.1 | async-start | bytes 262144 | tf_op jit(solution)/shard_map/all_to_all | solution.py:41
  58.6 2.2 %copy-start = (bf16[4096,512]{1,0:T(8,128)(2,1)S(1)}, bf16[4096,512]{1,0:T(8,128)(2,1)}, u32[]{:S(2)}) copy-start(bf16[4096,512]{1,0:T(8,128)(2,1)} %all-gather.5.cloned.1.call-done) | copy-start | bytes 12582916
  62.6 10.0 %collective-permute-start.5 = (bf16[8,128,256]{2,1,0:T(8,128)(2,1)S(1)}, bf16[8,128,256]{2,1,0:T(8,128)(2,1)S(1)}, u32[]{:S(2)}, u32[]{:S(2)}) collective-permute-start(bf16[8,128,256]{2,1,0:T(8,128)(2,1)S(1)} %get-tuple-element.37), channel_id=1, source_target_pairs={{0,32},{8,136},{16,48},{24,152},{32,0},{40,168},{48,16},{56,184},{... | collective-permute-start | bytes 1572872 | tf_op jit(solution)/shard_map/ppermute | solution.py:32
  65.1 12.9 %collective-permute-start.4 = (bf16[8,128,256]{2,1,0:T(8,128)(2,1)S(1)}, bf16[8,128,256]{2,1,0:T(8,128)(2,1)S(1)}, u32[]{:S(2)}, u32[]{:S(2)}) collective-permute-start(bf16[8,128,256]{2,1,0:T(8,128)(2,1)S(1)} %get-tuple-element.36), channel_id=1, source_target_pairs={{0,48},{8,200},{16,0},{24,216},{32,16},{40,232},{48,32},{56,248},{... | collective-permute-start | bytes 1572872 | tf_op jit(solution)/shard_map/ppermute | solution.py:32
  66.0 12.3 %collective-permute-start.3 = (bf16[8,128,256]{2,1,0:T(8,128)(2,1)S(1)}, bf16[8,128,256]{2,1,0:T(8,128)(2,1)S(1)}, u32[]{:S(2)}, u32[]{:S(2)}) collective-permute-start(bf16[8,128,256]{2,1,0:T(8,128)(2,1)S(1)} %get-tuple-element.35), channel_id=1, source_target_pairs={{0,16},{8,72},{16,32},{24,88},{32,48},{40,104},{48,0},{56,120},{64... | collective-permute-start | bytes 1572872 | tf_op jit(solution)/shard_map/ppermute | solution.py:32
  78.5 9.7 %collective-permute-start.6 = (bf16[8,128,256]{2,1,0:T(8,128)(2,1)S(1)}, bf16[8,128,256]{2,1,0:T(8,128)(2,1)S(1)}, u32[]{:S(2)}, u32[]{:S(2)}) collective-permute-start(bf16[8,128,256]{2,1,0:T(8,128)(2,1)S(1)} %add_convert_fusion.own), channel_id=1, source_target_pairs={{0,64},{8,24},{16,80},{24,40},{32,96},{40,56},{48,112},{56,8},{64,... | collective-permute-start | bytes 1572872 | tf_op jit(solution)/shard_map/ppermute | solution.py:32
  79.5 13.5 %collective-permute-start.7 = (bf16[8,128,256]{2,1,0:T(8,128)(2,1)S(1)}, bf16[8,128,256]{2,1,0:T(8,128)(2,1)S(1)}, u32[]{:S(2)}, u32[]{:S(2)}) collective-permute-start(bf16[8,128,256]{2,1,0:T(8,128)(2,1)S(1)} %add_convert_fusion.own), channel_id=1, source_target_pairs={{0,192},{8,56},{16,208},{24,8},{32,224},{40,24},{48,240},{56,40},{... | collective-permute-start | bytes 1572872 | tf_op jit(solution)/shard_map/ppermute | solution.py:32
  81.3 13.1 %collective-permute-start.8 = (bf16[8,128,256]{2,1,0:T(8,128)(2,1)S(1)}, bf16[8,128,256]{2,1,0:T(8,128)(2,1)S(1)}, u32[]{:S(2)}, u32[]{:S(2)}) collective-permute-start(bf16[8,128,256]{2,1,0:T(8,128)(2,1)S(1)} %add_convert_fusion.own), channel_id=1, source_target_pairs={{0,128},{8,40},{16,144},{24,56},{32,160},{40,8},{48,176},{56,24},{... | collective-permute-start | bytes 1572872 | tf_op jit(solution)/shard_map/ppermute | solution.py:32
  96.5 22.1 %all-to-all-start.2 = ((bf16[8,144,256]{2,1,0:T(8,128)(2,1)}), bf16[8,144,256]{2,1,0:T(8,128)(2,1)S(1)}, u32[]{:S(2)}, u32[]{:S(2)}) async-start(bf16[8,144,256]{2,1,0:T(8,128)(2,1)} %get-tuple-element.39), calls=%async_computation.2 | async-start | bytes 1179648 | tf_op jit(solution)/shard_map/all_to_all | solution.py:323
  100.8 13.9 %collective-permute-start.9 = (bf16[8,128,256]{2,1,0:T(8,128)(2,1)S(1)}, bf16[8,128,256]{2,1,0:T(8,128)(2,1)S(1)}, u32[]{:S(2)}, u32[]{:S(2)}) collective-permute-start(bf16[8,128,256]{2,1,0:T(8,128)(2,1)S(1)} %get-tuple-element.40.refs_0_), channel_id=1, source_target_pairs={{0,48},{8,200},{16,0},{24,216},{32,16},{40,232},{48,32},{56,248},{... | collective-permute-start | bytes 1572872 | tf_op jit(solution)/shard_map/ppermute | solution.py:32
  103.0 11.7 %collective-permute-start.10 = (bf16[8,128,256]{2,1,0:T(8,128)(2,1)S(1)}, bf16[8,128,256]{2,1,0:T(8,128)(2,1)S(1)}, u32[]{:S(2)}, u32[]{:S(2)}) collective-permute-start(bf16[8,128,256]{2,1,0:T(8,128)(2,1)S(1)} %get-tuple-element.40.refs_0_), channel_id=1, source_target_pairs={{0,32},{8,136},{16,48},{24,152},{32,0},{40,168},{48,16},{56,184},{... | collective-permute-start | bytes 1572872 | tf_op jit(solution)/shard_map/ppermute | solution.py:32
  103.6 15.0 %collective-permute-start.11 = (bf16[8,128,256]{2,1,0:T(8,128)(2,1)S(1)}, bf16[8,128,256]{2,1,0:T(8,128)(2,1)}, u32[]{:S(2)}, u32[]{:S(2)}) collective-permute-start(bf16[8,128,256]{2,1,0:T(8,128)(2,1)S(1)} %get-tuple-element.40.refs_0_), channel_id=1, source_target_pairs={{0,16},{8,72},{16,32},{24,88},{32,48},{40,104},{48,0},{56,120},{64... | collective-permute-start | bytes 1572872 | tf_op jit(solution)/shard_map/ppermute | solution.py:32
  118.5 12.3 %collective-permute-start.12 = (bf16[8,256,512]{2,1,0:T(8,128)(2,1)}, bf16[8,256,512]{2,1,0:T(8,128)(2,1)S(1)}, u32[]{:S(2)}, u32[]{:S(2)}) collective-permute-start(bf16[8,256,512]{2,1,0:T(8,128)(2,1)} %bitcast.49), channel_id=1, source_target_pairs={{0,8},{8,0},{1,9},{9,1},{2,10},{10,2},{3,11},{11,3},{4,12},{12,4},... | collective-permute-start | bytes 6291464 | tf_op jit(solution)/shard_map/ppermute | solution.py:36
  122.0 15.5 %collective-permute-start.14 = (bf16[8,144,256]{2,1,0:T(8,128)(2,1)S(1)}, bf16[8,144,256]{2,1,0:T(8,128)(2,1)S(1)}, u32[]{:S(2)}, u32[]{:S(2)}) collective-permute-start(bf16[8,144,256]{2,1,0:T(8,128)(2,1)S(1)} %all-to-all-done.2.refs_0_), channel_id=1, source_target_pairs={{0,48},{8,200},{16,0},{24,216},{32,16},{40,232},{48,32},{56,248},{... | collective-permute-start | bytes 1769480 | tf_op jit(solution)/shard_map/ppermute | solution.py:32
  124.4 13.2 %collective-permute-start.15 = (bf16[8,144,256]{2,1,0:T(8,128)(2,1)S(1)}, bf16[8,144,256]{2,1,0:T(8,128)(2,1)S(1)}, u32[]{:S(2)}, u32[]{:S(2)}) collective-permute-start(bf16[8,144,256]{2,1,0:T(8,128)(2,1)S(1)} %all-to-all-done.2.refs_0_), channel_id=1, source_target_pairs={{0,32},{8,136},{16,48},{24,152},{32,0},{40,168},{48,16},{56,184},{... | collective-permute-start | bytes 1769480 | tf_op jit(solution)/shard_map/ppermute | solution.py:32
  125.0 15.9 %collective-permute-start.16 = (bf16[8,144,256]{2,1,0:T(8,128)(2,1)S(1)}, bf16[8,144,256]{2,1,0:T(8,128)(2,1)S(1)}, u32[]{:S(2)}, u32[]{:S(2)}) collective-permute-start(bf16[8,144,256]{2,1,0:T(8,128)(2,1)S(1)} %all-to-all-done.2.refs_0_), channel_id=1, source_target_pairs={{0,16},{8,72},{16,32},{24,88},{32,48},{40,104},{48,0},{56,120},{64... | collective-permute-start | bytes 1769480 | tf_op jit(solution)/shard_map/ppermute | solution.py:32
  125.1 2.2 %copy-start.1 = (bf16[4096,512]{1,0:T(8,128)(2,1)S(1)}, bf16[4096,512]{1,0:T(8,128)(2,1)}, u32[]{:S(2)}) copy-start(bf16[4096,512]{1,0:T(8,128)(2,1)} %all-gather.5.cloned.1.call-done) | copy-start | bytes 12582916
  127.3 3.6 %copy-start.5 = (bf16[2048,512]{1,0:T(8,128)(2,1)S(1)}, bf16[2048,512]{1,0:T(8,128)(2,1)}, u32[]{:S(2)}) copy-start(bf16[2048,512]{1,0:T(8,128)(2,1)} %all-gather.7.cloned.1.call-done) | copy-start | bytes 6291460
  132.0 14.1 %collective-permute-start.13 = (f32[272,512]{1,0:T(8,128)S(1)}, f32[272,512]{1,0:T(8,128)S(1)}, u32[]{:S(2)}, u32[]{:S(2)}) collective-permute-start(f32[272,512]{1,0:T(8,128)S(1)} %get-tuple-element.47), channel_id=1, source_target_pairs={{0,8},{8,0},{1,9},{9,1},{2,10},{10,2},{3,11},{11,3},{4,12},{12,4},... | collective-permute-start | bytes 1671176 | tf_op jit(solution)/shard_map/ppermute | solution.py:36
  140.9 5.2 %copy-start.2 = (bf16[256,512]{1,0:T(8,128)(2,1)S(1)}, bf16[256,512]{1,0:T(8,128)(2,1)}, u32[]{:S(2)}) copy-start(bf16[256,512]{1,0:T(8,128)(2,1)} %param.2) | copy-start | bytes 786436
  141.0 5.3 %copy-start.4 = (bf16[256,512]{1,0:T(8,128)(2,1)S(1)}, bf16[256,512]{1,0:T(8,128)(2,1)}, u32[]{:S(2)}) copy-start(bf16[256,512]{1,0:T(8,128)(2,1)} %param.3) | copy-start | bytes 786436
  143.3 2.0 %collective-permute-start.17 = (bf16[256,256]{1,0:T(8,128)(2,1)S(1)}, bf16[256,256]{1,0:T(8,128)(2,1)S(1)}, u32[]{:S(2)}, u32[]{:S(2)}) collective-permute-start(bf16[256,256]{1,0:T(8,128)(2,1)S(1)} %get-tuple-element.53), channel_id=1, source_target_pairs={{0,8},{8,0},{1,9},{9,1},{2,10},{10,2},{3,11},{11,3},{4,12},{12,4},... | collective-permute-start | bytes 393224 | tf_op jit(solution)/shard_map/ppermute | solution.py:36
  143.4 1.3 collective-permute-start.18
Sparse Core Ops, SparseCore 0:
  9.8 48.7 all-gather.4
  60.4 35.5 all-gather.6

commit v2 on v1

--- a/solution.py
+++ b/solution.py
@@ -248,6 +248,44 @@
     )(*operands)
 
 
+def join_body(
+    images, at, near, other, loss, other_loss, near_part, far_part, view, norm, vec, grad_a, grad_b, total
+):
+    rows, half = near.shape
+    for which, value in enumerate((near, other)):
+        spot = (1 - at[2] if which else at[2]) * half
+        grad_b[:, pl.ds(pl.multiple_of(spot, half), half)] = value[...]
+    total[...] = loss[...] + other_loss[...]
+    ends = near_part[rows:] + far_part[rows:]
+    for line in range(0, rows, 64):
+        lines = slice(line, line + 64)
+        grad_a[lines] = finish(
+            view[lines],
+            norm[lines],
+            vec,
+            near_part[lines] + far_part[lines],
+            ends[0:1],
+            ends[8:9],
+            0,
+            7,
+            images,
+        )
+
+
+def join(images, at, near, *operands):
+    rows, half = near.shape
+    grad = jax.ShapeDtypeStruct((rows, 2 * half), BF16)
+    return pl.pallas_call(
+        functools.partial(join_body, images),
+        in_specs=[SMEM] + [VMEM] * (1 + len(operands)),
+        out_specs=[VMEM] * 3,
+        out_shape=[grad, grad, jax.ShapeDtypeStruct((1, 128), F32)],
+        compiler_params=pltpu.CompilerParams(vmem_limit_bytes=6 * MIB),
+        cost_estimate=pl.CostEstimate(flops=MIB, bytes_accessed=2 * MIB, transcendentals=0),
+        name="join",
+    )(at, near, *operands)
+
+
 def local(view_a, view_b):
     rows, width = view_a.shape
     chips = lax.axis_size("y") * lax.axis_size("x")
@@ -343,18 +381,6 @@
         *row_pieces,
     )
     far_a, far_part = lax.optimization_barrier((far_a, far_part))
-    near_part = near_part + swap(far_part)
-    grad_a = finish(
-        view_a,
-        norm_b,
-        vec,
-        near_part[:rows],
-        near_part[rows : rows + 1],
-        near_part[rows + 8 : rows + 9],
-        0,
-        7,
-        images,
-    )
     near_grad, far_grad, loss = gradient(
         functools.partial(cols_body, images),
         [jax.ShapeDtypeStruct((rows, half), BF16)] * 2 + [jax.ShapeDtypeStruct((1, 128), F32)],
@@ -369,13 +395,20 @@
         vec,
         *col_pieces,
     )
-    loss_value = (loss + swap(loss))[0, 0]
-    other_grad = swap(far_grad)
-    grad_b = jnp.where(
-        c_at == 0,
-        jnp.concatenate([near_grad, other_grad], axis=1),
-        jnp.concatenate([other_grad, near_grad], axis=1),
-    )
+    grad_a, grad_b, total_loss = join(
+        images,
+        at,
+        near_grad,
+        swap(far_grad),
+        loss,
+        swap(loss),
+        near_part,
+        swap(far_part),
+        view_a,
+        norm_b,
+        vec,
+    )
+    loss_value = total_loss[0, 0]
     return (grad_a, grad_b, loss_value)
 
 

time: 155 us -> 154 us (level)
  other arithmetic: 9.46 us -> 7.13 us
    ppermute x12, waiting for transfers between devices: 47.1 us -> 44.7 us  [shift(): return lax.ppermute(value, ('y', 'x', 'c'), pairs)]
  transfers between devices with their start and end apart: 24 -> 24, of which waited for: 15 -> 16; matrix products, arithmetic and copies ran while one was open for 7% -> 6% of each run, Pallas kernels for 6% -> 6%
where the time goes in v2:
time: 154 us; the launch traced here: 153 us
  waiting for transfers between devices  70.6 us (46%)
  starting transfers between devices  42.2 us (27%)
  between operations  14.9 us (10%)
  Pallas kernels  11.3 us (7%)
  other arithmetic  7.13 us (5%)
  local copies, waits for them, and re-layouts  7.04 us (5%)
    ppermute x12, waiting for transfers between devices, shift(): return lax.ppermute(value, ('y', 'x', 'c'), pairs)  44.7 us
    all_to_all x2, waiting for transfers between devices, spread(): return lax.all_to_all(copies, axes, split_axis=0, concat_axis=0, tiled=True)  15 us
    ppermute x12, starting transfers between devices, shift(): return lax.ppermute(value, ('y', 'x', 'c'), pairs)  13.9 us
    all_to_all x2, starting transfers between devices, spread(): return lax.all_to_all(copies, axes, split_axis=0, concat_axis=0, tiled=True)  13.2 us
    ppermute x7, starting transfers between devices, swap(): return lax.ppermute(value, 'c', [(0, 1), (1, 0)])  10.7 us
    all_gather x1, waiting for transfers between devices, local(): raw_b = lax.all_gather(view_b, ('c', 'z'), axis=0, tiled=False)  6.87 us
    pallas_call x2, Pallas kernels, gradient(): pl.pallas_call(body, in_specs=[SMEM] + [VMEM] * (len(operands) - 1), out_...  5.9 us
    unnamed x13, local copies, waits for them, and re-layouts  4.4 us
  transfers between devices with their start and end apart: 24, of which 16 were waited for; matrix products, arithmetic and copies ran while one was open for 6% of the time, Pallas kernels for 6%

profile of v2, /device:TPU:1, one launch (start us, length us, event | category | flops | bytes accessed | tf_op | source)
XLA Modules:
  0.0 153.2 jit_solution(15812992175944368068)
XLA Ops:
  7.2 0.7 all-gather.5.cloned.1.call-update
  7.9 1.0 convert_reduce_fusion
  8.9 1.0 convert_reduce_fusion.1
  10.0 1.2 fusion.5
  11.2 3.3 %collective-permute-start = (f32[5,512]{1,0:T(8,128)S(1)}, f32[5,512]{1,0:T(8,128)S(1)}, u32[]{:S(2)}, u32[]{:S(2)}) collective-permute-start(f32[5,512]{1,0:T(8,128)S(1)} %stack.46), channel_id=1, source_target_pairs={{0,8},{8,0},{1,9},{9,1},{2,10},{10,2},{3,11},{11,3},{4,12},{12,4},... | collective-permute-start | bytes 30728 | tf_op jit(solution)/shard_map/ppermute | solution.py:36
  14.5 0.8 collective-permute-done
  15.4 0.7 broadcast_in_dim.8
  16.2 5.0 %all-to-all-start = ((f32[16,5,512]{2,1,0:T(8,128)}), f32[16,5,512]{2,1,0:T(8,128)S(1)}, u32[]{:S(2)}, u32[]{:S(2)}) async-start(f32[16,5,512]{2,1,0:T(8,128)} %broadcast_in_dim.8), calls=%async_computation | async-start | bytes 524288 | tf_op jit(solution)/shard_map/all_to_all | solution.py:41
  21.2 0.7 collective-permute-start.2
  22.1 7.3 %all-to-all-done = f32[16,5,512]{2,1,0:T(8,128)S(1)} async-done(((f32[16,5,512]{2,1,0:T(8,128)}), f32[16,5,512]{2,1,0:T(8,128)S(1)}, u32[]{:S(2)}, u32[]{:S(2)}) %all-to-all-start) | async-done | bytes 163872 | tf_op jit(solution)/shard_map/all_to_all | solution.py:41
  29.6 1.0 fusion.8
  30.6 1.6 %collective-permute-start.1 = (bf16[256,512]{1,0:T(8,128)(2,1)S(1)}, bf16[256,512]{1,0:T(8,128)(2,1)S(1)}, u32[]{:S(2)}, u32[]{:S(2)}) collective-permute-start(bf16[256,512]{1,0:T(8,128)(2,1)S(1)} %fusion.8), channel_id=1, source_target_pairs={{0,8},{8,0},{1,9},{9,1},{2,10},{10,2},{3,11},{11,3},{4,12},{12,4},... | collective-permute-start | bytes 786440 | tf_op jit(solution)/shard_map/ppermute | solution.py:36
  32.9 8.2 %all-to-all-start.1 = ((f32[8,6,512]{2,1,0:T(8,128)}), f32[8,6,512]{2,1,0:T(8,128)S(1)}, u32[]{:S(2)}, u32[]{:S(2)}) async-start(f32[8,6,512]{2,1,0:T(8,128)} %broadcast_in_dim.9), calls=%async_computation.1 | async-start | bytes 262144 | tf_op jit(solution)/shard_map/all_to_all | solution.py:41
  42.7 1.0 fusion.12
  44.0 7.7 %all-to-all-done.1.stats = f32[8,6,512]{2,1,0:T(8,128)S(1)} async-done(((f32[8,6,512]{2,1,0:T(8,128)}), f32[8,6,512]{2,1,0:T(8,128)S(1)}, u32[]{:S(2)}, u32[]{:S(2)}) %all-to-all-start.1) | async-done | bytes 98336 | tf_op jit(solution)/shard_map/all_to_all | solution.py:41
  51.7 6.9 %all-gather.5.cloned.1.call-done = bf16[4096,512]{1,0:T(8,128)(2,1)} async-done(((bf16[256,512]{1,0:T(8,128)(2,1)}), bf16[4096,512]{1,0:T(8,128)(2,1)}) %all-gather.5.cloned.1.call-update) | async-done | bytes 4194320 | tf_op jit(solution)/shard_map/all_gather | solution.py:299
  58.6 2.2 %copy-done = bf16[4096,512]{1,0:T(8,128)(2,1)S(1)} copy-done((bf16[4096,512]{1,0:T(8,128)(2,1)S(1)}, bf16[4096,512]{1,0:T(8,128)(2,1)}, u32[]{:S(2)}) %copy-start) | copy-done | bytes 4194328
  60.8 1.8 %correlate.1 = (bf16[8,128,256]{2,1,0:T(8,128)(2,1)S(1)}, bf16[8,128,256]{2,1,0:T(8,128)(2,1)S(1)}, bf16[8,128,256]{2,1,0:T(8,128)(2,1)S(1)}, bf16[8,128,256]{2,1,0:T(8,128)(2,1)S(1)}) custom-call(s32[5]{0:T(128)S(1)} %stack.41.at, f32[8,6,512]{2,1,0:T(8,128)S(1)} %all-to-all-done.1.stats, bf16[16,256,512]{2,1,0:T(8,128)(2,1)S(1)} %bitcast.41, ...), custom_call_target="tpu_custom_call" | custom-call | flops 1073741824 | bytes 6291456 | tf_op jit(solution)/shard_map/correlate/pallas_call | solution.py:84
  62.6 1.0 collective-permute-start.3
  63.6 1.8 %collective-permute-start.4 = (bf16[8,128,256]{2,1,0:T(8,128)(2,1)S(1)}, bf16[8,128,256]{2,1,0:T(8,128)(2,1)S(1)}, u32[]{:S(2)}, u32[]{:S(2)}) collective-permute-start(bf16[8,128,256]{2,1,0:T(8,128)(2,1)S(1)} %get-tuple-element.38), channel_id=1, source_target_pairs={{0,48},{8,200},{16,0},{24,216},{32,16},{40,232},{48,32},{56,248},{... | collective-permute-start | bytes 1572872 | tf_op jit(solution)/shard_map/ppermute | solution.py:32
  65.4 1.2 collective-permute-start.5
  66.5 5.7 %collective-permute-done.3 = bf16[8,128,256]{2,1,0:T(8,128)(2,1)S(1)} collective-permute-done((bf16[8,128,256]{2,1,0:T(8,128)(2,1)S(1)}, bf16[8,128,256]{2,1,0:T(8,128)(2,1)S(1)}, u32[]{:S(2)}, u32[]{:S(2)}) %collective-permute-start.3) | collective-permute-done | bytes 524320 | tf_op jit(solution)/shard_map/ppermute | solution.py:32
  72.2 4.9 %collective-permute-done.4 = bf16[8,128,256]{2,1,0:T(8,128)(2,1)S(1)} collective-permute-done((bf16[8,128,256]{2,1,0:T(8,128)(2,1)S(1)}, bf16[8,128,256]{2,1,0:T(8,128)(2,1)S(1)}, u32[]{:S(2)}, u32[]{:S(2)}) %collective-permute-start.4) | collective-permute-done | bytes 524320 | tf_op jit(solution)/shard_map/ppermute | solution.py:32
  77.1 1.3 collective-permute-done.5
  78.7 1.0 collective-permute-start.6
  79.7 1.8 %collective-permute-start.7 = (bf16[8,128,256]{2,1,0:T(8,128)(2,1)S(1)}, bf16[8,128,256]{2,1,0:T(8,128)(2,1)S(1)}, u32[]{:S(2)}, u32[]{:S(2)}) collective-permute-start(bf16[8,128,256]{2,1,0:T(8,128)(2,1)S(1)} %add_convert_fusion.own), channel_id=1, source_target_pairs={{0,192},{8,56},{16,208},{24,8},{32,224},{40,24},{48,240},{56,40},{... | collective-permute-start | bytes 1572872 | tf_op jit(solution)/shard_map/ppermute | solution.py:32
  81.5 1.2 collective-permute-start.8
  82.7 5.8 %collective-permute-done.6.ahead = bf16[8,128,256]{2,1,0:T(8,128)(2,1)S(1)} collective-permute-done((bf16[8,128,256]{2,1,0:T(8,128)(2,1)S(1)}, bf16[8,128,256]{2,1,0:T(8,128)(2,1)S(1)}, u32[]{:S(2)}, u32[]{:S(2)}) %collective-permute-start.6) | collective-permute-done | bytes 524320 | tf_op jit(solution)/shard_map/ppermute | solution.py:32
  88.4 4.8 %collective-permute-done.7.behind = bf16[8,128,256]{2,1,0:T(8,128)(2,1)S(1)} collective-permute-done((bf16[8,128,256]{2,1,0:T(8,128)(2,1)S(1)}, bf16[8,128,256]{2,1,0:T(8,128)(2,1)S(1)}, u32[]{:S(2)}, u32[]{:S(2)}) %collective-permute-start.7) | collective-permute-done | bytes 524320 | tf_op jit(solution)/shard_map/ppermute | solution.py:32
  93.2 1.6 %collective-permute-done.8.across = bf16[8,128,256]{2,1,0:T(8,128)(2,1)S(1)} collective-permute-done((bf16[8,128,256]{2,1,0:T(8,128)(2,1)S(1)}, bf16[8,128,256]{2,1,0:T(8,128)(2,1)S(1)}, u32[]{:S(2)}, u32[]{:S(2)}) %collective-permute-start.8) | collective-permute-done | bytes 524320 | tf_op jit(solution)/shard_map/ppermute | solution.py:32
  94.8 2.1 %tile.1 = (bf16[8,128,256]{2,1,0:T(8,128)(2,1)S(1)}, bf16[8,144,256]{2,1,0:T(8,128)(2,1)}) custom-call(s32[5]{0:T(128)S(1)} %stack.41.at, f32[1,128]{1,0:T(1,128)S(1)} %broadcast_in_dim.11.diagonal, bf16[8,128,256]{2,1,0:T(8,128)(2,1)S(1)} %add_convert_fusion.own, bf16[8,128,256]{2,1,0:T(8,128)(2,1)S(1)} %collective-permute-done.6.ahead, ...), custom_call_target="tpu_custom_call" | custom-call | flops 1572864 | bytes 3145728 | tf_op jit(solution)/shard_map/tile/pallas_call | solution.py:126
  96.9 4.3 %all-to-all-start.2 = ((bf16[8,144,256]{2,1,0:T(8,128)(2,1)}), bf16[8,144,256]{2,1,0:T(8,128)(2,1)S(1)}, u32[]{:S(2)}, u32[]{:S(2)}) async-start(bf16[8,144,256]{2,1,0:T(8,128)(2,1)} %get-tuple-element.41), calls=%async_computation.2 | async-start | bytes 1179648 | tf_op jit(solution)/shard_map/all_to_all | solution.py:361
  101.8 2.0 %collective-permute-start.11 = (bf16[8,128,256]{2,1,0:T(8,128)(2,1)S(1)}, bf16[8,128,256]{2,1,0:T(8,128)(2,1)S(1)}, u32[]{:S(2)}, u32[]{:S(2)}) collective-permute-start(bf16[8,128,256]{2,1,0:T(8,128)(2,1)S(1)} %get-tuple-element.43.refs_0_), channel_id=1, source_target_pairs={{0,16},{8,72},{16,32},{24,88},{32,48},{40,104},{48,0},{56,120},{64... | collective-permute-start | bytes 1572872 | tf_op jit(solution)/shard_map/ppermute | solution.py:32
  104.5 6.6 %collective-permute-done.10.refs_2_ = bf16[8,128,256]{2,1,0:T(8,128)(2,1)S(1)} collective-permute-done((bf16[8,128,256]{2,1,0:T(8,128)(2,1)S(1)}, bf16[8,128,256]{2,1,0:T(8,128)(2,1)S(1)}, u32[]{:S(2)}, u32[]{:S(2)}) %collective-permute-start.10) | collective-permute-done | bytes 524320 | tf_op jit(solution)/shard_map/ppermute | solution.py:32
  111.1 5.6 %collective-permute-done.11.refs_3_ = bf16[8,128,256]{2,1,0:T(8,128)(2,1)S(1)} collective-permute-done((bf16[8,128,256]{2,1,0:T(8,128)(2,1)S(1)}, bf16[8,128,256]{2,1,0:T(8,128)(2,1)S(1)}, u32[]{:S(2)}, u32[]{:S(2)}) %collective-permute-start.11) | collective-permute-done | bytes 524320 | tf_op jit(solution)/shard_map/ppermute | solution.py:32
  116.6 1.5 all-to-all-done.2.refs_0_
  118.2 2.9 %collective-permute-start.12 = (bf16[8,256,512]{2,1,0:T(8,128)(2,1)}, bf16[8,256,512]{2,1,0:T(8,128)(2,1)S(1)}, u32[]{:S(2)}, u32[]{:S(2)}) collective-permute-start(bf16[8,256,512]{2,1,0:T(8,128)(2,1)} %bitcast.44), channel_id=1, source_target_pairs={{0,8},{8,0},{1,9},{9,1},{2,10},{10,2},{3,11},{11,3},{4,12},{12,4},... | collective-permute-start | bytes 6291464 | tf_op jit(solution)/shard_map/ppermute | solution.py:36
  121.1 2.1 %collective-permute-start.13 = (bf16[8,144,256]{2,1,0:T(8,128)(2,1)S(1)}, bf16[8,144,256]{2,1,0:T(8,128)(2,1)S(1)}, u32[]{:S(2)}, u32[]{:S(2)}) collective-permute-start(bf16[8,144,256]{2,1,0:T(8,128)(2,1)S(1)} %all-to-all-done.2.refs_0_), channel_id=1, source_target_pairs={{0,48},{8,200},{16,0},{24,216},{32,16},{40,232},{48,32},{56,248},{... | collective-permute-start | bytes 1769480 | tf_op jit(solution)/shard_map/ppermute | solution.py:32
  123.9 2.2 %copy-done.1 = bf16[4096,512]{1,0:T(8,128)(2,1)S(1)} copy-done((bf16[4096,512]{1,0:T(8,128)(2,1)S(1)}, bf16[4096,512]{1,0:T(8,128)(2,1)}, u32[]{:S(2)}) %copy-start.1) | copy-done | bytes 4194328
  126.1 3.6 %rows.1 = (f32[272,512]{1,0:T(8,128)S(1)}, f32[272,512]{1,0:T(8,128)S(1)}) custom-call(s32[5]{0:T(128)S(1)} %stack.41.at, bf16[16,256,512]{2,1,0:T(8,128)(2,1)S(1)} %bitcast.42, f32[8,6,512]{2,1,0:T(8,128)S(1)} %all-to-all-done.1.stats, bf16[8,128,256]{2,1,0:T(8,128)(2,1)S(1)} %get-tuple-element.43.refs_0_, ...), custom_call_target="tpu_custom_call" | custom-call | flops 1073741824 | bytes 7340032 | tf_op jit(solution)/shard_map/rows/pallas_call | solution.py:237
  129.7 1.1 reduce-precision_convert_fusion
  130.8 0.8 collective-permute-start.18
  131.5 4.8 %collective-permute-done.13.refs_1_ = bf16[8,144,256]{2,1,0:T(8,128)(2,1)S(1)} collective-permute-done((bf16[8,144,256]{2,1,0:T(8,128)(2,1)S(1)}, bf16[8,144,256]{2,1,0:T(8,128)(2,1)S(1)}, u32[]{:S(2)}, u32[]{:S(2)}) %collective-permute-start.13) | collective-permute-done | bytes 589856 | tf_op jit(solution)/shard_map/ppermute | solution.py:32
  136.3 3.7 %collective-permute-done.15.refs_3_ = bf16[8,144,256]{2,1,0:T(8,128)(2,1)S(1)} collective-permute-done((bf16[8,144,256]{2,1,0:T(8,128)(2,1)S(1)}, bf16[8,144,256]{2,1,0:T(8,128)(2,1)S(1)}, u32[]{:S(2)}, u32[]{:S(2)}) %collective-permute-start.15) | collective-permute-done | bytes 589856 | tf_op jit(solution)/shard_map/ppermute | solution.py:32
  140.0 2.3 %cols.1 = (bf16[256,256]{1,0:T(8,128)(2,1)S(1)}, bf16[256,256]{1,0:T(8,128)(2,1)S(1)}, f32[1,128]{1,0:T(1,128)S(1)}) custom-call(s32[5]{0:T(128)S(1)} %stack.41.at, bf16[8,256,512]{2,1,0:T(8,128)(2,1)S(1)} %get-tuple-element.78.near, bf16[8,256,512]{2,1,0:T(8,128)(2,1)S(1)} %get-tuple-element.48.far, f32[8,6,512]{2,1,0:T(8,128)S(1)} %all-to-all-done.1.stats, ...), custom_call_target="tpu_custom_call" | custom-call | flops 1073741824 | bytes 7340032 | tf_op jit(solution)/shard_map/cols/pallas_call | solution.py:237
  142.4 1.4 collective-permute-start.16
  143.9 1.0 collective-permute-done.17.other_loss
  144.9 1.5 join.1
  (56 shorter events, 4.9 us)
Async XLA Ops:
  7.2 35.3 %copy-start.3 = (bf16[256,512]{1,0:T(8,128)(2,1)S(1)}, bf16[256,512]{1,0:T(8,128)(2,1)}, u32[]{:S(2)}) copy-start(bf16[256,512]{1,0:T(8,128)(2,1)} %param.3) | copy-start | bytes 786436
  7.2 51.4 %all-gather.5.cloned.1.call-start = ((), (), s32[]{:S(2)}) async-start(), calls=%async_computation.3 | async-start | bytes 4456448 | tf_op jit(solution)/shard_map/all_gather | solution.py:299
  11.2 4.2 %collective-permute-start = (f32[5,512]{1,0:T(8,128)S(1)}, f32[5,512]{1,0:T(8,128)S(1)}, u32[]{:S(2)}, u32[]{:S(2)}) collective-permute-start(f32[5,512]{1,0:T(8,128)S(1)} %stack.46), channel_id=1, source_target_pairs={{0,8},{8,0},{1,9},{9,1},{2,10},{10,2},{3,11},{11,3},{4,12},{12,4},... | collective-permute-start | bytes 30728 | tf_op jit(solution)/shard_map/ppermute | solution.py:36
  16.2 13.2 %all-to-all-start = ((f32[16,5,512]{2,1,0:T(8,128)}), f32[16,5,512]{2,1,0:T(8,128)S(1)}, u32[]{:S(2)}, u32[]{:S(2)}) async-start(f32[16,5,512]{2,1,0:T(8,128)} %broadcast_in_dim.8), calls=%async_computation | async-start | bytes 524288 | tf_op jit(solution)/shard_map/all_to_all | solution.py:41
  21.2 83.3 %all-gather.7.cloned.1.call-start = ((), (), s32[]{:S(2)}) async-start(), calls=%async_computation.4 | async-start | bytes 2359296 | tf_op jit(solution)/shard_map/all_gather | solution.py:300
  21.2 21.2 %collective-permute-start.2 = (bf16[256,512]{1,0:T(8,128)(2,1)}, bf16[256,512]{1,0:T(8,128)(2,1)S(1)}, u32[]{:S(2)}, u32[]{:S(2)}) collective-permute-start(bf16[256,512]{1,0:T(8,128)(2,1)} %param.3), channel_id=1, source_target_pairs={{0,8},{8,0},{1,9},{9,1},{2,10},{10,2},{3,11},{11,3},{4,12},{12,4},... | collective-permute-start | bytes 786440 | tf_op jit(solution)/shard_map/ppermute | solution.py:36
  30.6 11.9 %collective-permute-start.1 = (bf16[256,512]{1,0:T(8,128)(2,1)S(1)}, bf16[256,512]{1,0:T(8,128)(2,1)S(1)}, u32[]{:S(2)}, u32[]{:S(2)}) collective-permute-start(bf16[256,512]{1,0:T(8,128)(2,1)S(1)} %fusion.8), channel_id=1, source_target_pairs={{0,8},{8,0},{1,9},{9,1},{2,10},{10,2},{3,11},{11,3},{4,12},{12,4},... | collective-permute-start | bytes 786440 | tf_op jit(solution)/shard_map/ppermute | solution.py:36
  32.9 18.9 %all-to-all-start.1 = ((f32[8,6,512]{2,1,0:T(8,128)}), f32[8,6,512]{2,1,0:T(8,128)S(1)}, u32[]{:S(2)}, u32[]{:S(2)}) async-start(f32[8,6,512]{2,1,0:T(8,128)} %broadcast_in_dim.9), calls=%async_computation.1 | async-start | bytes 262144 | tf_op jit(solution)/shard_map/all_to_all | solution.py:41
  58.6 2.2 %copy-start = (bf16[4096,512]{1,0:T(8,128)(2,1)S(1)}, bf16[4096,512]{1,0:T(8,128)(2,1)}, u32[]{:S(2)}) copy-start(bf16[4096,512]{1,0:T(8,128)(2,1)} %all-gather.5.cloned.1.call-done) | copy-start | bytes 12582916
  62.6 9.6 %collective-permute-start.3 = (bf16[8,128,256]{2,1,0:T(8,128)(2,1)S(1)}, bf16[8,128,256]{2,1,0:T(8,128)(2,1)S(1)}, u32[]{:S(2)}, u32[]{:S(2)}) collective-permute-start(bf16[8,128,256]{2,1,0:T(8,128)(2,1)S(1)} %get-tuple-element.37), channel_id=1, source_target_pairs={{0,16},{8,72},{16,32},{24,88},{32,48},{40,104},{48,0},{56,120},{64... | collective-permute-start | bytes 1572872 | tf_op jit(solution)/shard_map/ppermute | solution.py:32
  63.6 13.5 %collective-permute-start.4 = (bf16[8,128,256]{2,1,0:T(8,128)(2,1)S(1)}, bf16[8,128,256]{2,1,0:T(8,128)(2,1)S(1)}, u32[]{:S(2)}, u32[]{:S(2)}) collective-permute-start(bf16[8,128,256]{2,1,0:T(8,128)(2,1)S(1)} %get-tuple-element.38), channel_id=1, source_target_pairs={{0,48},{8,200},{16,0},{24,216},{32,16},{40,232},{48,32},{56,248},{... | collective-permute-start | bytes 1572872 | tf_op jit(solution)/shard_map/ppermute | solution.py:32
  65.4 13.1 %collective-permute-start.5 = (bf16[8,128,256]{2,1,0:T(8,128)(2,1)S(1)}, bf16[8,128,256]{2,1,0:T(8,128)(2,1)S(1)}, u32[]{:S(2)}, u32[]{:S(2)}) collective-permute-start(bf16[8,128,256]{2,1,0:T(8,128)(2,1)S(1)} %get-tuple-element.39), channel_id=1, source_target_pairs={{0,32},{8,136},{16,48},{24,152},{32,0},{40,168},{48,16},{56,184},{... | collective-permute-start | bytes 1572872 | tf_op jit(solution)/shard_map/ppermute | solution.py:32
  78.7 9.7 %collective-permute-start.6 = (bf16[8,128,256]{2,1,0:T(8,128)(2,1)S(1)}, bf16[8,128,256]{2,1,0:T(8,128)(2,1)S(1)}, u32[]{:S(2)}, u32[]{:S(2)}) collective-permute-start(bf16[8,128,256]{2,1,0:T(8,128)(2,1)S(1)} %add_convert_fusion.own), channel_id=1, source_target_pairs={{0,64},{8,24},{16,80},{24,40},{32,96},{40,56},{48,112},{56,8},{64,... | collective-permute-start | bytes 1572872 | tf_op jit(solution)/shard_map/ppermute | solution.py:32
  79.7 13.5 %collective-permute-start.7 = (bf16[8,128,256]{2,1,0:T(8,128)(2,1)S(1)}, bf16[8,128,256]{2,1,0:T(8,128)(2,1)S(1)}, u32[]{:S(2)}, u32[]{:S(2)}) collective-permute-start(bf16[8,128,256]{2,1,0:T(8,128)(2,1)S(1)} %add_convert_fusion.own), channel_id=1, source_target_pairs={{0,192},{8,56},{16,208},{24,8},{32,224},{40,24},{48,240},{56,40},{... | collective-permute-start | bytes 1572872 | tf_op jit(solution)/shard_map/ppermute | solution.py:32
  81.5 13.3 %collective-permute-start.8 = (bf16[8,128,256]{2,1,0:T(8,128)(2,1)S(1)}, bf16[8,128,256]{2,1,0:T(8,128)(2,1)S(1)}, u32[]{:S(2)}, u32[]{:S(2)}) collective-permute-start(bf16[8,128,256]{2,1,0:T(8,128)(2,1)S(1)} %add_convert_fusion.own), channel_id=1, source_target_pairs={{0,128},{8,40},{16,144},{24,56},{32,160},{40,8},{48,176},{56,24},{... | collective-permute-start | bytes 1572872 | tf_op jit(solution)/shard_map/ppermute | solution.py:32
  96.9 21.2 %all-to-all-start.2 = ((bf16[8,144,256]{2,1,0:T(8,128)(2,1)}), bf16[8,144,256]{2,1,0:T(8,128)(2,1)S(1)}, u32[]{:S(2)}, u32[]{:S(2)}) async-start(bf16[8,144,256]{2,1,0:T(8,128)(2,1)} %get-tuple-element.41), calls=%async_computation.2 | async-start | bytes 1179648 | tf_op jit(solution)/shard_map/all_to_all | solution.py:361
  101.2 9.9 %collective-permute-start.10 = (bf16[8,128,256]{2,1,0:T(8,128)(2,1)S(1)}, bf16[8,128,256]{2,1,0:T(8,128)(2,1)S(1)}, u32[]{:S(2)}, u32[]{:S(2)}) collective-permute-start(bf16[8,128,256]{2,1,0:T(8,128)(2,1)S(1)} %get-tuple-element.43.refs_0_), channel_id=1, source_target_pairs={{0,32},{8,136},{16,48},{24,152},{32,0},{40,168},{48,16},{56,184},{... | collective-permute-start | bytes 1572872 | tf_op jit(solution)/shard_map/ppermute | solution.py:32
  101.8 14.8 %collective-permute-start.11 = (bf16[8,128,256]{2,1,0:T(8,128)(2,1)S(1)}, bf16[8,128,256]{2,1,0:T(8,128)(2,1)S(1)}, u32[]{:S(2)}, u32[]{:S(2)}) collective-permute-start(bf16[8,128,256]{2,1,0:T(8,128)(2,1)S(1)} %get-tuple-element.43.refs_0_), channel_id=1, source_target_pairs={{0,16},{8,72},{16,32},{24,88},{32,48},{40,104},{48,0},{56,120},{64... | collective-permute-start | bytes 1572872 | tf_op jit(solution)/shard_map/ppermute | solution.py:32
  103.8 12.8 %collective-permute-start.9 = (bf16[8,128,256]{2,1,0:T(8,128)(2,1)S(1)}, bf16[8,128,256]{2,1,0:T(8,128)(2,1)}, u32[]{:S(2)}, u32[]{:S(2)}) collective-permute-start(bf16[8,128,256]{2,1,0:T(8,128)(2,1)S(1)} %get-tuple-element.43.refs_0_), channel_id=1, source_target_pairs={{0,48},{8,200},{16,0},{24,216},{32,16},{40,232},{48,32},{56,248},{... | collective-permute-start | bytes 1572872 | tf_op jit(solution)/shard_map/ppermute | solution.py:32
  118.2 11.5 %collective-permute-start.12 = (bf16[8,256,512]{2,1,0:T(8,128)(2,1)}, bf16[8,256,512]{2,1,0:T(8,128)(2,1)S(1)}, u32[]{:S(2)}, u32[]{:S(2)}) collective-permute-start(bf16[8,256,512]{2,1,0:T(8,128)(2,1)} %bitcast.44), channel_id=1, source_target_pairs={{0,8},{8,0},{1,9},{9,1},{2,10},{10,2},{3,11},{11,3},{4,12},{12,4},... | collective-permute-start | bytes 6291464 | tf_op jit(solution)/shard_map/ppermute | solution.py:36
  121.1 15.3 %collective-permute-start.13 = (bf16[8,144,256]{2,1,0:T(8,128)(2,1)S(1)}, bf16[8,144,256]{2,1,0:T(8,128)(2,1)S(1)}, u32[]{:S(2)}, u32[]{:S(2)}) collective-permute-start(bf16[8,144,256]{2,1,0:T(8,128)(2,1)S(1)} %all-to-all-done.2.refs_0_), channel_id=1, source_target_pairs={{0,48},{8,200},{16,0},{24,216},{32,16},{40,232},{48,32},{56,248},{... | collective-permute-start | bytes 1769480 | tf_op jit(solution)/shard_map/ppermute | solution.py:32
  123.2 13.2 %collective-permute-start.14 = (bf16[8,144,256]{2,1,0:T(8,128)(2,1)S(1)}, bf16[8,144,256]{2,1,0:T(8,128)(2,1)S(1)}, u32[]{:S(2)}, u32[]{:S(2)}) collective-permute-start(bf16[8,144,256]{2,1,0:T(8,128)(2,1)S(1)} %all-to-all-done.2.refs_0_), channel_id=1, source_target_pairs={{0,32},{8,136},{16,48},{24,152},{32,0},{40,168},{48,16},{56,184},{... | collective-permute-start | bytes 1769480 | tf_op jit(solution)/shard_map/ppermute | solution.py:32
  123.5 16.5 %collective-permute-start.15 = (bf16[8,144,256]{2,1,0:T(8,128)(2,1)S(1)}, bf16[8,144,256]{2,1,0:T(8,128)(2,1)S(1)}, u32[]{:S(2)}, u32[]{:S(2)}) collective-permute-start(bf16[8,144,256]{2,1,0:T(8,128)(2,1)S(1)} %all-to-all-done.2.refs_0_), channel_id=1, source_target_pairs={{0,16},{8,72},{16,32},{24,88},{32,48},{40,104},{48,0},{56,120},{64... | collective-permute-start | bytes 1769480 | tf_op jit(solution)/shard_map/ppermute | solution.py:32
  123.9 2.2 %copy-start.1 = (bf16[4096,512]{1,0:T(8,128)(2,1)S(1)}, bf16[4096,512]{1,0:T(8,128)(2,1)}, u32[]{:S(2)}) copy-start(bf16[4096,512]{1,0:T(8,128)(2,1)} %all-gather.5.cloned.1.call-done) | copy-start | bytes 12582916
  126.1 3.6 %copy-start.5 = (bf16[2048,512]{1,0:T(8,128)(2,1)S(1)}, bf16[2048,512]{1,0:T(8,128)(2,1)}, u32[]{:S(2)}) copy-start(bf16[2048,512]{1,0:T(8,128)(2,1)} %all-gather.7.cloned.1.call-done) | copy-start | bytes 6291460
  130.8 13.1 %copy-start.4 = (bf16[256,512]{1,0:T(8,128)(2,1)S(1)}, bf16[256,512]{1,0:T(8,128)(2,1)}, u32[]{:S(2)}) copy-start(bf16[256,512]{1,0:T(8,128)(2,1)} %param.3) | copy-start | bytes 786436
  130.8 14.1 %copy-start.2 = (bf16[256,512]{1,0:T(8,128)(2,1)S(1)}, bf16[256,512]{1,0:T(8,128)(2,1)}, u32[]{:S(2)}) copy-start(bf16[256,512]{1,0:T(8,128)(2,1)} %view.1) | copy-start | bytes 786436
  130.8 14.1 %collective-permute-start.18 = (f32[272,512]{1,0:T(8,128)S(1)}, f32[272,512]{1,0:T(8,128)S(1)}, u32[]{:S(2)}, u32[]{:S(2)}) collective-permute-start(f32[272,512]{1,0:T(8,128)S(1)} %get-tuple-element.57), channel_id=1, source_target_pairs={{0,8},{8,0},{1,9},{9,1},{2,10},{10,2},{3,11},{11,3},{4,12},{12,4},... | collective-permute-start | bytes 1671176 | tf_op jit(solution)/shard_map/ppermute | solution.py:36
  142.4 2.5 %collective-permute-start.16 = (bf16[256,256]{1,0:T(8,128)(2,1)S(1)}, bf16[256,256]{1,0:T(8,128)(2,1)S(1)}, u32[]{:S(2)}, u32[]{:S(2)}) collective-permute-start(bf16[256,256]{1,0:T(8,128)(2,1)S(1)} %get-tuple-element.54), channel_id=1, source_target_pairs={{0,8},{8,0},{1,9},{9,1},{2,10},{10,2},{3,11},{11,3},{4,12},{12,4},... | collective-permute-start | bytes 393224 | tf_op jit(solution)/shard_map/ppermute | solution.py:36
  143.8 1.1 collective-permute-start.17
Sparse Core Ops, SparseCore 0:
  9.8 48.7 all-gather.4
  60.4 35.5 all-gather.6

commit v3 on v2

--- a/solution.py
+++ b/solution.py
@@ -152,6 +152,40 @@
     along = weight + pull * match
     white = (view.astype(F32) - mean) * inverse
     return (inverse * (back - centre - white * along)).astype(BF16)
+
+
+def gather_share(lines):
+    lines = lines.astype(F32)
+    return (lines[0:1] + lines[1:2]) + lines[2:3]
+
+
+def compact_body(inward, out):
+    blocks, lines, half = inward.shape
+    quarter = lines - EXTRA
+    share = jnp.zeros((1, half), F32)
+    for g in range(blocks):
+        out[g * quarter : (g + 1) * quarter] = inward[g, :quarter]
+        share = share + gather_share(inward[g, quarter:])
+    share = jnp.broadcast_to(share, (EXTRA, half))
+    high = share.astype(BF16)
+    share = share - high.astype(F32)
+    middle = share.astype(BF16)
+    low = (share - middle.astype(F32)).astype(BF16)
+    line = lax.broadcasted_iota(jnp.int32, (EXTRA, half), 0)
+    out[blocks * quarter :] = jnp.where(line == 0, high, jnp.where(line == 1, middle, low))
+
+
+def compact(inward):
+    blocks, lines, half = inward.shape
+    return pl.pallas_call(
+        compact_body,
+        in_specs=[VMEM],
+        out_specs=VMEM,
+        out_shape=jax.ShapeDtypeStruct((blocks * (lines - EXTRA) + EXTRA, half), BF16),
+        compiler_params=pltpu.CompilerParams(vmem_limit_bytes=2 * MIB),
+        cost_estimate=pl.CostEstimate(flops=1, bytes_accessed=MIB, transcendentals=0),
+        name="compact",
+    )(inward)
 
 
 def rows_body(at, raw, stats, *refs):
@@ -198,7 +232,8 @@
     size = jnp.zeros((1, half), F32)
     for g in range(blocks):
         for turned in range(4):
-            packed[g, place(at, turned, width // 4)] = pieces[turned][g, : width // 4]
+            lines = slice(g * (width // 4), (g + 1) * (width // 4))
+            packed[g, place(at, turned, width // 4)] = pieces[turned][lines]
         rhs = packed[g]
         square = rhs.astype(F32)
         size = size + jnp.sum(square * square, axis=0, keepdims=True)
@@ -209,13 +244,7 @@
             total[...] += part
         else:
             total[...] = part
-    shares = []
-    for turned in range(4):
-        share = jnp.zeros((1, 128), F32)
-        for g in range(blocks):
-            lines = pieces[turned][g, width // 4 :, :128].astype(F32)
-            share = share + ((lines[0:1] + lines[1:2]) + lines[2:3])
-        shares.append(share)
+    shares = [gather_share(piece[blocks * (width // 4) :, :128]) for piece in pieces]
     loss[...] = (shares[0] + shares[2]) + (shares[1] + shares[3])
     weight = size * (0.5 / OFF_WEIGHT)
     for which, grad in enumerate((near_grad, far_grad)):
@@ -363,6 +392,7 @@
     ahead, behind, across = others(pull)
     row_pieces = [pull, behind, across, ahead]
     row_pieces, inward, raw_a = lax.optimization_barrier((row_pieces, inward, raw_a))
+    inward = compact(inward)
     ahead, behind, across = others(inward)
     col_pieces = [inward, behind, across, ahead]
 

time: 154 us -> 153 us (level)
  no operation moved by 1% of the time
where the time goes in v3:
time: 153 us; the launch traced here: 152 us
  waiting for transfers between devices  69.4 us (45%)
  starting transfers between devices  42.2 us (28%)
  between operations  15 us (10%)
  Pallas kernels  11.3 us (7%)
  other arithmetic  7.13 us (5%)
  local copies, waits for them, and re-layouts  7.04 us (5%)
    ppermute x12, waiting for transfers between devices, shift(): return lax.ppermute(value, ('y', 'x', 'c'), pairs)  43.5 us
    all_to_all x2, waiting for transfers between devices, spread(): return lax.all_to_all(copies, axes, split_axis=0, concat_axis=0, tiled=True)  15 us
    ppermute x12, starting transfers between devices, shift(): return lax.ppermute(value, ('y', 'x', 'c'), pairs)  13.9 us
    all_to_all x2, starting transfers between devices, spread(): return lax.all_to_all(copies, axes, split_axis=0, concat_axis=0, tiled=True)  13.2 us
    ppermute x7, starting transfers between devices, swap(): return lax.ppermute(value, 'c', [(0, 1), (1, 0)])  10.8 us
    all_gather x1, waiting for transfers between devices, local(): raw_b = lax.all_gather(view_b, ('c', 'z'), axis=0, tiled=False)  6.87 us
    pallas_call x2, Pallas kernels, gradient(): pl.pallas_call(body, in_specs=[SMEM] + [VMEM] * (len(operands) - 1), out_...  5.88 us
    unnamed x13, local copies, waits for them, and re-layouts  4.4 us
  transfers between devices with their start and end apart: 24, of which 16 were waited for; matrix products, arithmetic and copies ran while one was open for 6% of the time, Pallas kernels for 6%

profile of v3, /device:TPU:1, one launch (start us, length us, event | category | flops | bytes accessed | tf_op | source)
XLA Modules:
  0.0 152.0 jit_solution(6892132277691663262)
XLA Ops:
  7.2 0.7 all-gather.5.cloned.1.call-update
  7.9 1.0 convert_reduce_fusion
  8.9 1.0 convert_reduce_fusion.1
  10.0 1.2 fusion.5
  11.2 3.3 %collective-permute-start = (f32[5,512]{1,0:T(8,128)S(1)}, f32[5,512]{1,0:T(8,128)S(1)}, u32[]{:S(2)}, u32[]{:S(2)}) collective-permute-start(f32[5,512]{1,0:T(8,128)S(1)} %stack.46), channel_id=1, source_target_pairs={{0,8},{8,0},{1,9},{9,1},{2,10},{10,2},{3,11},{11,3},{4,12},{12,4},... | collective-permute-start | bytes 30728 | tf_op jit(solution)/shard_map/ppermute | solution.py:36
  14.5 0.8 collective-permute-done
  15.4 0.7 broadcast_in_dim.8
  16.2 5.0 %all-to-all-start = ((f32[16,5,512]{2,1,0:T(8,128)}), f32[16,5,512]{2,1,0:T(8,128)S(1)}, u32[]{:S(2)}, u32[]{:S(2)}) async-start(f32[16,5,512]{2,1,0:T(8,128)} %broadcast_in_dim.8), calls=%async_computation | async-start | bytes 524288 | tf_op jit(solution)/shard_map/all_to_all | solution.py:41
  21.2 0.7 collective-permute-start.2
  22.1 7.3 %all-to-all-done = f32[16,5,512]{2,1,0:T(8,128)S(1)} async-done(((f32[16,5,512]{2,1,0:T(8,128)}), f32[16,5,512]{2,1,0:T(8,128)S(1)}, u32[]{:S(2)}, u32[]{:S(2)}) %all-to-all-start) | async-done | bytes 163872 | tf_op jit(solution)/shard_map/all_to_all | solution.py:41
  29.6 1.0 fusion.8
  30.6 1.6 %collective-permute-start.1 = (bf16[256,512]{1,0:T(8,128)(2,1)S(1)}, bf16[256,512]{1,0:T(8,128)(2,1)S(1)}, u32[]{:S(2)}, u32[]{:S(2)}) collective-permute-start(bf16[256,512]{1,0:T(8,128)(2,1)S(1)} %fusion.8), channel_id=1, source_target_pairs={{0,8},{8,0},{1,9},{9,1},{2,10},{10,2},{3,11},{11,3},{4,12},{12,4},... | collective-permute-start | bytes 786440 | tf_op jit(solution)/shard_map/ppermute | solution.py:36
  32.9 8.2 %all-to-all-start.1 = ((f32[8,6,512]{2,1,0:T(8,128)}), f32[8,6,512]{2,1,0:T(8,128)S(1)}, u32[]{:S(2)}, u32[]{:S(2)}) async-start(f32[8,6,512]{2,1,0:T(8,128)} %broadcast_in_dim.9), calls=%async_computation.1 | async-start | bytes 262144 | tf_op jit(solution)/shard_map/all_to_all | solution.py:41
  42.7 1.0 fusion.12
  44.0 7.7 %all-to-all-done.1.stats = f32[8,6,512]{2,1,0:T(8,128)S(1)} async-done(((f32[8,6,512]{2,1,0:T(8,128)}), f32[8,6,512]{2,1,0:T(8,128)S(1)}, u32[]{:S(2)}, u32[]{:S(2)}) %all-to-all-start.1) | async-done | bytes 98336 | tf_op jit(solution)/shard_map/all_to_all | solution.py:41
  51.7 6.9 %all-gather.5.cloned.1.call-done = bf16[4096,512]{1,0:T(8,128)(2,1)} async-done(((bf16[256,512]{1,0:T(8,128)(2,1)}), bf16[4096,512]{1,0:T(8,128)(2,1)}) %all-gather.5.cloned.1.call-update) | async-done | bytes 4194320 | tf_op jit(solution)/shard_map/all_gather | solution.py:328
  58.6 2.2 %copy-done = bf16[4096,512]{1,0:T(8,128)(2,1)S(1)} copy-done((bf16[4096,512]{1,0:T(8,128)(2,1)S(1)}, bf16[4096,512]{1,0:T(8,128)(2,1)}, u32[]{:S(2)}) %copy-start) | copy-done | bytes 4194328
  60.8 1.8 %correlate.1 = (bf16[8,128,256]{2,1,0:T(8,128)(2,1)S(1)}, bf16[8,128,256]{2,1,0:T(8,128)(2,1)S(1)}, bf16[8,128,256]{2,1,0:T(8,128)(2,1)S(1)}, bf16[8,128,256]{2,1,0:T(8,128)(2,1)S(1)}) custom-call(s32[5]{0:T(128)S(1)} %stack.41.at, f32[8,6,512]{2,1,0:T(8,128)S(1)} %all-to-all-done.1.stats, bf16[16,256,512]{2,1,0:T(8,128)(2,1)S(1)} %bitcast.41, ...), custom_call_target="tpu_custom_call" | custom-call | flops 1073741824 | bytes 6291456 | tf_op jit(solution)/shard_map/correlate/pallas_call | solution.py:84
  62.6 1.0 collective-permute-start.3
  63.6 1.8 %collective-permute-start.4 = (bf16[8,128,256]{2,1,0:T(8,128)(2,1)S(1)}, bf16[8,128,256]{2,1,0:T(8,128)(2,1)S(1)}, u32[]{:S(2)}, u32[]{:S(2)}) collective-permute-start(bf16[8,128,256]{2,1,0:T(8,128)(2,1)S(1)} %get-tuple-element.38), channel_id=1, source_target_pairs={{0,48},{8,200},{16,0},{24,216},{32,16},{40,232},{48,32},{56,248},{... | collective-permute-start | bytes 1572872 | tf_op jit(solution)/shard_map/ppermute | solution.py:32
  65.4 1.2 collective-permute-start.5
  66.5 5.7 %collective-permute-done.3 = bf16[8,128,256]{2,1,0:T(8,128)(2,1)S(1)} collective-permute-done((bf16[8,128,256]{2,1,0:T(8,128)(2,1)S(1)}, bf16[8,128,256]{2,1,0:T(8,128)(2,1)S(1)}, u32[]{:S(2)}, u32[]{:S(2)}) %collective-permute-start.3) | collective-permute-done | bytes 524320 | tf_op jit(solution)/shard_map/ppermute | solution.py:32
  72.2 4.9 %collective-permute-done.4 = bf16[8,128,256]{2,1,0:T(8,128)(2,1)S(1)} collective-permute-done((bf16[8,128,256]{2,1,0:T(8,128)(2,1)S(1)}, bf16[8,128,256]{2,1,0:T(8,128)(2,1)S(1)}, u32[]{:S(2)}, u32[]{:S(2)}) %collective-permute-start.4) | collective-permute-done | bytes 524320 | tf_op jit(solution)/shard_map/ppermute | solution.py:32
  77.1 1.3 collective-permute-done.5
  78.7 1.0 collective-permute-start.6
  79.7 1.8 %collective-permute-start.7 = (bf16[8,128,256]{2,1,0:T(8,128)(2,1)S(1)}, bf16[8,128,256]{2,1,0:T(8,128)(2,1)S(1)}, u32[]{:S(2)}, u32[]{:S(2)}) collective-permute-start(bf16[8,128,256]{2,1,0:T(8,128)(2,1)S(1)} %add_convert_fusion.own), channel_id=1, source_target_pairs={{0,192},{8,56},{16,208},{24,8},{32,224},{40,24},{48,240},{56,40},{... | collective-permute-start | bytes 1572872 | tf_op jit(solution)/shard_map/ppermute | solution.py:32
  81.5 1.2 collective-permute-start.8
  82.7 5.8 %collective-permute-done.6.ahead = bf16[8,128,256]{2,1,0:T(8,128)(2,1)S(1)} collective-permute-done((bf16[8,128,256]{2,1,0:T(8,128)(2,1)S(1)}, bf16[8,128,256]{2,1,0:T(8,128)(2,1)S(1)}, u32[]{:S(2)}, u32[]{:S(2)}) %collective-permute-start.6) | collective-permute-done | bytes 524320 | tf_op jit(solution)/shard_map/ppermute | solution.py:32
  88.4 4.8 %collective-permute-done.7.behind = bf16[8,128,256]{2,1,0:T(8,128)(2,1)S(1)} collective-permute-done((bf16[8,128,256]{2,1,0:T(8,128)(2,1)S(1)}, bf16[8,128,256]{2,1,0:T(8,128)(2,1)S(1)}, u32[]{:S(2)}, u32[]{:S(2)}) %collective-permute-start.7) | collective-permute-done | bytes 524320 | tf_op jit(solution)/shard_map/ppermute | solution.py:32
  93.2 1.6 %collective-permute-done.8.across = bf16[8,128,256]{2,1,0:T(8,128)(2,1)S(1)} collective-permute-done((bf16[8,128,256]{2,1,0:T(8,128)(2,1)S(1)}, bf16[8,128,256]{2,1,0:T(8,128)(2,1)S(1)}, u32[]{:S(2)}, u32[]{:S(2)}) %collective-permute-start.8) | collective-permute-done | bytes 524320 | tf_op jit(solution)/shard_map/ppermute | solution.py:32
  94.8 2.1 %tile.1 = (bf16[8,128,256]{2,1,0:T(8,128)(2,1)S(1)}, bf16[8,144,256]{2,1,0:T(8,128)(2,1)}) custom-call(s32[5]{0:T(128)S(1)} %stack.41.at, f32[1,128]{1,0:T(1,128)S(1)} %broadcast_in_dim.11.diagonal, bf16[8,128,256]{2,1,0:T(8,128)(2,1)S(1)} %add_convert_fusion.own, bf16[8,128,256]{2,1,0:T(8,128)(2,1)S(1)} %collective-permute-done.6.ahead, ...), custom_call_target="tpu_custom_call" | custom-call | flops 1572864 | bytes 3145728 | tf_op jit(solution)/shard_map/tile/pallas_call | solution.py:126
  96.9 4.3 %all-to-all-start.2 = ((bf16[8,144,256]{2,1,0:T(8,128)(2,1)}), bf16[8,144,256]{2,1,0:T(8,128)(2,1)S(1)}, u32[]{:S(2)}, u32[]{:S(2)}) async-start(bf16[8,144,256]{2,1,0:T(8,128)(2,1)} %get-tuple-element.41), calls=%async_computation.2 | async-start | bytes 1179648 | tf_op jit(solution)/shard_map/all_to_all | solution.py:390
  101.8 2.0 %collective-permute-start.11 = (bf16[8,128,256]{2,1,0:T(8,128)(2,1)S(1)}, bf16[8,128,256]{2,1,0:T(8,128)(2,1)S(1)}, u32[]{:S(2)}, u32[]{:S(2)}) collective-permute-start(bf16[8,128,256]{2,1,0:T(8,128)(2,1)S(1)} %get-tuple-element.43.refs_0_), channel_id=1, source_target_pairs={{0,16},{8,72},{16,32},{24,88},{32,48},{40,104},{48,0},{56,120},{64... | collective-permute-start | bytes 1572872 | tf_op jit(solution)/shard_map/ppermute | solution.py:32
  104.5 6.6 %collective-permute-done.10.refs_2_ = bf16[8,128,256]{2,1,0:T(8,128)(2,1)S(1)} collective-permute-done((bf16[8,128,256]{2,1,0:T(8,128)(2,1)S(1)}, bf16[8,128,256]{2,1,0:T(8,128)(2,1)S(1)}, u32[]{:S(2)}, u32[]{:S(2)}) %collective-permute-start.10) | collective-permute-done | bytes 524320 | tf_op jit(solution)/shard_map/ppermute | solution.py:32
  111.1 5.6 %collective-permute-done.11.refs_3_ = bf16[8,128,256]{2,1,0:T(8,128)(2,1)S(1)} collective-permute-done((bf16[8,128,256]{2,1,0:T(8,128)(2,1)S(1)}, bf16[8,128,256]{2,1,0:T(8,128)(2,1)S(1)}, u32[]{:S(2)}, u32[]{:S(2)}) %collective-permute-start.11) | collective-permute-done | bytes 524320 | tf_op jit(solution)/shard_map/ppermute | solution.py:32
  116.6 1.5 all-to-all-done.2.inward
  118.2 2.9 %collective-permute-start.12 = (bf16[8,256,512]{2,1,0:T(8,128)(2,1)}, bf16[8,256,512]{2,1,0:T(8,128)(2,1)S(1)}, u32[]{:S(2)}, u32[]{:S(2)}) collective-permute-start(bf16[8,256,512]{2,1,0:T(8,128)(2,1)} %bitcast.44), channel_id=1, source_target_pairs={{0,8},{8,0},{1,9},{9,1},{2,10},{10,2},{3,11},{11,3},{4,12},{12,4},... | collective-permute-start | bytes 6291464 | tf_op jit(solution)/shard_map/ppermute | solution.py:36
  121.1 2.1 %collective-permute-start.13 = (bf16[1040,256]{1,0:T(8,128)(2,1)S(1)}, bf16[1040,256]{1,0:T(8,128)(2,1)S(1)}, u32[]{:S(2)}, u32[]{:S(2)}) collective-permute-start(bf16[1040,256]{1,0:T(8,128)(2,1)S(1)} %compact.1.refs_0_), channel_id=1, source_target_pairs={{0,48},{8,200},{16,0},{24,216},{32,16},{40,232},{48,32},{56,248},{... | collective-permute-start | bytes 1597448 | tf_op jit(solution)/shard_map/ppermute | solution.py:32
  123.9 2.2 %copy-done.1 = bf16[4096,512]{1,0:T(8,128)(2,1)S(1)} copy-done((bf16[4096,512]{1,0:T(8,128)(2,1)S(1)}, bf16[4096,512]{1,0:T(8,128)(2,1)}, u32[]{:S(2)}) %copy-start.1) | copy-done | bytes 4194328
  126.1 3.6 %rows.1 = (f32[272,512]{1,0:T(8,128)S(1)}, f32[272,512]{1,0:T(8,128)S(1)}) custom-call(s32[5]{0:T(128)S(1)} %stack.41.at, bf16[16,256,512]{2,1,0:T(8,128)(2,1)S(1)} %bitcast.42, f32[8,6,512]{2,1,0:T(8,128)S(1)} %all-to-all-done.1.stats, bf16[8,128,256]{2,1,0:T(8,128)(2,1)S(1)} %get-tuple-element.43.refs_0_, ...), custom_call_target="tpu_custom_call" | custom-call | flops 1073741824 | bytes 7340032 | tf_op jit(solution)/shard_map/rows/pallas_call | solution.py:266
  129.7 1.1 reduce-precision_convert_fusion
  130.9 0.8 collective-permute-start.18
  131.6 3.5 %collective-permute-done.13.refs_1_ = bf16[1040,256]{1,0:T(8,128)(2,1)S(1)} collective-permute-done((bf16[1040,256]{1,0:T(8,128)(2,1)S(1)}, bf16[1040,256]{1,0:T(8,128)(2,1)S(1)}, u32[]{:S(2)}, u32[]{:S(2)}) %collective-permute-start.13) | collective-permute-done | bytes 532512 | tf_op jit(solution)/shard_map/ppermute | solution.py:32
  135.2 3.7 %collective-permute-done.15.refs_3_ = bf16[1040,256]{1,0:T(8,128)(2,1)S(1)} collective-permute-done((bf16[1040,256]{1,0:T(8,128)(2,1)S(1)}, bf16[1040,256]{1,0:T(8,128)(2,1)S(1)}, u32[]{:S(2)}, u32[]{:S(2)}) %collective-permute-start.15) | collective-permute-done | bytes 532512 | tf_op jit(solution)/shard_map/ppermute | solution.py:32
  138.9 2.3 %cols.1 = (bf16[256,256]{1,0:T(8,128)(2,1)S(1)}, bf16[256,256]{1,0:T(8,128)(2,1)S(1)}, f32[1,128]{1,0:T(1,128)S(1)}) custom-call(s32[5]{0:T(128)S(1)} %stack.41.at, bf16[8,256,512]{2,1,0:T(8,128)(2,1)S(1)} %get-tuple-element.78.near, bf16[8,256,512]{2,1,0:T(8,128)(2,1)S(1)} %get-tuple-element.48.far, f32[8,6,512]{2,1,0:T(8,128)S(1)} %all-to-all-done.1.stats, ...), custom_call_target="tpu_custom_call" | custom-call | flops 1073741824 | bytes 7340032 | tf_op jit(solution)/shard_map/cols/pallas_call | solution.py:266
  141.2 1.4 collective-permute-start.16
  142.7 1.0 collective-permute-done.17.other_loss
  143.7 1.5 join.1
  (57 shorter events, 5.0 us)
Async XLA Ops:
  7.2 35.3 %copy-start.3 = (bf16[256,512]{1,0:T(8,128)(2,1)S(1)}, bf16[256,512]{1,0:T(8,128)(2,1)}, u32[]{:S(2)}) copy-start(bf16[256,512]{1,0:T(8,128)(2,1)} %param.3) | copy-start | bytes 786436
  7.2 51.4 %all-gather.5.cloned.1.call-start = ((), (), s32[]{:S(2)}) async-start(), calls=%async_computation.3 | async-start | bytes 4456448 | tf_op jit(solution)/shard_map/all_gather | solution.py:328
  11.2 4.2 %collective-permute-start = (f32[5,512]{1,0:T(8,128)S(1)}, f32[5,512]{1,0:T(8,128)S(1)}, u32[]{:S(2)}, u32[]{:S(2)}) collective-permute-start(f32[5,512]{1,0:T(8,128)S(1)} %stack.46), channel_id=1, source_target_pairs={{0,8},{8,0},{1,9},{9,1},{2,10},{10,2},{3,11},{11,3},{4,12},{12,4},... | collective-permute-start | bytes 30728 | tf_op jit(solution)/shard_map/ppermute | solution.py:36
  16.2 13.2 %all-to-all-start = ((f32[16,5,512]{2,1,0:T(8,128)}), f32[16,5,512]{2,1,0:T(8,128)S(1)}, u32[]{:S(2)}, u32[]{:S(2)}) async-start(f32[16,5,512]{2,1,0:T(8,128)} %broadcast_in_dim.8), calls=%async_computation | async-start | bytes 524288 | tf_op jit(solution)/shard_map/all_to_all | solution.py:41
  21.2 83.3 %all-gather.7.cloned.1.call-start = ((), (), s32[]{:S(2)}) async-start(), calls=%async_computation.4 | async-start | bytes 2359296 | tf_op jit(solution)/shard_map/all_gather | solution.py:329
  21.2 21.2 %collective-permute-start.2 = (bf16[256,512]{1,0:T(8,128)(2,1)}, bf16[256,512]{1,0:T(8,128)(2,1)S(1)}, u32[]{:S(2)}, u32[]{:S(2)}) collective-permute-start(bf16[256,512]{1,0:T(8,128)(2,1)} %param.3), channel_id=1, source_target_pairs={{0,8},{8,0},{1,9},{9,1},{2,10},{10,2},{3,11},{11,3},{4,12},{12,4},... | collective-permute-start | bytes 786440 | tf_op jit(solution)/shard_map/ppermute | solution.py:36
  30.6 11.9 %collective-permute-start.1 = (bf16[256,512]{1,0:T(8,128)(2,1)S(1)}, bf16[256,512]{1,0:T(8,128)(2,1)S(1)}, u32[]{:S(2)}, u32[]{:S(2)}) collective-permute-start(bf16[256,512]{1,0:T(8,128)(2,1)S(1)} %fusion.8), channel_id=1, source_target_pairs={{0,8},{8,0},{1,9},{9,1},{2,10},{10,2},{3,11},{11,3},{4,12},{12,4},... | collective-permute-start | bytes 786440 | tf_op jit(solution)/shard_map/ppermute | solution.py:36
  32.9 18.9 %all-to-all-start.1 = ((f32[8,6,512]{2,1,0:T(8,128)}), f32[8,6,512]{2,1,0:T(8,128)S(1)}, u32[]{:S(2)}, u32[]{:S(2)}) async-start(f32[8,6,512]{2,1,0:T(8,128)} %broadcast_in_dim.9), calls=%async_computation.1 | async-start | bytes 262144 | tf_op jit(solution)/shard_map/all_to_all | solution.py:41
  58.6 2.2 %copy-start = (bf16[4096,512]{1,0:T(8,128)(2,1)S(1)}, bf16[4096,512]{1,0:T(8,128)(2,1)}, u32[]{:S(2)}) copy-start(bf16[4096,512]{1,0:T(8,128)(2,1)} %all-gather.5.cloned.1.call-done) | copy-start | bytes 12582916
  62.6 9.6 %collective-permute-start.3 = (bf16[8,128,256]{2,1,0:T(8,128)(2,1)S(1)}, bf16[8,128,256]{2,1,0:T(8,128)(2,1)S(1)}, u32[]{:S(2)}, u32[]{:S(2)}) collective-permute-start(bf16[8,128,256]{2,1,0:T(8,128)(2,1)S(1)} %get-tuple-element.37), channel_id=1, source_target_pairs={{0,16},{8,72},{16,32},{24,88},{32,48},{40,104},{48,0},{56,120},{64... | collective-permute-start | bytes 1572872 | tf_op jit(solution)/shard_map/ppermute | solution.py:32
  63.6 13.5 %collective-permute-start.4 = (bf16[8,128,256]{2,1,0:T(8,128)(2,1)S(1)}, bf16[8,128,256]{2,1,0:T(8,128)(2,1)S(1)}, u32[]{:S(2)}, u32[]{:S(2)}) collective-permute-start(bf16[8,128,256]{2,1,0:T(8,128)(2,1)S(1)} %get-tuple-element.38), channel_id=1, source_target_pairs={{0,48},{8,200},{16,0},{24,216},{32,16},{40,232},{48,32},{56,248},{... | collective-permute-start | bytes 1572872 | tf_op jit(solution)/shard_map/ppermute | solution.py:32
  65.4 13.1 %collective-permute-start.5 = (bf16[8,128,256]{2,1,0:T(8,128)(2,1)S(1)}, bf16[8,128,256]{2,1,0:T(8,128)(2,1)S(1)}, u32[]{:S(2)}, u32[]{:S(2)}) collective-permute-start(bf16[8,128,256]{2,1,0:T(8,128)(2,1)S(1)} %get-tuple-element.39), channel_id=1, source_target_pairs={{0,32},{8,136},{16,48},{24,152},{32,0},{40,168},{48,16},{56,184},{... | collective-permute-start | bytes 1572872 | tf_op jit(solution)/shard_map/ppermute | solution.py:32
  78.7 9.7 %collective-permute-start.6 = (bf16[8,128,256]{2,1,0:T(8,128)(2,1)S(1)}, bf16[8,128,256]{2,1,0:T(8,128)(2,1)S(1)}, u32[]{:S(2)}, u32[]{:S(2)}) collective-permute-start(bf16[8,128,256]{2,1,0:T(8,128)(2,1)S(1)} %add_convert_fusion.own), channel_id=1, source_target_pairs={{0,64},{8,24},{16,80},{24,40},{32,96},{40,56},{48,112},{56,8},{64,... | collective-permute-start | bytes 1572872 | tf_op jit(solution)/shard_map/ppermute | solution.py:32
  79.7 13.5 %collective-permute-start.7 = (bf16[8,128,256]{2,1,0:T(8,128)(2,1)S(1)}, bf16[8,128,256]{2,1,0:T(8,128)(2,1)S(1)}, u32[]{:S(2)}, u32[]{:S(2)}) collective-permute-start(bf16[8,128,256]{2,1,0:T(8,128)(2,1)S(1)} %add_convert_fusion.own), channel_id=1, source_target_pairs={{0,192},{8,56},{16,208},{24,8},{32,224},{40,24},{48,240},{56,40},{... | collective-permute-start | bytes 1572872 | tf_op jit(solution)/shard_map/ppermute | solution.py:32
  81.5 13.3 %collective-permute-start.8 = (bf16[8,128,256]{2,1,0:T(8,128)(2,1)S(1)}, bf16[8,128,256]{2,1,0:T(8,128)(2,1)S(1)}, u32[]{:S(2)}, u32[]{:S(2)}) collective-permute-start(bf16[8,128,256]{2,1,0:T(8,128)(2,1)S(1)} %add_convert_fusion.own), channel_id=1, source_target_pairs={{0,128},{8,40},{16,144},{24,56},{32,160},{40,8},{48,176},{56,24},{... | collective-permute-start | bytes 1572872 | tf_op jit(solution)/shard_map/ppermute | solution.py:32
  96.9 21.2 %all-to-all-start.2 = ((bf16[8,144,256]{2,1,0:T(8,128)(2,1)}), bf16[8,144,256]{2,1,0:T(8,128)(2,1)S(1)}, u32[]{:S(2)}, u32[]{:S(2)}) async-start(bf16[8,144,256]{2,1,0:T(8,128)(2,1)} %get-tuple-element.41), calls=%async_computation.2 | async-start | bytes 1179648 | tf_op jit(solution)/shard_map/all_to_all | solution.py:390
  101.2 9.9 %collective-permute-start.10 = (bf16[8,128,256]{2,1,0:T(8,128)(2,1)S(1)}, bf16[8,128,256]{2,1,0:T(8,128)(2,1)S(1)}, u32[]{:S(2)}, u32[]{:S(2)}) collective-permute-start(bf16[8,128,256]{2,1,0:T(8,128)(2,1)S(1)} %get-tuple-element.43.refs_0_), channel_id=1, source_target_pairs={{0,32},{8,136},{16,48},{24,152},{32,0},{40,168},{48,16},{56,184},{... | collective-permute-start | bytes 1572872 | tf_op jit(solution)/shard_map/ppermute | solution.py:32
  101.8 14.8 %collective-permute-start.11 = (bf16[8,128,256]{2,1,0:T(8,128)(2,1)S(1)}, bf16[8,128,256]{2,1,0:T(8,128)(2,1)S(1)}, u32[]{:S(2)}, u32[]{:S(2)}) collective-permute-start(bf16[8,128,256]{2,1,0:T(8,128)(2,1)S(1)} %get-tuple-element.43.refs_0_), channel_id=1, source_target_pairs={{0,16},{8,72},{16,32},{24,88},{32,48},{40,104},{48,0},{56,120},{64... | collective-permute-start | bytes 1572872 | tf_op jit(solution)/shard_map/ppermute | solution.py:32
  103.8 12.8 %collective-permute-start.9 = (bf16[8,128,256]{2,1,0:T(8,128)(2,1)S(1)}, bf16[8,128,256]{2,1,0:T(8,128)(2,1)}, u32[]{:S(2)}, u32[]{:S(2)}) collective-permute-start(bf16[8,128,256]{2,1,0:T(8,128)(2,1)S(1)} %get-tuple-element.43.refs_0_), channel_id=1, source_target_pairs={{0,48},{8,200},{16,0},{24,216},{32,16},{40,232},{48,32},{56,248},{... | collective-permute-start | bytes 1572872 | tf_op jit(solution)/shard_map/ppermute | solution.py:32
  118.2 11.6 %collective-permute-start.12 = (bf16[8,256,512]{2,1,0:T(8,128)(2,1)}, bf16[8,256,512]{2,1,0:T(8,128)(2,1)S(1)}, u32[]{:S(2)}, u32[]{:S(2)}) collective-permute-start(bf16[8,256,512]{2,1,0:T(8,128)(2,1)} %bitcast.44), channel_id=1, source_target_pairs={{0,8},{8,0},{1,9},{9,1},{2,10},{10,2},{3,11},{11,3},{4,12},{12,4},... | collective-permute-start | bytes 6291464 | tf_op jit(solution)/shard_map/ppermute | solution.py:36
  121.1 14.0 %collective-permute-start.13 = (bf16[1040,256]{1,0:T(8,128)(2,1)S(1)}, bf16[1040,256]{1,0:T(8,128)(2,1)S(1)}, u32[]{:S(2)}, u32[]{:S(2)}) collective-permute-start(bf16[1040,256]{1,0:T(8,128)(2,1)S(1)} %compact.1.refs_0_), channel_id=1, source_target_pairs={{0,48},{8,200},{16,0},{24,216},{32,16},{40,232},{48,32},{56,248},{... | collective-permute-start | bytes 1597448 | tf_op jit(solution)/shard_map/ppermute | solution.py:32
  123.3 11.9 %collective-permute-start.14 = (bf16[1040,256]{1,0:T(8,128)(2,1)S(1)}, bf16[1040,256]{1,0:T(8,128)(2,1)S(1)}, u32[]{:S(2)}, u32[]{:S(2)}) collective-permute-start(bf16[1040,256]{1,0:T(8,128)(2,1)S(1)} %compact.1.refs_0_), channel_id=1, source_target_pairs={{0,32},{8,136},{16,48},{24,152},{32,0},{40,168},{48,16},{56,184},{... | collective-permute-start | bytes 1597448 | tf_op jit(solution)/shard_map/ppermute | solution.py:32
  123.6 15.3 %collective-permute-start.15 = (bf16[1040,256]{1,0:T(8,128)(2,1)S(1)}, bf16[1040,256]{1,0:T(8,128)(2,1)S(1)}, u32[]{:S(2)}, u32[]{:S(2)}) collective-permute-start(bf16[1040,256]{1,0:T(8,128)(2,1)S(1)} %compact.1.refs_0_), channel_id=1, source_target_pairs={{0,16},{8,72},{16,32},{24,88},{32,48},{40,104},{48,0},{56,120},{64... | collective-permute-start | bytes 1597448 | tf_op jit(solution)/shard_map/ppermute | solution.py:32
  123.9 2.2 %copy-start.1 = (bf16[4096,512]{1,0:T(8,128)(2,1)S(1)}, bf16[4096,512]{1,0:T(8,128)(2,1)}, u32[]{:S(2)}) copy-start(bf16[4096,512]{1,0:T(8,128)(2,1)} %all-gather.5.cloned.1.call-done) | copy-start | bytes 12582916
  126.1 3.6 %copy-start.5 = (bf16[2048,512]{1,0:T(8,128)(2,1)S(1)}, bf16[2048,512]{1,0:T(8,128)(2,1)}, u32[]{:S(2)}) copy-start(bf16[2048,512]{1,0:T(8,128)(2,1)} %all-gather.7.cloned.1.call-done) | copy-start | bytes 6291460
  130.8 11.8 %copy-start.4 = (bf16[256,512]{1,0:T(8,128)(2,1)S(1)}, bf16[256,512]{1,0:T(8,128)(2,1)}, u32[]{:S(2)}) copy-start(bf16[256,512]{1,0:T(8,128)(2,1)} %param.3) | copy-start | bytes 786436
  130.8 12.9 %copy-start.2 = (bf16[256,512]{1,0:T(8,128)(2,1)S(1)}, bf16[256,512]{1,0:T(8,128)(2,1)}, u32[]{:S(2)}) copy-start(bf16[256,512]{1,0:T(8,128)(2,1)} %view.1) | copy-start | bytes 786436
  130.9 12.8 %collective-permute-start.18 = (f32[272,512]{1,0:T(8,128)S(1)}, f32[272,512]{1,0:T(8,128)S(1)}, u32[]{:S(2)}, u32[]{:S(2)}) collective-permute-start(f32[272,512]{1,0:T(8,128)S(1)} %get-tuple-element.57), channel_id=1, source_target_pairs={{0,8},{8,0},{1,9},{9,1},{2,10},{10,2},{3,11},{11,3},{4,12},{12,4},... | collective-permute-start | bytes 1671176 | tf_op jit(solution)/shard_map/ppermute | solution.py:36
  141.2 2.5 %collective-permute-start.16 = (bf16[256,256]{1,0:T(8,128)(2,1)S(1)}, bf16[256,256]{1,0:T(8,128)(2,1)S(1)}, u32[]{:S(2)}, u32[]{:S(2)}) collective-permute-start(bf16[256,256]{1,0:T(8,128)(2,1)S(1)} %get-tuple-element.54), channel_id=1, source_target_pairs={{0,8},{8,0},{1,9},{9,1},{2,10},{10,2},{3,11},{11,3},{4,12},{12,4},... | collective-permute-start | bytes 393224 | tf_op jit(solution)/shard_map/ppermute | solution.py:36
  142.6 1.1 collective-permute-start.17
Sparse Core Ops, SparseCore 0:
  9.8 48.7 all-gather.4
  60.4 35.5 all-gather.6

commit v4 on v3

--- a/solution.py
+++ b/solution.py
@@ -159,20 +159,24 @@
     return (lines[0:1] + lines[1:2]) + lines[2:3]
 
 
-def compact_body(inward, out):
-    blocks, lines, half = inward.shape
-    quarter = lines - EXTRA
-    share = jnp.zeros((1, half), F32)
-    for g in range(blocks):
-        out[g * quarter : (g + 1) * quarter] = inward[g, :quarter]
-        share = share + gather_share(inward[g, quarter:])
+def strips(share, half):
     share = jnp.broadcast_to(share, (EXTRA, half))
     high = share.astype(BF16)
     share = share - high.astype(F32)
     middle = share.astype(BF16)
     low = (share - middle.astype(F32)).astype(BF16)
     line = lax.broadcasted_iota(jnp.int32, (EXTRA, half), 0)
-    out[blocks * quarter :] = jnp.where(line == 0, high, jnp.where(line == 1, middle, low))
+    return jnp.where(line == 0, high, jnp.where(line == 1, middle, low))
+
+
+def compact_body(inward, out):
+    blocks, lines, half = inward.shape
+    quarter = lines - EXTRA
+    share = jnp.zeros((1, half), F32)
+    for g in range(blocks):
+        out[g * quarter : (g + 1) * quarter] = inward[g, :quarter]
+        share = share + gather_share(inward[g, quarter:])
+    out[blocks * quarter :] = strips(share, half)
 
 
 def compact(inward):
@@ -245,11 +249,13 @@
         else:
             total[...] = part
     shares = [gather_share(piece[blocks * (width // 4) :, :128]) for piece in pieces]
-    loss[...] = (shares[0] + shares[2]) + (shares[1] + shares[3])
+    sent = strips(((shares[0] + shares[2]) + (shares[1] + shares[3]))[:, :1], half)
+    far_grad[rows:] = sent
+    loss[...] = gather_share(sent[:, :128])
     weight = size * (0.5 / OFF_WEIGHT)
     for which, grad in enumerate((near_grad, far_grad)):
         part = slice(which * rows, (which + 1) * rows)
-        grad[...] = finish(
+        grad[:rows] = finish(
             view[part, spot],
             norm[part, spot],
             vec[:, spot],
@@ -278,13 +284,13 @@
 
 
 def join_body(
-    images, at, near, other, loss, other_loss, near_part, far_part, view, norm, vec, grad_a, grad_b, total
+    images, at, near, other, loss, near_part, far_part, view, norm, vec, grad_a, grad_b, total
 ):
     rows, half = near.shape
     for which, value in enumerate((near, other)):
         spot = (1 - at[2] if which else at[2]) * half
-        grad_b[:, pl.ds(pl.multiple_of(spot, half), half)] = value[...]
-    total[...] = loss[...] + other_loss[...]
+        grad_b[:, pl.ds(pl.multiple_of(spot, half), half)] = value[:rows]
+    total[...] = loss[...] + gather_share(other[rows:, :128])
     ends = near_part[rows:] + far_part[rows:]
     for line in range(0, rows, 64):
         lines = slice(line, line + 64)
@@ -413,7 +419,11 @@
     far_a, far_part = lax.optimization_barrier((far_a, far_part))
     near_grad, far_grad, loss = gradient(
         functools.partial(cols_body, images),
-        [jax.ShapeDtypeStruct((rows, half), BF16)] * 2 + [jax.ShapeDtypeStruct((1, 128), F32)],
+        [
+            jax.ShapeDtypeStruct((rows, half), BF16),
+            jax.ShapeDtypeStruct((rows + EXTRA, half), BF16),
+            jax.ShapeDtypeStruct((1, 128), F32),
+        ],
         [pltpu.VMEM((blocks, width, half), BF16), pltpu.VMEM((2 * rows + EXTRA, half), F32)],
         "cols",
         at,
@@ -431,7 +441,6 @@
         near_grad,
         swap(far_grad),
         loss,
-        swap(loss),
         near_part,
         swap(far_part),
         view_a,

time: 153 us -> 152 us (level)
    ppermute x7 -> x6, starting transfers between devices: 10.8 us -> 10.6 us  [swap(): return lax.ppermute(value, 'c', [(0, 1), (1, 0)])]
  transfers between devices with their start and end apart: 24 -> 23, of which waited for: 16 -> 16; matrix products, arithmetic and copies ran while one was open for 6% -> 6% of each run, Pallas kernels for 6% -> 6%
where the time goes in v4:
time: 152 us
  waiting for transfers between devices  69.3 us (46%)
  starting transfers between devices  42.1 us (28%)
  between operations  14.9 us (10%)
  Pallas kernels  11.4 us (8%)
  other arithmetic  7.13 us (5%)
  local copies, waits for them, and re-layouts  7.04 us (5%)
    ppermute x12, waiting for transfers between devices, shift(): return lax.ppermute(value, ('y', 'x', 'c'), pairs)  43.5 us
    all_to_all x2, waiting for transfers between devices, spread(): return lax.all_to_all(copies, axes, split_axis=0, concat_axis=0, tiled=True)  15 us
    ppermute x12, starting transfers between devices, shift(): return lax.ppermute(value, ('y', 'x', 'c'), pairs)  13.9 us
    all_to_all x2, starting transfers between devices, spread(): return lax.all_to_all(copies, axes, split_axis=0, concat_axis=0, tiled=True)  13.2 us
    ppermute x6, starting transfers between devices, swap(): return lax.ppermute(value, 'c', [(0, 1), (1, 0)])  10.6 us
    all_gather x1, waiting for transfers between devices, local(): raw_b = lax.all_gather(view_b, ('c', 'z'), axis=0, tiled=False)  6.87 us
    pallas_call x2, Pallas kernels, gradient(): pl.pallas_call(body, in_specs=[SMEM] + [VMEM] * (len(operands) - 1), out_...  5.89 us
    unnamed x13, local copies, waits for them, and re-layouts  4.4 us
  transfers between devices with their start and end apart: 23, of which 16 were waited for; matrix products, arithmetic and copies ran while one was open for 6% of the time, Pallas kernels for 6%

profile of v4, /device:TPU:1, one launch (start us, length us, event | category | flops | bytes accessed | tf_op | source)
XLA Modules:
  0.0 151.9 jit_solution(10879835440418780048)
XLA Ops:
  7.2 0.7 all-gather.5.cloned.1.call-update
  7.9 1.0 convert_reduce_fusion
  8.9 1.0 convert_reduce_fusion.1
  10.0 1.2 fusion.5
  11.2 3.3 %collective-permute-start = (f32[5,512]{1,0:T(8,128)S(1)}, f32[5,512]{1,0:T(8,128)S(1)}, u32[]{:S(2)}, u32[]{:S(2)}) collective-permute-start(f32[5,512]{1,0:T(8,128)S(1)} %stack.46), channel_id=1, source_target_pairs={{0,8},{8,0},{1,9},{9,1},{2,10},{10,2},{3,11},{11,3},{4,12},{12,4},... | collective-permute-start | bytes 30728 | tf_op jit(solution)/shard_map/ppermute | solution.py:36
  14.5 0.8 collective-permute-done
  15.4 0.7 broadcast_in_dim.8
  16.2 5.0 %all-to-all-start = ((f32[16,5,512]{2,1,0:T(8,128)}), f32[16,5,512]{2,1,0:T(8,128)S(1)}, u32[]{:S(2)}, u32[]{:S(2)}) async-start(f32[16,5,512]{2,1,0:T(8,128)} %broadcast_in_dim.8), calls=%async_computation | async-start | bytes 524288 | tf_op jit(solution)/shard_map/all_to_all | solution.py:41
  21.2 0.7 collective-permute-start.2
  22.1 7.3 %all-to-all-done = f32[16,5,512]{2,1,0:T(8,128)S(1)} async-done(((f32[16,5,512]{2,1,0:T(8,128)}), f32[16,5,512]{2,1,0:T(8,128)S(1)}, u32[]{:S(2)}, u32[]{:S(2)}) %all-to-all-start) | async-done | bytes 163872 | tf_op jit(solution)/shard_map/all_to_all | solution.py:41
  29.6 1.0 fusion.8
  30.6 1.6 %collective-permute-start.1 = (bf16[256,512]{1,0:T(8,128)(2,1)S(1)}, bf16[256,512]{1,0:T(8,128)(2,1)S(1)}, u32[]{:S(2)}, u32[]{:S(2)}) collective-permute-start(bf16[256,512]{1,0:T(8,128)(2,1)S(1)} %fusion.8), channel_id=1, source_target_pairs={{0,8},{8,0},{1,9},{9,1},{2,10},{10,2},{3,11},{11,3},{4,12},{12,4},... | collective-permute-start | bytes 786440 | tf_op jit(solution)/shard_map/ppermute | solution.py:36
  32.9 8.2 %all-to-all-start.1 = ((f32[8,6,512]{2,1,0:T(8,128)}), f32[8,6,512]{2,1,0:T(8,128)S(1)}, u32[]{:S(2)}, u32[]{:S(2)}) async-start(f32[8,6,512]{2,1,0:T(8,128)} %broadcast_in_dim.9), calls=%async_computation.1 | async-start | bytes 262144 | tf_op jit(solution)/shard_map/all_to_all | solution.py:41
  42.7 1.0 fusion.12
  44.0 7.7 %all-to-all-done.1.stats = f32[8,6,512]{2,1,0:T(8,128)S(1)} async-done(((f32[8,6,512]{2,1,0:T(8,128)}), f32[8,6,512]{2,1,0:T(8,128)S(1)}, u32[]{:S(2)}, u32[]{:S(2)}) %all-to-all-start.1) | async-done | bytes 98336 | tf_op jit(solution)/shard_map/all_to_all | solution.py:41
  51.7 6.9 %all-gather.5.cloned.1.call-done = bf16[4096,512]{1,0:T(8,128)(2,1)} async-done(((bf16[256,512]{1,0:T(8,128)(2,1)}), bf16[4096,512]{1,0:T(8,128)(2,1)}) %all-gather.5.cloned.1.call-update) | async-done | bytes 4194320 | tf_op jit(solution)/shard_map/all_gather | solution.py:334
  58.6 2.2 %copy-done = bf16[4096,512]{1,0:T(8,128)(2,1)S(1)} copy-done((bf16[4096,512]{1,0:T(8,128)(2,1)S(1)}, bf16[4096,512]{1,0:T(8,128)(2,1)}, u32[]{:S(2)}) %copy-start) | copy-done | bytes 4194328
  60.8 1.8 %correlate.1 = (bf16[8,128,256]{2,1,0:T(8,128)(2,1)S(1)}, bf16[8,128,256]{2,1,0:T(8,128)(2,1)S(1)}, bf16[8,128,256]{2,1,0:T(8,128)(2,1)S(1)}, bf16[8,128,256]{2,1,0:T(8,128)(2,1)S(1)}) custom-call(s32[5]{0:T(128)S(1)} %stack.41.at, f32[8,6,512]{2,1,0:T(8,128)S(1)} %all-to-all-done.1.stats, bf16[16,256,512]{2,1,0:T(8,128)(2,1)S(1)} %bitcast.41, ...), custom_call_target="tpu_custom_call" | custom-call | flops 1073741824 | bytes 6291456 | tf_op jit(solution)/shard_map/correlate/pallas_call | solution.py:84
  62.6 1.0 collective-permute-start.3
  63.6 1.8 %collective-permute-start.4 = (bf16[8,128,256]{2,1,0:T(8,128)(2,1)S(1)}, bf16[8,128,256]{2,1,0:T(8,128)(2,1)S(1)}, u32[]{:S(2)}, u32[]{:S(2)}) collective-permute-start(bf16[8,128,256]{2,1,0:T(8,128)(2,1)S(1)} %get-tuple-element.38), channel_id=1, source_target_pairs={{0,48},{8,200},{16,0},{24,216},{32,16},{40,232},{48,32},{56,248},{... | collective-permute-start | bytes 1572872 | tf_op jit(solution)/shard_map/ppermute | solution.py:32
  65.4 1.2 collective-permute-start.5
  66.5 5.7 %collective-permute-done.3 = bf16[8,128,256]{2,1,0:T(8,128)(2,1)S(1)} collective-permute-done((bf16[8,128,256]{2,1,0:T(8,128)(2,1)S(1)}, bf16[8,128,256]{2,1,0:T(8,128)(2,1)S(1)}, u32[]{:S(2)}, u32[]{:S(2)}) %collective-permute-start.3) | collective-permute-done | bytes 524320 | tf_op jit(solution)/shard_map/ppermute | solution.py:32
  72.2 4.9 %collective-permute-done.4 = bf16[8,128,256]{2,1,0:T(8,128)(2,1)S(1)} collective-permute-done((bf16[8,128,256]{2,1,0:T(8,128)(2,1)S(1)}, bf16[8,128,256]{2,1,0:T(8,128)(2,1)S(1)}, u32[]{:S(2)}, u32[]{:S(2)}) %collective-permute-start.4) | collective-permute-done | bytes 524320 | tf_op jit(solution)/shard_map/ppermute | solution.py:32
  77.1 1.3 collective-permute-done.5
  78.7 1.0 collective-permute-start.6
  79.7 1.8 %collective-permute-start.7 = (bf16[8,128,256]{2,1,0:T(8,128)(2,1)S(1)}, bf16[8,128,256]{2,1,0:T(8,128)(2,1)S(1)}, u32[]{:S(2)}, u32[]{:S(2)}) collective-permute-start(bf16[8,128,256]{2,1,0:T(8,128)(2,1)S(1)} %add_convert_fusion.own), channel_id=1, source_target_pairs={{0,192},{8,56},{16,208},{24,8},{32,224},{40,24},{48,240},{56,40},{... | collective-permute-start | bytes 1572872 | tf_op jit(solution)/shard_map/ppermute | solution.py:32
  81.5 1.2 collective-permute-start.8
  82.6 5.8 %collective-permute-done.6.ahead = bf16[8,128,256]{2,1,0:T(8,128)(2,1)S(1)} collective-permute-done((bf16[8,128,256]{2,1,0:T(8,128)(2,1)S(1)}, bf16[8,128,256]{2,1,0:T(8,128)(2,1)S(1)}, u32[]{:S(2)}, u32[]{:S(2)}) %collective-permute-start.6) | collective-permute-done | bytes 524320 | tf_op jit(solution)/shard_map/ppermute | solution.py:32
  88.5 4.8 %collective-permute-done.7.behind = bf16[8,128,256]{2,1,0:T(8,128)(2,1)S(1)} collective-permute-done((bf16[8,128,256]{2,1,0:T(8,128)(2,1)S(1)}, bf16[8,128,256]{2,1,0:T(8,128)(2,1)S(1)}, u32[]{:S(2)}, u32[]{:S(2)}) %collective-permute-start.7) | collective-permute-done | bytes 524320 | tf_op jit(solution)/shard_map/ppermute | solution.py:32
  93.2 1.6 %collective-permute-done.8.across = bf16[8,128,256]{2,1,0:T(8,128)(2,1)S(1)} collective-permute-done((bf16[8,128,256]{2,1,0:T(8,128)(2,1)S(1)}, bf16[8,128,256]{2,1,0:T(8,128)(2,1)S(1)}, u32[]{:S(2)}, u32[]{:S(2)}) %collective-permute-start.8) | collective-permute-done | bytes 524320 | tf_op jit(solution)/shard_map/ppermute | solution.py:32
  94.8 2.1 %tile.1 = (bf16[8,128,256]{2,1,0:T(8,128)(2,1)S(1)}, bf16[8,144,256]{2,1,0:T(8,128)(2,1)}) custom-call(s32[5]{0:T(128)S(1)} %stack.41.at, f32[1,128]{1,0:T(1,128)S(1)} %broadcast_in_dim.11.diagonal, bf16[8,128,256]{2,1,0:T(8,128)(2,1)S(1)} %add_convert_fusion.own, bf16[8,128,256]{2,1,0:T(8,128)(2,1)S(1)} %collective-permute-done.6.ahead, ...), custom_call_target="tpu_custom_call" | custom-call | flops 1572864 | bytes 3145728 | tf_op jit(solution)/shard_map/tile/pallas_call | solution.py:126
  96.9 4.3 %all-to-all-start.2 = ((bf16[8,144,256]{2,1,0:T(8,128)(2,1)}), bf16[8,144,256]{2,1,0:T(8,128)(2,1)S(1)}, u32[]{:S(2)}, u32[]{:S(2)}) async-start(bf16[8,144,256]{2,1,0:T(8,128)(2,1)} %get-tuple-element.41), calls=%async_computation.2 | async-start | bytes 1179648 | tf_op jit(solution)/shard_map/all_to_all | solution.py:396
  101.8 2.0 %collective-permute-start.11 = (bf16[8,128,256]{2,1,0:T(8,128)(2,1)S(1)}, bf16[8,128,256]{2,1,0:T(8,128)(2,1)S(1)}, u32[]{:S(2)}, u32[]{:S(2)}) collective-permute-start(bf16[8,128,256]{2,1,0:T(8,128)(2,1)S(1)} %get-tuple-element.43.refs_0_), channel_id=1, source_target_pairs={{0,16},{8,72},{16,32},{24,88},{32,48},{40,104},{48,0},{56,120},{64... | collective-permute-start | bytes 1572872 | tf_op jit(solution)/shard_map/ppermute | solution.py:32
  104.5 6.6 %collective-permute-done.10.refs_2_ = bf16[8,128,256]{2,1,0:T(8,128)(2,1)S(1)} collective-permute-done((bf16[8,128,256]{2,1,0:T(8,128)(2,1)S(1)}, bf16[8,128,256]{2,1,0:T(8,128)(2,1)S(1)}, u32[]{:S(2)}, u32[]{:S(2)}) %collective-permute-start.10) | collective-permute-done | bytes 524320 | tf_op jit(solution)/shard_map/ppermute | solution.py:32
  111.1 5.6 %collective-permute-done.11.refs_3_ = bf16[8,128,256]{2,1,0:T(8,128)(2,1)S(1)} collective-permute-done((bf16[8,128,256]{2,1,0:T(8,128)(2,1)S(1)}, bf16[8,128,256]{2,1,0:T(8,128)(2,1)S(1)}, u32[]{:S(2)}, u32[]{:S(2)}) %collective-permute-start.11) | collective-permute-done | bytes 524320 | tf_op jit(solution)/shard_map/ppermute | solution.py:32
  116.6 1.5 all-to-all-done.2.inward
  118.2 2.9 %collective-permute-start.12 = (bf16[8,256,512]{2,1,0:T(8,128)(2,1)}, bf16[8,256,512]{2,1,0:T(8,128)(2,1)S(1)}, u32[]{:S(2)}, u32[]{:S(2)}) collective-permute-start(bf16[8,256,512]{2,1,0:T(8,128)(2,1)} %bitcast.44), channel_id=1, source_target_pairs={{0,8},{8,0},{1,9},{9,1},{2,10},{10,2},{3,11},{11,3},{4,12},{12,4},... | collective-permute-start | bytes 6291464 | tf_op jit(solution)/shard_map/ppermute | solution.py:36
  121.2 2.1 %collective-permute-start.13 = (bf16[1040,256]{1,0:T(8,128)(2,1)S(1)}, bf16[1040,256]{1,0:T(8,128)(2,1)S(1)}, u32[]{:S(2)}, u32[]{:S(2)}) collective-permute-start(bf16[1040,256]{1,0:T(8,128)(2,1)S(1)} %compact.1.refs_0_), channel_id=1, source_target_pairs={{0,48},{8,200},{16,0},{24,216},{32,16},{40,232},{48,32},{56,248},{... | collective-permute-start | bytes 1597448 | tf_op jit(solution)/shard_map/ppermute | solution.py:32
  123.9 2.2 %copy-done.1 = bf16[4096,512]{1,0:T(8,128)(2,1)S(1)} copy-done((bf16[4096,512]{1,0:T(8,128)(2,1)S(1)}, bf16[4096,512]{1,0:T(8,128)(2,1)}, u32[]{:S(2)}) %copy-start.1) | copy-done | bytes 4194328
  126.1 3.6 %rows.1 = (f32[272,512]{1,0:T(8,128)S(1)}, f32[272,512]{1,0:T(8,128)S(1)}) custom-call(s32[5]{0:T(128)S(1)} %stack.41.at, bf16[16,256,512]{2,1,0:T(8,128)(2,1)S(1)} %bitcast.42, f32[8,6,512]{2,1,0:T(8,128)S(1)} %all-to-all-done.1.stats, bf16[8,128,256]{2,1,0:T(8,128)(2,1)S(1)} %get-tuple-element.43.refs_0_, ...), custom_call_target="tpu_custom_call" | custom-call | flops 1073741824 | bytes 7340032 | tf_op jit(solution)/shard_map/rows/pallas_call | solution.py:272
  129.7 1.1 reduce-precision_convert_fusion
  130.9 0.8 collective-permute-start.17
  131.6 3.5 %collective-permute-done.13.refs_1_ = bf16[1040,256]{1,0:T(8,128)(2,1)S(1)} collective-permute-done((bf16[1040,256]{1,0:T(8,128)(2,1)S(1)}, bf16[1040,256]{1,0:T(8,128)(2,1)S(1)}, u32[]{:S(2)}, u32[]{:S(2)}) %collective-permute-start.13) | collective-permute-done | bytes 532512 | tf_op jit(solution)/shard_map/ppermute | solution.py:32
  135.2 3.7 %collective-permute-done.15.refs_3_ = bf16[1040,256]{1,0:T(8,128)(2,1)S(1)} collective-permute-done((bf16[1040,256]{1,0:T(8,128)(2,1)S(1)}, bf16[1040,256]{1,0:T(8,128)(2,1)S(1)}, u32[]{:S(2)}, u32[]{:S(2)}) %collective-permute-start.15) | collective-permute-done | bytes 532512 | tf_op jit(solution)/shard_map/ppermute | solution.py:32
  138.9 2.3 %cols.1 = (bf16[256,256]{1,0:T(8,128)(2,1)S(1)}, bf16[272,256]{1,0:T(8,128)(2,1)S(1)}, f32[1,128]{1,0:T(1,128)S(1)}) custom-call(s32[5]{0:T(128)S(1)} %stack.41.at, bf16[8,256,512]{2,1,0:T(8,128)(2,1)S(1)} %get-tuple-element.78.near, bf16[8,256,512]{2,1,0:T(8,128)(2,1)S(1)} %get-tuple-element.48.far, f32[8,6,512]{2,1,0:T(8,128)S(1)} %all-to-all-done.1.stats, ...), custom_call_target="tpu_custom_call" | custom-call | flops 1073741824 | bytes 7340032 | tf_op jit(solution)/shard_map/cols/pallas_call | solution.py:272
  141.2 1.4 collective-permute-start.16
  142.6 0.9 collective-permute-done.16.other
  143.6 1.5 join.1
  (55 shorter events, 4.9 us)
Async XLA Ops:
  7.2 35.3 %copy-start.3 = (bf16[256,512]{1,0:T(8,128)(2,1)S(1)}, bf16[256,512]{1,0:T(8,128)(2,1)}, u32[]{:S(2)}) copy-start(bf16[256,512]{1,0:T(8,128)(2,1)} %param.3) | copy-start | bytes 786436
  7.2 51.4 %all-gather.5.cloned.1.call-start = ((), (), s32[]{:S(2)}) async-start(), calls=%async_computation.3 | async-start | bytes 4456448 | tf_op jit(solution)/shard_map/all_gather | solution.py:334
  11.2 4.2 %collective-permute-start = (f32[5,512]{1,0:T(8,128)S(1)}, f32[5,512]{1,0:T(8,128)S(1)}, u32[]{:S(2)}, u32[]{:S(2)}) collective-permute-start(f32[5,512]{1,0:T(8,128)S(1)} %stack.46), channel_id=1, source_target_pairs={{0,8},{8,0},{1,9},{9,1},{2,10},{10,2},{3,11},{11,3},{4,12},{12,4},... | collective-permute-start | bytes 30728 | tf_op jit(solution)/shard_map/ppermute | solution.py:36
  16.2 13.2 %all-to-all-start = ((f32[16,5,512]{2,1,0:T(8,128)}), f32[16,5,512]{2,1,0:T(8,128)S(1)}, u32[]{:S(2)}, u32[]{:S(2)}) async-start(f32[16,5,512]{2,1,0:T(8,128)} %broadcast_in_dim.8), calls=%async_computation | async-start | bytes 524288 | tf_op jit(solution)/shard_map/all_to_all | solution.py:41
  21.2 83.3 %all-gather.7.cloned.1.call-start = ((), (), s32[]{:S(2)}) async-start(), calls=%async_computation.4 | async-start | bytes 2359296 | tf_op jit(solution)/shard_map/all_gather | solution.py:335
  21.2 21.2 %collective-permute-start.2 = (bf16[256,512]{1,0:T(8,128)(2,1)}, bf16[256,512]{1,0:T(8,128)(2,1)S(1)}, u32[]{:S(2)}, u32[]{:S(2)}) collective-permute-start(bf16[256,512]{1,0:T(8,128)(2,1)} %param.3), channel_id=1, source_target_pairs={{0,8},{8,0},{1,9},{9,1},{2,10},{10,2},{3,11},{11,3},{4,12},{12,4},... | collective-permute-start | bytes 786440 | tf_op jit(solution)/shard_map/ppermute | solution.py:36
  30.6 11.9 %collective-permute-start.1 = (bf16[256,512]{1,0:T(8,128)(2,1)S(1)}, bf16[256,512]{1,0:T(8,128)(2,1)S(1)}, u32[]{:S(2)}, u32[]{:S(2)}) collective-permute-start(bf16[256,512]{1,0:T(8,128)(2,1)S(1)} %fusion.8), channel_id=1, source_target_pairs={{0,8},{8,0},{1,9},{9,1},{2,10},{10,2},{3,11},{11,3},{4,12},{12,4},... | collective-permute-start | bytes 786440 | tf_op jit(solution)/shard_map/ppermute | solution.py:36
  32.9 18.9 %all-to-all-start.1 = ((f32[8,6,512]{2,1,0:T(8,128)}), f32[8,6,512]{2,1,0:T(8,128)S(1)}, u32[]{:S(2)}, u32[]{:S(2)}) async-start(f32[8,6,512]{2,1,0:T(8,128)} %broadcast_in_dim.9), calls=%async_computation.1 | async-start | bytes 262144 | tf_op jit(solution)/shard_map/all_to_all | solution.py:41
  58.6 2.2 %copy-start = (bf16[4096,512]{1,0:T(8,128)(2,1)S(1)}, bf16[4096,512]{1,0:T(8,128)(2,1)}, u32[]{:S(2)}) copy-start(bf16[4096,512]{1,0:T(8,128)(2,1)} %all-gather.5.cloned.1.call-done) | copy-start | bytes 12582916
  62.6 9.6 %collective-permute-start.3 = (bf16[8,128,256]{2,1,0:T(8,128)(2,1)S(1)}, bf16[8,128,256]{2,1,0:T(8,128)(2,1)S(1)}, u32[]{:S(2)}, u32[]{:S(2)}) collective-permute-start(bf16[8,128,256]{2,1,0:T(8,128)(2,1)S(1)} %get-tuple-element.37), channel_id=1, source_target_pairs={{0,16},{8,72},{16,32},{24,88},{32,48},{40,104},{48,0},{56,120},{64... | collective-permute-start | bytes 1572872 | tf_op jit(solution)/shard_map/ppermute | solution.py:32
  63.6 13.5 %collective-permute-start.4 = (bf16[8,128,256]{2,1,0:T(8,128)(2,1)S(1)}, bf16[8,128,256]{2,1,0:T(8,128)(2,1)S(1)}, u32[]{:S(2)}, u32[]{:S(2)}) collective-permute-start(bf16[8,128,256]{2,1,0:T(8,128)(2,1)S(1)} %get-tuple-element.38), channel_id=1, source_target_pairs={{0,48},{8,200},{16,0},{24,216},{32,16},{40,232},{48,32},{56,248},{... | collective-permute-start | bytes 1572872 | tf_op jit(solution)/shard_map/ppermute | solution.py:32
  65.4 13.1 %collective-permute-start.5 = (bf16[8,128,256]{2,1,0:T(8,128)(2,1)S(1)}, bf16[8,128,256]{2,1,0:T(8,128)(2,1)S(1)}, u32[]{:S(2)}, u32[]{:S(2)}) collective-permute-start(bf16[8,128,256]{2,1,0:T(8,128)(2,1)S(1)} %get-tuple-element.39), channel_id=1, source_target_pairs={{0,32},{8,136},{16,48},{24,152},{32,0},{40,168},{48,16},{56,184},{... | collective-permute-start | bytes 1572872 | tf_op jit(solution)/shard_map/ppermute | solution.py:32
  78.7 9.7 %collective-permute-start.6 = (bf16[8,128,256]{2,1,0:T(8,128)(2,1)S(1)}, bf16[8,128,256]{2,1,0:T(8,128)(2,1)S(1)}, u32[]{:S(2)}, u32[]{:S(2)}) collective-permute-start(bf16[8,128,256]{2,1,0:T(8,128)(2,1)S(1)} %add_convert_fusion.own), channel_id=1, source_target_pairs={{0,64},{8,24},{16,80},{24,40},{32,96},{40,56},{48,112},{56,8},{64,... | collective-permute-start | bytes 1572872 | tf_op jit(solution)/shard_map/ppermute | solution.py:32
  79.7 13.5 %collective-permute-start.7 = (bf16[8,128,256]{2,1,0:T(8,128)(2,1)S(1)}, bf16[8,128,256]{2,1,0:T(8,128)(2,1)S(1)}, u32[]{:S(2)}, u32[]{:S(2)}) collective-permute-start(bf16[8,128,256]{2,1,0:T(8,128)(2,1)S(1)} %add_convert_fusion.own), channel_id=1, source_target_pairs={{0,192},{8,56},{16,208},{24,8},{32,224},{40,24},{48,240},{56,40},{... | collective-permute-start | bytes 1572872 | tf_op jit(solution)/shard_map/ppermute | solution.py:32
  81.5 13.3 %collective-permute-start.8 = (bf16[8,128,256]{2,1,0:T(8,128)(2,1)S(1)}, bf16[8,128,256]{2,1,0:T(8,128)(2,1)S(1)}, u32[]{:S(2)}, u32[]{:S(2)}) collective-permute-start(bf16[8,128,256]{2,1,0:T(8,128)(2,1)S(1)} %add_convert_fusion.own), channel_id=1, source_target_pairs={{0,128},{8,40},{16,144},{24,56},{32,160},{40,8},{48,176},{56,24},{... | collective-permute-start | bytes 1572872 | tf_op jit(solution)/shard_map/ppermute | solution.py:32
  96.9 21.2 %all-to-all-start.2 = ((bf16[8,144,256]{2,1,0:T(8,128)(2,1)}), bf16[8,144,256]{2,1,0:T(8,128)(2,1)S(1)}, u32[]{:S(2)}, u32[]{:S(2)}) async-start(bf16[8,144,256]{2,1,0:T(8,128)(2,1)} %get-tuple-element.41), calls=%async_computation.2 | async-start | bytes 1179648 | tf_op jit(solution)/shard_map/all_to_all | solution.py:396
  101.2 9.9 %collective-permute-start.10 = (bf16[8,128,256]{2,1,0:T(8,128)(2,1)S(1)}, bf16[8,128,256]{2,1,0:T(8,128)(2,1)S(1)}, u32[]{:S(2)}, u32[]{:S(2)}) collective-permute-start(bf16[8,128,256]{2,1,0:T(8,128)(2,1)S(1)} %get-tuple-element.43.refs_0_), channel_id=1, source_target_pairs={{0,32},{8,136},{16,48},{24,152},{32,0},{40,168},{48,16},{56,184},{... | collective-permute-start | bytes 1572872 | tf_op jit(solution)/shard_map/ppermute | solution.py:32
  101.8 14.8 %collective-permute-start.11 = (bf16[8,128,256]{2,1,0:T(8,128)(2,1)S(1)}, bf16[8,128,256]{2,1,0:T(8,128)(2,1)S(1)}, u32[]{:S(2)}, u32[]{:S(2)}) collective-permute-start(bf16[8,128,256]{2,1,0:T(8,128)(2,1)S(1)} %get-tuple-element.43.refs_0_), channel_id=1, source_target_pairs={{0,16},{8,72},{16,32},{24,88},{32,48},{40,104},{48,0},{56,120},{64... | collective-permute-start | bytes 1572872 | tf_op jit(solution)/shard_map/ppermute | solution.py:32
  103.8 12.8 %collective-permute-start.9 = (bf16[8,128,256]{2,1,0:T(8,128)(2,1)S(1)}, bf16[8,128,256]{2,1,0:T(8,128)(2,1)}, u32[]{:S(2)}, u32[]{:S(2)}) collective-permute-start(bf16[8,128,256]{2,1,0:T(8,128)(2,1)S(1)} %get-tuple-element.43.refs_0_), channel_id=1, source_target_pairs={{0,48},{8,200},{16,0},{24,216},{32,16},{40,232},{48,32},{56,248},{... | collective-permute-start | bytes 1572872 | tf_op jit(solution)/shard_map/ppermute | solution.py:32
  118.2 11.6 %collective-permute-start.12 = (bf16[8,256,512]{2,1,0:T(8,128)(2,1)}, bf16[8,256,512]{2,1,0:T(8,128)(2,1)S(1)}, u32[]{:S(2)}, u32[]{:S(2)}) collective-permute-start(bf16[8,256,512]{2,1,0:T(8,128)(2,1)} %bitcast.44), channel_id=1, source_target_pairs={{0,8},{8,0},{1,9},{9,1},{2,10},{10,2},{3,11},{11,3},{4,12},{12,4},... | collective-permute-start | bytes 6291464 | tf_op jit(solution)/shard_map/ppermute | solution.py:36
  121.2 14.0 %collective-permute-start.13 = (bf16[1040,256]{1,0:T(8,128)(2,1)S(1)}, bf16[1040,256]{1,0:T(8,128)(2,1)S(1)}, u32[]{:S(2)}, u32[]{:S(2)}) collective-permute-start(bf16[1040,256]{1,0:T(8,128)(2,1)S(1)} %compact.1.refs_0_), channel_id=1, source_target_pairs={{0,48},{8,200},{16,0},{24,216},{32,16},{40,232},{48,32},{56,248},{... | collective-permute-start | bytes 1597448 | tf_op jit(solution)/shard_map/ppermute | solution.py:32
  123.3 11.9 %collective-permute-start.14 = (bf16[1040,256]{1,0:T(8,128)(2,1)S(1)}, bf16[1040,256]{1,0:T(8,128)(2,1)S(1)}, u32[]{:S(2)}, u32[]{:S(2)}) collective-permute-start(bf16[1040,256]{1,0:T(8,128)(2,1)S(1)} %compact.1.refs_0_), channel_id=1, source_target_pairs={{0,32},{8,136},{16,48},{24,152},{32,0},{40,168},{48,16},{56,184},{... | collective-permute-start | bytes 1597448 | tf_op jit(solution)/shard_map/ppermute | solution.py:32
  123.6 15.3 %collective-permute-start.15 = (bf16[1040,256]{1,0:T(8,128)(2,1)S(1)}, bf16[1040,256]{1,0:T(8,128)(2,1)S(1)}, u32[]{:S(2)}, u32[]{:S(2)}) collective-permute-start(bf16[1040,256]{1,0:T(8,128)(2,1)S(1)} %compact.1.refs_0_), channel_id=1, source_target_pairs={{0,16},{8,72},{16,32},{24,88},{32,48},{40,104},{48,0},{56,120},{64... | collective-permute-start | bytes 1597448 | tf_op jit(solution)/shard_map/ppermute | solution.py:32
  123.9 2.2 %copy-start.1 = (bf16[4096,512]{1,0:T(8,128)(2,1)S(1)}, bf16[4096,512]{1,0:T(8,128)(2,1)}, u32[]{:S(2)}) copy-start(bf16[4096,512]{1,0:T(8,128)(2,1)} %all-gather.5.cloned.1.call-done) | copy-start | bytes 12582916
  126.1 3.6 %copy-start.5 = (bf16[2048,512]{1,0:T(8,128)(2,1)S(1)}, bf16[2048,512]{1,0:T(8,128)(2,1)}, u32[]{:S(2)}) copy-start(bf16[2048,512]{1,0:T(8,128)(2,1)} %all-gather.7.cloned.1.call-done) | copy-start | bytes 6291460
  130.8 11.7 %copy-start.4 = (bf16[256,512]{1,0:T(8,128)(2,1)S(1)}, bf16[256,512]{1,0:T(8,128)(2,1)}, u32[]{:S(2)}) copy-start(bf16[256,512]{1,0:T(8,128)(2,1)} %param.3) | copy-start | bytes 786436
  130.9 12.7 %copy-start.2 = (bf16[256,512]{1,0:T(8,128)(2,1)S(1)}, bf16[256,512]{1,0:T(8,128)(2,1)}, u32[]{:S(2)}) copy-start(bf16[256,512]{1,0:T(8,128)(2,1)} %view.1) | copy-start | bytes 786436
  130.9 12.7 %collective-permute-start.17 = (f32[272,512]{1,0:T(8,128)S(1)}, f32[272,512]{1,0:T(8,128)S(1)}, u32[]{:S(2)}, u32[]{:S(2)}) collective-permute-start(f32[272,512]{1,0:T(8,128)S(1)} %get-tuple-element.57), channel_id=1, source_target_pairs={{0,8},{8,0},{1,9},{9,1},{2,10},{10,2},{3,11},{11,3},{4,12},{12,4},... | collective-permute-start | bytes 1671176 | tf_op jit(solution)/shard_map/ppermute | solution.py:36
  141.2 2.4 %collective-permute-start.16 = (bf16[272,256]{1,0:T(8,128)(2,1)S(1)}, bf16[272,256]{1,0:T(8,128)(2,1)S(1)}, u32[]{:S(2)}, u32[]{:S(2)}) collective-permute-start(bf16[272,256]{1,0:T(8,128)(2,1)S(1)} %get-tuple-element.54), channel_id=1, source_target_pairs={{0,8},{8,0},{1,9},{9,1},{2,10},{10,2},{3,11},{11,3},{4,12},{12,4},... | collective-permute-start | bytes 417800 | tf_op jit(solution)/shard_map/ppermute | solution.py:36
Sparse Core Ops, SparseCore 0:
  9.8 48.7 all-gather.4
  60.4 35.5 all-gather.6
